TPU v7x, 256 devices: a whole 4x4x8 slice. The times are simulated.
256 devices in a mesh: dp: 4 (over z_lo, core), space: 64 (over z_hi, y, x).
Axes of the slice: x: 4, y: 4, z: 8 (z_hi: 4, z_lo: 2; z = z_hi * 2 + z_lo), core: 2. Of those that a mesh axis runs over, the one named last changes fastest.
Arguments:
- field_in: bfloat16 [4, 64, 128, 128, 128], P('dp', None, 'space'), may hold values from -6 to 6
- cotangent: bfloat16 [4, 64, 128, 128, 128], P('dp', None, 'space'), may hold values from -6 to 6
- spectral_one: bfloat16 [2, 16, 256, 64, 64], P(None, None, 'space'), may hold values from -3 to 3
- spectral_two: bfloat16 [2, 16, 256, 64, 64], P(None, None, 'space'), may hold values from -3 to 3
- point_one: bfloat16 [64, 64], replicated, may hold values from -0.75 to 0.75
- point_two: bfloat16 [64, 64], replicated, may hold values from -0.75 to 0.75
- bias_one: float32 [64], replicated, may hold values from -3 to 3
- bias_two: float32 [64], replicated, may hold values from -3 to 3
Outputs:
- spectral_grad_one: bfloat16 [2, 16, 256, 64, 64], P(None, None, 'space')
- spectral_grad_two: bfloat16 [2, 16, 256, 64, 64], P(None, None, 'space')
- point_grad_one: float32 [64, 64], replicated
- point_grad_two: float32 [64, 64], replicated
- bias_grad_one: float32 [64], replicated
- bias_grad_two: float32 [64], replicated
All inputs are finite; a program needn't handle non-finite values.
Results may differ from a plain program's by a relative error of at most 0.035.
Values may be sent and summed in bfloat16 or wider, within the bound.
No kernel may reach another device: no remote copies, remote signals or barrier semaphores. Data moves between devices by JAX's collectives and lax.ppermute only.
A program may use at most 128 MiB of HBM per device.

v0:
```python
import math

import jax
import jax.numpy as jnp
from jax import lax
from jax.sharding import PartitionSpec as P

MY = 16
MZ = 16


root_coef = math.sqrt(2.0 / math.pi)


def angles(length, modes, two_sided):
    places = jnp.arange(length, dtype=jnp.int32)[:, None]
    orders = jnp.arange(modes, dtype=jnp.int32)[None, :]
    if two_sided:
        orders = jnp.where(orders < modes // 2, orders, orders - modes + length)
    phases = places * orders % length
    return 2.0 * math.pi / length * phases.astype(jnp.float32)


def complex_tables(length, modes):
    radians = angles(length, modes, True)
    factor = 1.0 / math.sqrt(length)
    cosines = jnp.cos(radians) * factor
    sine_table = jnp.sin(radians) * factor
    forward = jnp.stack(
        [jnp.stack([cosines, -sine_table], axis=1), jnp.stack([sine_table, cosines], axis=1)],
        axis=0,
    )
    cosine_rows = cosines.T
    sine_rows = sine_table.T
    inverse = jnp.stack(
        [jnp.stack([cosine_rows, sine_rows], axis=1), jnp.stack([-sine_rows, cosine_rows], axis=1)],
        axis=0,
    )
    return (forward.astype(jnp.bfloat16), inverse.astype(jnp.bfloat16))


def real_tables(length, modes):
    radians = angles(length, modes, False)
    factor = 1.0 / math.sqrt(length)
    cosines = jnp.cos(radians) * factor
    sine_table = jnp.sin(radians) * factor
    forward = jnp.concatenate([cosines, -sine_table], axis=1)
    doubled = jnp.where(
        jnp.arange(modes, dtype=jnp.int32) == 0, jnp.float32(1.0), jnp.float32(2.0)
    )[None, :]
    inverse = jnp.concatenate([(cosines * doubled).T, (-sine_table * doubled).T], axis=0)
    return (forward.astype(jnp.bfloat16), inverse.astype(jnp.bfloat16))


def flipped(table):
    return jnp.transpose(table, (2, 3, 0, 1))


def gelu_slope(preact):
    inner = root_coef * (preact + 0.044715 * preact * preact * preact)
    tangent = jnp.tanh(inner)
    return 0.5 * (1.0 + tangent) + 0.5 * preact * (1.0 - tangent * tangent) * root_coef * (
        1.0 + 3.0 * 0.044715 * preact * preact
    )


def product(form, left, right):
    return jnp.einsum(form, left, right, preferred_element_type=jnp.float32)


def partial_spectrum(values, table_third, table_second):
    channels, planes, grid_second = (values.shape[0], values.shape[1], values.shape[2])
    modes_third = table_third.shape[1] // 2
    modes_second = table_second.shape[3]
    third_done = product("cxyz,zj->cxjy", values, table_third).astype(jnp.bfloat16)
    third_done = third_done.reshape(channels, planes, 2, modes_third, grid_second)
    second_done = product("cxrky,rysm->cxskm", third_done, table_second).astype(jnp.bfloat16)
    return second_done.reshape(channels, planes, 2, modes_third * modes_second)


def partial_field(values, table_second, table_third):
    channels, planes = (values.shape[0], values.shape[1])
    modes_second = table_second.shape[1]
    modes_third = table_third.shape[0] // 2
    grid_second = table_second.shape[3]
    unfolded = values.reshape(channels, planes, 2, modes_third, modes_second)
    second_done = product("cxskm,smry->cxrky", unfolded, table_second).astype(jnp.bfloat16)
    second_done = second_done.reshape(channels, planes, 2 * modes_third, grid_second)
    return product("cxjy,jz->cxyz", second_done, table_third)


def first_spectrum(values, table_first):
    return product("cxrp,rxsm->smpc", values, table_first).astype(jnp.bfloat16)


def first_field(spectrum, table_first):
    return product("smpc,smrx->cxrp", spectrum, table_first).astype(jnp.bfloat16)


def mix_modes(spectrum, weights):
    products = product("smpc,tmpco->stmpo", spectrum, weights)
    return jnp.stack([products[0, 0] - products[1, 1], products[0, 1] + products[1, 0]]).astype(
        jnp.bfloat16
    )


def unmix_modes(gspectrum, weights):
    products = product("tmpco,smpo->tsmpc", weights, gspectrum)
    return jnp.stack([products[0, 0] + products[1, 1], products[0, 1] - products[1, 0]]).astype(
        jnp.bfloat16
    )


def weight_term(spectrum, gspectrum):
    products = product("smpc,tmpo->stmpco", spectrum, gspectrum)
    return jnp.stack([products[0, 0] + products[1, 1], products[0, 1] - products[1, 0]])


def body(field_in, cotangent, spectral_one, spectral_two, point_one, point_two, bias_one, bias_two):
    values = field_in[0]
    grad_out = cotangent[0]
    channels, planes, grid_second, grid_third = values.shape
    modes_first = spectral_one.shape[1]
    grid_first = planes * lax.axis_size("space")
    forward_first, inverse_first = complex_tables(grid_first, modes_first)
    forward_second, inverse_second = complex_tables(grid_second, MY)
    forward_third, inverse_third = real_tables(grid_third, MZ)

    def to_modes(partial_value, table_first):
        return first_spectrum(
            lax.all_to_all(partial_value, "space", split_axis=3, concat_axis=1, tiled=True),
            table_first,
        )

    def to_slabs(spectrum, table_first, table_second, table_third):
        return partial_field(
            lax.all_to_all(
                first_field(spectrum, table_first), "space", split_axis=1, concat_axis=3, tiled=True
            ),
            table_second,
            table_third,
        )

    def layer_forward(inputs, weights, point, bias):
        spectrum = to_modes(partial_spectrum(inputs, forward_third, forward_second), forward_first)
        branch = to_slabs(
            mix_modes(spectrum, weights), inverse_first, inverse_second, inverse_third
        )
        preact = product("cxyz,co->oxyz", inputs, point) + bias[:, None, None, None] + branch
        return (spectrum, preact)

    def adjoint_spectrum(grads):
        return to_modes(
            partial_spectrum(grads, inverse_third.T, flipped(inverse_second)),
            flipped(inverse_first),
        )

    def spectral_sum(spectrum, gspectrum):
        summed = lax.psum(weight_term(spectrum, gspectrum).astype(jnp.bfloat16), "dp")
        return summed

    spec_one, pre_one = layer_forward(values, spectral_one, point_one, bias_one)
    hidden = jax.nn.gelu(pre_one, approximate=True).astype(jnp.bfloat16)
    spec_two, pre_two = layer_forward(hidden, spectral_two, point_two, bias_two)
    grad_two = (grad_out.astype(jnp.float32) * gelu_slope(pre_two)).astype(jnp.bfloat16)
    gspec_two = adjoint_spectrum(grad_two)
    spectral_grad_two = spectral_sum(spec_two, gspec_two)
    returned = to_slabs(
        unmix_modes(gspec_two, spectral_two),
        flipped(forward_first),
        flipped(forward_second),
        forward_third.T,
    )
    grad_hidden = product("oxyz,co->cxyz", grad_two, point_two) + returned
    grad_one = (grad_hidden * gelu_slope(pre_one)).astype(jnp.bfloat16)
    gspec_one = adjoint_spectrum(grad_one)
    spectral_grad_one = spectral_sum(spec_one, gspec_one)
    point_term_one = product("cxyz,oxyz->co", values, grad_one)
    point_term_two = product("cxyz,oxyz->co", hidden, grad_two)
    bias_term_one = jnp.sum(grad_one.astype(jnp.float32), axis=(1, 2, 3))
    bias_term_two = jnp.sum(grad_two.astype(jnp.float32), axis=(1, 2, 3))
    point_sum_one, point_sum_two, bias_sum_one, bias_sum_two = lax.psum(
        (point_term_one, point_term_two, bias_term_one, bias_term_two), ("dp", "space")
    )
    factor = 1.0 / math.sqrt(lax.axis_size("dp") * grid_first * grid_second * grid_third)
    return (
        spectral_grad_one,
        spectral_grad_two,
        point_sum_one * factor,
        point_sum_two * factor,
        bias_sum_one * factor,
        bias_sum_two * factor,
    )


def solution(mesh):
    placed = (
        P("dp", None, "space", None, None),
        P("dp", None, "space", None, None),
        P(None, None, "space", None, None),
        P(None, None, "space", None, None),
        P(),
        P(),
        P(),
        P(),
    )
    return jax.shard_map(
        body,
        mesh=mesh,
        in_specs=placed,
        out_specs=(
            P(None, None, "space", None, None),
            P(None, None, "space", None, None),
            P(),
            P(),
            P(),
            P(),
        ),
        check_vma=False,
    )
```

profile of v0, /device:TPU:1, one launch (start us, length us, event | category | flops | bytes accessed | tf_op | source)
XLA Modules:
  0.0 354.1 jit_solution(14804572216067182446)
XLA Ops:
  13.6 15.1 %all-to-all-start = ((bf16[64,2,512]{2,1,0:T(2,128)(2,1)}), bf16[64,2,512]{2,1,0:T(2,128)(2,1)S(1)}, u32[]{:S(2)}, u32[]{:S(2)}) async-start(bf16[64,2,512]{2,1,0:T(2,128)(2,1)} %reshape.582), calls=%async_computation | async-start | bytes 262144 | tf_op jit(solution)/shard_map/all_to_all | solution.py:131
  28.8 8.7 %fusion.30 = f32[64,2,128,128]{3,0,2,1:T(8,128)} fusion(bf16[64,2,128,128]{3,2,1,0:T(8,128)(2,1)} %bitcast.396, bf16[64,64]{1,0:T(8,128)(2,1)S(1)} %copy-done.9), kind=kOutput, calls=%fused_computation.42 | convolution fusion | flops 268435456 | bytes 12591104 | tf_op jit(solution)/shard_map/cxyz,co->oxyz/dot_general | solution.py:68
  44.0 10.2 %all-to-all-start.1 = ((bf16[64,2,512]{2,1,0:T(2,128)(2,1)}), bf16[64,2,512]{2,1,0:T(2,128)(2,1)S(1)}, u32[]{:S(2)}, u32[]{:S(2)}) async-start(bf16[64,2,512]{2,1,0:T(2,128)(2,1)} %reshape.584), calls=%async_computation.1 | async-start | bytes 262144 | tf_op jit(solution)/shard_map/all_to_all | solution.py:137
  54.2 11.3 %all-to-all-done.1 = bf16[64,2,512]{2,1,0:T(2,128)(2,1)S(1)} async-done(((bf16[64,2,512]{2,1,0:T(2,128)(2,1)}), bf16[64,2,512]{2,1,0:T(2,128)(2,1)S(1)}, u32[]{:S(2)}, u32[]{:S(2)}) %all-to-all-start.1) | async-done | bytes 131104 | tf_op jit(solution)/shard_map/all_to_all | solution.py:137
  67.2 4.3 %copy.363 = bf16[64,2,32,128]{0,2,3,1:T(8,128)(2,1)} copy(bf16[64,2,32,128]{3,2,1,0:T(8,128)(2,1)S(1)} %bitcast.400) | data formatting | bytes 2097152 | tf_op jit(solution)/shard_map/reshape | solution.py:88
  71.5 11.8 %fusion.7 = (bf16[64,2,128,128]{3,0,2,1:T(8,128)(2,1)S(1)}, f32[64,2,128,128]{3,0,2,1:T(8,128)}) fusion(bf16[64,2,32,128]{0,2,3,1:T(8,128)(2,1)} %copy.363, bf16[16,128]{1,0:T(8,128)(2,1)S(1)} %get-tuple-element.74, bf16[16,128]{1,0:T(8,128)(2,1)S(1)} %get-tuple-element.75, f32[64,2,128,128]{3,0,2,1:T(8,128)} %fusion.30, f32[64]{0:T(128)S(1)} %copy-done.10), kind=kOutput, calls=%fused_computation.12 | convolution fusion | flops 157302784 | bytes 22028544 | tf_op jit(solution)/shard_map/cxjy,jz->cxyz/dot_general | solution.py:68
  92.0 5.4 %all-to-all-start.2 = ((bf16[64,2,512]{2,1,0:T(2,128)(2,1)}), bf16[64,2,512]{2,1,0:T(2,128)(2,1)S(1)}, u32[]{:S(2)}, u32[]{:S(2)}) async-start(bf16[64,2,512]{2,1,0:T(2,128)(2,1)} %reshape.586), calls=%async_computation.2 | async-start | bytes 262144 | tf_op jit(solution)/shard_map/all_to_all | solution.py:131
  97.5 11.2 %all-to-all-done.2 = bf16[64,2,512]{2,1,0:T(2,128)(2,1)S(1)} async-done(((bf16[64,2,512]{2,1,0:T(2,128)(2,1)}), bf16[64,2,512]{2,1,0:T(2,128)(2,1)S(1)}, u32[]{:S(2)}, u32[]{:S(2)}) %all-to-all-start.2) | async-done | bytes 131104 | tf_op jit(solution)/shard_map/all_to_all | solution.py:131
  111.2 4.9 %all-to-all-start.3 = ((bf16[64,2,512]{2,1,0:T(2,128)(2,1)}), bf16[64,2,512]{2,1,0:T(2,128)(2,1)S(1)}, u32[]{:S(2)}, u32[]{:S(2)}) async-start(bf16[64,2,512]{2,1,0:T(2,128)(2,1)} %reshape.588), calls=%async_computation.3 | async-start | bytes 262144 | tf_op jit(solution)/shard_map/all_to_all | solution.py:137
  116.1 6.8 %fusion.126 = f32[2,128,128,64]{2,3,1,0:T(8,128)} fusion(bf16[64,2,128,128]{3,0,2,1:T(8,128)(2,1)} %copy-done.2, bf16[64,64]{1,0:T(8,128)(2,1)S(1)} %copy-done.8), kind=kOutput, calls=%fused_computation.169 | convolution fusion | flops 268435456 | bytes 12591104 | tf_op jit(solution)/shard_map/cxyz,co->oxyz/dot_general | solution.py:68
  122.9 4.5 %all-to-all-done.3 = bf16[64,2,512]{2,1,0:T(2,128)(2,1)S(1)} async-done(((bf16[64,2,512]{2,1,0:T(2,128)(2,1)}), bf16[64,2,512]{2,1,0:T(2,128)(2,1)S(1)}, u32[]{:S(2)}, u32[]{:S(2)}) %all-to-all-start.3) | async-done | bytes 131104 | tf_op jit(solution)/shard_map/all_to_all | solution.py:137
  133.4 12.4 %convert_reduce_fusion = (f32[64]{0:T(128)S(1)}, bf16[64,2,128,128]{3,0,2,1:T(8,128)(2,1)S(1)}) fusion(bf16[64,2,32,128]{0,2,3,1:T(8,128)(2,1)} %copy.373, bf16[16,128]{1,0:T(8,128)(2,1)S(1)} %get-tuple-element.74, bf16[16,128]{1,0:T(8,128)(2,1)S(1)} %get-tuple-element.75, f32[2,128,128,64]{2,3,1,0:T(8,128)} %fusion.126, f32[64]{0:T(128)S(1)} %copy-done.11, ...), kind=kOutput, calls=%fused_computation.29 | convolution fusion | flops 184565696 | bytes 17834496 | tf_op jit(solution)/shard_map/cxjy,jz->cxyz/dot_general | solution.py:68
  154.5 7.7 %all-to-all-start.4 = ((bf16[64,2,512]{2,1,0:T(2,128)(2,1)}), bf16[64,2,512]{2,1,0:T(2,128)(2,1)S(1)}, u32[]{:S(2)}, u32[]{:S(2)}) async-start(bf16[64,2,512]{2,1,0:T(2,128)(2,1)} %reshape.590), calls=%async_computation.4 | async-start | bytes 262144 | tf_op jit(solution)/shard_map/all_to_all | solution.py:131
  162.2 6.7 %fusion.124 = f32[2,128,128,64]{2,3,1,0:T(8,128)} fusion(bf16[64,2,128,128]{3,0,2,1:T(8,128)(2,1)} %copy-done.3, bf16[64,64]{1,0:T(8,128)(2,1)S(1)} %copy-done.8), kind=kOutput, calls=%fused_computation.167 | convolution fusion | flops 268435456 | bytes 12591104 | tf_op jit(solution)/shard_map/oxyz,co->cxyz/dot_general | solution.py:68
  168.9 4.6 %all-to-all-done.4 = bf16[64,2,512]{2,1,0:T(2,128)(2,1)S(1)} async-done(((bf16[64,2,512]{2,1,0:T(2,128)(2,1)}), bf16[64,2,512]{2,1,0:T(2,128)(2,1)S(1)}, u32[]{:S(2)}, u32[]{:S(2)}) %all-to-all-start.4) | async-done | bytes 131104 | tf_op jit(solution)/shard_map/all_to_all | solution.py:131
  177.3 7.8 %all-to-all-start.5 = ((bf16[64,2,512]{2,1,0:T(2,128)(2,1)}), bf16[64,2,512]{2,1,0:T(2,128)(2,1)S(1)}, u32[]{:S(2)}, u32[]{:S(2)}) async-start(bf16[64,2,512]{2,1,0:T(2,128)(2,1)} %reshape.592), calls=%async_computation.5 | async-start | bytes 262144 | tf_op jit(solution)/shard_map/all_to_all | solution.py:137
  189.2 7.2 %all-to-all-done.5 = bf16[64,2,512]{2,1,0:T(2,128)(2,1)S(1)} async-done(((bf16[64,2,512]{2,1,0:T(2,128)(2,1)}), bf16[64,2,512]{2,1,0:T(2,128)(2,1)S(1)}, u32[]{:S(2)}, u32[]{:S(2)}) %all-to-all-start.5) | async-done | bytes 131104 | tf_op jit(solution)/shard_map/all_to_all | solution.py:137
  202.4 10.5 %convert_reduce_fusion.1 = (f32[64]{0:T(128)S(1)}, bf16[64,2,128,128]{3,0,2,1:T(8,128)(2,1)S(1)}) fusion(f32[64,2,128,128]{3,0,2,1:T(8,128)} %get-tuple-element.67, bf16[64,2,32,128]{0,2,3,1:T(8,128)(2,1)} %copy.386, bf16[128,16]{0,1:T(8,128)(2,1)S(1)} %get-tuple-element.72, bf16[128,16]{0,1:T(8,128)(2,1)S(1)} %get-tuple-element.73, ...), kind=kOutput, calls=%fused_computation.30 | convolution fusion | flops 180371392 | bytes 22028544 | tf_op jit(solution)/shard_map/cxjy,jz->cxyz/dot_general | solution.py:68
  221.5 5.0 %all-to-all-start.6 = ((bf16[64,2,512]{2,1,0:T(2,128)(2,1)}), bf16[64,2,512]{2,1,0:T(2,128)(2,1)S(1)}, u32[]{:S(2)}, u32[]{:S(2)}) async-start(bf16[64,2,512]{2,1,0:T(2,128)(2,1)} %reshape.594), calls=%async_computation.6 | async-start | bytes 262144 | tf_op jit(solution)/shard_map/all_to_all | solution.py:131
  226.7 4.5 %fusion.75 = (bf16[1,16,4,64,64]{4,3,2,1,0:T(8,128)(2,1)S(1)}, bf16[1,16,4,64,64]{4,3,2,1,0:T(8,128)(2,1)S(1)}) fusion(f32[2,2,16,4,64,64]{5,4,3,2,1,0:T(8,128)} %multiply_bitcast_fusion), kind=kLoop, calls=%fused_computation.101 | loop fusion | flops 1048576 | bytes 5242880 | tf_op jit(solution)/shard_map/add | solution.py:116
  233.0 5.0 %all-to-all-done.6 = bf16[64,2,512]{2,1,0:T(2,128)(2,1)S(1)} async-done(((bf16[64,2,512]{2,1,0:T(2,128)(2,1)}), bf16[64,2,512]{2,1,0:T(2,128)(2,1)S(1)}, u32[]{:S(2)}, u32[]{:S(2)}) %all-to-all-start.6) | async-done | bytes 131104 | tf_op jit(solution)/shard_map/all_to_all | solution.py:131
  243.3 4.8 %convolution_bitcast_fusion.11 = f32[64,64]{0,1:T(8,128)S(1)} fusion(bf16[64,2,128,128]{3,0,2,1:T(8,128)(2,1)} %copy-done.2, bf16[64,2,128,128]{3,0,2,1:T(8,128)(2,1)} %copy-done.3), kind=kOutput, calls=%fused_computation.98 | convolution fusion | flops 268435456 | bytes 8404992 | tf_op jit(solution)/shard_map/cxyz,oxyz->co/dot_general | solution.py:68
  253.4 78.4 %all-reduce = (f32[64,64]{0,1:T(8,128)S(1)}, f32[64,64]{0,1:T(8,128)S(1)}, f32[64]{0:T(128)S(1)}, f32[64]{0:T(128)S(1)}) all-reduce(f32[64,64]{0,1:T(8,128)S(1)} %fusion.70, f32[64,64]{0,1:T(8,128)S(1)} %convolution_bitcast_fusion.11, f32[64]{0:T(128)S(1)} %get-tuple-element.68, ...), channel_id=1, replica_groups=mesh['dp'=4,'space'=64] {'dp','space'}, use_global_device_ids=true, to_apply=%region_2.3 | all-reduce | flops 8320 | bytes 66560 | tf_op jit(solution)/shard_map/psum | solution.py:182
  334.3 7.8 %all-reduce.4.cloned.1.call-done = (bf16[2,16,4,64,64]{4,3,2,1,0:T(8,128)(2,1)}, bf16[2,16,4,64,64]{4,3,2,1,0:T(8,128)(2,1)}) async-done(((bf16[2,16,4,64,64]{4,3,2,1,0:T(8,128)(2,1)}, bf16[2,16,4,64,64]{4,3,2,1,0:T(8,128)(2,1)}), (bf16[2,16,4,64,64]{4,3,2,1,0:T(8,128)(2,1)}, bf16[2,16,4,64,64]{4,3,2,1,0:T(8,128)(2,1)})) %all-reduce.4.cloned.1.call-update) | async-done | bytes 2097168 | tf_op jit(solution)/shard_map/psum | solution.py:159
  (126 shorter events, 82.1 us)
Async XLA Ops:
  7.2 102.3 %copy-start = (bf16[2,16,4,64,64]{4,3,2,1,0:T(8,128)(2,1)S(1)}, bf16[2,16,4,64,64]{4,3,2,1,0:T(8,128)(2,1)}, u32[]{:S(2)}) copy-start(bf16[2,16,4,64,64]{4,3,2,1,0:T(8,128)(2,1)} %param.11) | copy-start | bytes 3145732
  7.2 21.6 %copy-start.9 = (bf16[64,64]{1,0:T(8,128)(2,1)S(1)}, bf16[64,64]{1,0:T(8,128)(2,1)}, u32[]{:S(2)}) copy-start(bf16[64,64]{1,0:T(8,128)(2,1)} %param.12) | copy-start | bytes 24580
  13.6 26.4 %all-to-all-start = ((bf16[64,2,512]{2,1,0:T(2,128)(2,1)}), bf16[64,2,512]{2,1,0:T(2,128)(2,1)S(1)}, u32[]{:S(2)}, u32[]{:S(2)}) async-start(bf16[64,2,512]{2,1,0:T(2,128)(2,1)} %reshape.582), calls=%async_computation | async-start | bytes 262144 | tf_op jit(solution)/shard_map/all_to_all | solution.py:131
  44.0 27.5 %copy-start.10 = (f32[64]{0:T(128)S(1)}, f32[64]{0:T(128)}, u32[]{:S(2)}) copy-start(f32[64]{0:T(128)} %param.14) | copy-start | bytes 772
  44.0 21.6 %all-to-all-start.1 = ((bf16[64,2,512]{2,1,0:T(2,128)(2,1)}), bf16[64,2,512]{2,1,0:T(2,128)(2,1)S(1)}, u32[]{:S(2)}, u32[]{:S(2)}) async-start(bf16[64,2,512]{2,1,0:T(2,128)(2,1)} %reshape.584), calls=%async_computation.1 | async-start | bytes 262144 | tf_op jit(solution)/shard_map/all_to_all | solution.py:137
  83.3 2.0 copy-start.2
  89.6 26.5 %copy-start.8 = (bf16[64,64]{1,0:T(8,128)(2,1)S(1)}, bf16[64,64]{1,0:T(8,128)(2,1)}, u32[]{:S(2)}) copy-start(bf16[64,64]{1,0:T(8,128)(2,1)} %param.13) | copy-start | bytes 24580
  92.0 16.7 %all-to-all-start.2 = ((bf16[64,2,512]{2,1,0:T(2,128)(2,1)}), bf16[64,2,512]{2,1,0:T(2,128)(2,1)S(1)}, u32[]{:S(2)}, u32[]{:S(2)}) async-start(bf16[64,2,512]{2,1,0:T(2,128)(2,1)} %reshape.586), calls=%async_computation.2 | async-start | bytes 262144 | tf_op jit(solution)/shard_map/all_to_all | solution.py:131
  111.2 16.3 %all-to-all-start.3 = ((bf16[64,2,512]{2,1,0:T(2,128)(2,1)}), bf16[64,2,512]{2,1,0:T(2,128)(2,1)S(1)}, u32[]{:S(2)}, u32[]{:S(2)}) async-start(bf16[64,2,512]{2,1,0:T(2,128)(2,1)} %reshape.588), calls=%async_computation.3 | async-start | bytes 262144 | tf_op jit(solution)/shard_map/all_to_all | solution.py:137
  122.9 10.5 %copy-start.11 = (f32[64]{0:T(128)S(1)}, f32[64]{0:T(128)}, u32[]{:S(2)}) copy-start(f32[64]{0:T(128)} %param.15) | copy-start | bytes 772
  145.8 2.0 copy-start.3
  154.5 19.0 %all-to-all-start.4 = ((bf16[64,2,512]{2,1,0:T(2,128)(2,1)}), bf16[64,2,512]{2,1,0:T(2,128)(2,1)S(1)}, u32[]{:S(2)}, u32[]{:S(2)}) async-start(bf16[64,2,512]{2,1,0:T(2,128)(2,1)} %reshape.590), calls=%async_computation.4 | async-start | bytes 262144 | tf_op jit(solution)/shard_map/all_to_all | solution.py:131
  177.3 19.1 %all-to-all-start.5 = ((bf16[64,2,512]{2,1,0:T(2,128)(2,1)}), bf16[64,2,512]{2,1,0:T(2,128)(2,1)S(1)}, u32[]{:S(2)}, u32[]{:S(2)}) async-start(bf16[64,2,512]{2,1,0:T(2,128)(2,1)} %reshape.592), calls=%async_computation.5 | async-start | bytes 262144 | tf_op jit(solution)/shard_map/all_to_all | solution.py:137
  212.8 2.0 copy-start.5
  221.5 16.4 %all-to-all-start.6 = ((bf16[64,2,512]{2,1,0:T(2,128)(2,1)}), bf16[64,2,512]{2,1,0:T(2,128)(2,1)S(1)}, u32[]{:S(2)}, u32[]{:S(2)}) async-start(bf16[64,2,512]{2,1,0:T(2,128)(2,1)} %reshape.594), calls=%async_computation.6 | async-start | bytes 262144 | tf_op jit(solution)/shard_map/all_to_all | solution.py:131
  226.6 115.4 %all-reduce.4.cloned.1.call-start = ((), (), s32[]{:S(2)}) async-start(), calls=%async_computation.7 | async-start | bytes 8388608 | tf_op jit(solution)/shard_map/psum | solution.py:159
  243.3 4.9 %copy-start.4 = (bf16[1,64,2,128,128]{4,3,2,1,0:T(8,128)(2,1)S(1)}, bf16[1,64,2,128,128]{4,3,2,1,0:T(8,128)(2,1)}, u32[]{:S(2)}) copy-start(bf16[1,64,2,128,128]{4,3,2,1,0:T(8,128)(2,1)} %param.8) | copy-start | bytes 12582916
  243.3 5.9 %copy-start.6 = (bf16[64,2,128,128]{3,0,2,1:T(8,128)(2,1)S(1)}, bf16[64,2,128,128]{3,0,2,1:T(8,128)(2,1)}, u32[]{:S(2)}) copy-start(bf16[64,2,128,128]{3,0,2,1:T(8,128)(2,1)} %copy-done.5) | copy-start | bytes 12582916
  342.0 3.3 copy-start.7
  342.0 4.7 %copy-start.1 = (bf16[2,16,4,64,64]{4,3,2,1,0:T(8,128)(2,1)S(1)}, bf16[2,16,4,64,64]{4,3,2,1,0:T(8,128)(2,1)}, u32[]{:S(2)}) copy-start(bf16[2,16,4,64,64]{4,3,2,1,0:T(8,128)(2,1)} %param.11) | copy-start | bytes 3145732
Sparse Core Ops, SparseCore 0:
  243.4 98.6 all-reduce.3
where the time goes:
time: 361 us; the launch traced here: 354 us
  matrix products  94.5 us (26%)
  blocking collectives  78.4 us (22%)
  starting transfers between devices  56.1 us (16%)
  waiting for transfers between devices  54 us (15%)
  local copies, waits for them, and re-layouts  39.4 us (11%)
  other arithmetic  16.4 us (5%)
  between operations  15.2 us (4%)
    dot_general x29, matrix products, product(): return jnp.einsum(form, left, right, preferred_element_type=jnp.float32)  94.5 us
    psum x1, blocking collectives, body(): lax.psum((point_term_one, point_term_two, bias_term_one, bias_term_two),...  78.4 us
    all_to_all x4, starting transfers between devices, to_modes(): lax.all_to_all(partial_value, 'space', split_axis=3, concat_axis=1, tiled...  33.2 us
    all_to_all x4, waiting for transfers between devices, to_modes(): lax.all_to_all(partial_value, 'space', split_axis=3, concat_axis=1, tiled...  23.2 us
    all_to_all x3, waiting for transfers between devices, to_slabs(): lax.all_to_all(first_field(spectrum, table_first), 'space', split_axis=1,...  23 us
    all_to_all x3, starting transfers between devices, to_slabs(): lax.all_to_all(first_field(spectrum, table_first), 'space', split_axis=1,...  22.9 us
    unnamed x42, local copies, waits for them, and re-layouts  20.5 us
    reshape x3, local copies, waits for them, and re-layouts, partial_field(): second_done.reshape(channels, planes, 2 * modes_third, grid_second)  12.9 us
  transfers between devices with their start and end apart: 8, of which 8 were waited for; matrix products, arithmetic and copies ran while one was open for 13% of the time, Pallas kernels for 0%

commit v1 on v0

v1 whole, which is shorter than its diff:
```python
import functools
import math

import jax
import jax.numpy as jnp
import numpy as np
from jax import lax
from jax.experimental import pallas as pl
from jax.experimental.pallas import tpu as pltpu
from jax.sharding import PartitionSpec as P

MY = 16
MZ = 16
CHANNELS = 64
LANES = 128
ROOT = math.sqrt(2.0 / math.pi)
CUBIC = 0.044715
F32 = jnp.float32
BF16 = jnp.bfloat16
VMEM_LIMIT = 44 * 1024 * 1024


def angles(length, modes, two_sided):
    places = np.arange(length, dtype=np.int64)[:, None]
    orders = np.arange(modes, dtype=np.int64)[None, :]
    if two_sided:
        orders = np.where(orders < modes // 2, orders, orders - modes + length)
    phases = places * orders % length
    return np.float32(2.0 * math.pi / length) * phases.astype(np.float32)


def complex_tables(length, modes):
    radians = angles(length, modes, True)
    factor = np.float32(1.0 / math.sqrt(length))
    cosines = np.cos(radians) * factor
    sines = np.sin(radians) * factor
    forward = np.stack(
        [np.stack([cosines, -sines], axis=1), np.stack([sines, cosines], axis=1)], axis=0
    )
    inverse = np.stack(
        [np.stack([cosines.T, sines.T], axis=1), np.stack([-sines.T, cosines.T], axis=1)], axis=0
    )
    return forward.astype(BF16), inverse.astype(BF16)


def real_tables(length, modes):
    radians = angles(length, modes, False)
    factor = np.float32(1.0 / math.sqrt(length))
    cosines = np.cos(radians) * factor
    sines = np.sin(radians) * factor
    forward = np.concatenate([cosines, -sines], axis=1)
    doubled = np.where(np.arange(modes) == 0, 1.0, 2.0).astype(np.float32)[None, :]
    inverse = np.concatenate([(cosines * doubled).T, (-sines * doubled).T], axis=0)
    return forward.astype(BF16), inverse.astype(BF16)


def flipped(table):
    return np.transpose(table, (2, 3, 0, 1))


def second_natural(table):
    length = table.shape[1]
    split = table.reshape(2, length, 2, MY // 4, 4)
    return split.transpose(3, 2, 4, 0, 1).reshape(2 * MY, 2 * length)


def second_paired(table):
    length = table.shape[1]
    split = table.reshape(2, length // 2, 2, 2, MY // 4, 4)
    return split.transpose(2, 4, 3, 5, 0, 1).reshape(4 * MY, length)


def second_inverse(table):
    length = table.shape[3]
    split = table.reshape(2, MY // 4, 4, 2, length // 2, 2)
    return split.transpose(3, 4, 5, 1, 0, 2).reshape(length, 4 * MY)


def first_forward(table):
    length, modes = table.shape[1], table.shape[3]
    split = table.reshape(2, length // 2, 2, 2, modes)
    return split.transpose(2, 3, 4, 0, 1).reshape(4 * modes, length)


def first_inverse(table):
    modes, length = table.shape[1], table.shape[3]
    split = table.reshape(2, modes, 2, length // 2, 2)
    return split.transpose(2, 3, 4, 0, 1).reshape(length, 4 * modes)


def twice_diagonal(table):
    zero = np.zeros_like(table)
    return np.block([[table, zero], [zero, table]])


def mm(left, right):
    return lax.dot_general(left, right, (((1,), (0,)), ((), ())), preferred_element_type=F32)


def nt(left, right):
    return lax.dot_general(left, right, (((1,), (1,)), ((), ())), preferred_element_type=F32)


def tn(left, right):
    return lax.dot_general(left, right, (((0,), (0,)), ((), ())), preferred_element_type=F32)


def side(rows):
    return lax.broadcasted_iota(jnp.int32, (rows, LANES), 1) < LANES // 2


def turned(values):
    return pltpu.roll(values, LANES // 2, 1)


def whole(shape):
    return pl.BlockSpec(shape, lambda *_: (0,) * len(shape))


VM = pl.BlockSpec(memory_space=pltpu.VMEM)


GROUPS = 8
ROWS = 2 * LANES * CHANNELS


def near(value):
    return pltpu.with_memory_space_constraint(value, pltpu.VMEM)


def call(
    kernel, outs, scratch, flops, moved, *operands, big=(), kinds=(), plain=(), token=None
):
    cut = ROWS // GROUPS
    counts = [
        len(operands),
        len(big),
        0 if token is None else 1,
        len(outs),
        len(kinds),
        len(plain),
        len(scratch),
        len(outs),
        len(big),
        len(kinds),
        3,
    ]

    def whole_kernel(*refs):
        parts = []
        at = 0
        for count in counts:
            parts.append(refs[at : at + count])
            at += count
        small, big_far, _, outs_far, kinds_far, plains, own, outs_near, big_near, kinds_near, sems = parts
        in_sem, out_sem, end_sem = sems

        def group_of(far, close, sem, index, group, out):
            rows = pl.ds(pl.multiple_of(group * cut, cut), cut)
            pair = (close.at[rows], far.at[rows]) if out else (far.at[rows], close.at[rows])
            return pltpu.make_async_copy(*pair, sem.at[index, group])

        def coming(index, group):
            return group_of(big_far[index], big_near[index], in_sem, index, group, False)

        def going(index, group):
            return group_of(kinds_far[index], kinds_near[index], out_sem, index, group, True)

        for group in range(GROUPS):
            for index in range(len(big)):
                coming(index, group).start()

        def loop(body, carry=0, unroll=4):
            per = PAIRS // GROUPS

            def some(i, carry):
                for j in range(unroll):
                    carry = body(i * unroll + j, carry)
                return carry

            def each(group, carry):
                for index in range(len(big)):
                    coming(index, group).wait()
                first = group * (per // unroll)
                carry = lax.fori_loop(first, first + per // unroll, some, carry)
                for index in range(len(kinds)):
                    going(index, group).start()
                return carry

            return lax.fori_loop(0, GROUPS, each, carry)

        kernel(small, big_near, outs_near, kinds_near, plains, own, loop)
        last = [
            pltpu.make_async_copy(close, far, end_sem.at[index])
            for index, (close, far) in enumerate(zip(outs_near, outs_far))
        ]
        for copy in last:
            copy.start()
        for index in range(len(kinds)):
            for group in range(GROUPS):
                going(index, group).wait()
        for copy in last:
            copy.wait()

    operands = [near(operand) for operand in operands]
    far = pl.BlockSpec(memory_space=pl.ANY)
    extra = [] if token is None else [token]
    shapes = [pltpu.HBM(shape, kind) for shape, kind in outs]
    shapes += [pltpu.HBM((ROWS, LANES), kind) for kind in kinds]
    return pl.pallas_call(
        whole_kernel,
        out_shape=shapes + list(plain),
        in_specs=[VM] * len(operands) + [far] * (len(big) + len(extra)),
        out_specs=[far] * len(shapes) + [VM] * len(plain),
        scratch_shapes=list(scratch)
        + [pltpu.VMEM(shape, kind) for shape, kind in outs]
        + [pltpu.VMEM((ROWS, LANES), array.dtype) for array in big]
        + [pltpu.VMEM((ROWS, LANES), kind) for kind in kinds]
        + [
            pltpu.SemaphoreType.DMA((max(len(big), 1), GROUPS)),
            pltpu.SemaphoreType.DMA((max(len(kinds), 1), GROUPS)),
            pltpu.SemaphoreType.DMA((max(len(outs), 1),)),
        ],
        cost_estimate=pl.CostEstimate(flops=flops, bytes_accessed=moved, transcendentals=0),
        compiler_params=pltpu.CompilerParams(vmem_limit_bytes=VMEM_LIMIT),
    )(*operands, *big, *extra)


C_STEP = 8


def spectrum_kernel(field, third_far, second_far, out_far, near_field, third_ref, second_ref, chunk, spec, sems, extra):
    def coming(step):
        cut = pl.ds(step * C_STEP, C_STEP)
        return pltpu.make_async_copy(field.at[0, cut], near_field.at[cut], sems.at[step])

    tables = [
        pltpu.make_async_copy(third_far, third_ref, extra.at[0]),
        pltpu.make_async_copy(second_far, second_ref, extra.at[1]),
    ]
    for copy in tables:
        copy.start()
    for step in range(CHANNELS // C_STEP):
        coming(step).start()
    for copy in tables:
        copy.wait()
    third = third_ref[...]

    def some(step, carry):
        coming(step).wait()
        for x in range(2):
            rows = near_field[pl.ds(step * C_STEP, C_STEP), x].reshape(C_STEP * LANES, LANES)
            done = nt(third, rows)
            for c in range(C_STEP):
                place = pl.multiple_of((x * CHANNELS + step * C_STEP + c) * 2 * MZ, 2 * MZ)
                spec[pl.ds(place, 2 * MZ), :] = done[:, c * LANES : (c + 1) * LANES]
        return carry

    lax.fori_loop(0, CHANNELS // C_STEP, some, 0)
    second = second_ref[...]
    for k in range(MZ):
        real = spec[pl.ds(k, LANES, stride=2 * MZ), :]
        imag = spec[pl.ds(MZ + k, LANES, stride=2 * MZ), :]
        both = jnp.concatenate([real, imag], axis=1).astype(BF16)
        chunk[k * 32 : (k + 1) * 32, :] = nt(second, both).astype(BF16)
    out = pltpu.make_async_copy(chunk, out_far, extra.at[2])
    out.start()
    out.wait()


def first_partial(field, third, second):
    far = pl.BlockSpec(memory_space=pl.ANY)
    return pl.pallas_call(
        spectrum_kernel,
        out_shape=pltpu.HBM((512, LANES), BF16),
        in_specs=[far] * 3,
        out_specs=far,
        scratch_shapes=[
            pltpu.VMEM(field.shape[1:], BF16),
            pltpu.VMEM(third.shape, BF16),
            pltpu.VMEM(second.shape, BF16),
            pltpu.VMEM((512, LANES), BF16),
            pltpu.VMEM((4096, LANES), F32),
            pltpu.SemaphoreType.DMA((CHANNELS // C_STEP,)),
            pltpu.SemaphoreType.DMA((3,)),
        ],
        cost_estimate=pl.CostEstimate(
            flops=600_000_000, bytes_accessed=6 << 20, transcendentals=0
        ),
        compiler_params=pltpu.CompilerParams(vmem_limit_bytes=VMEM_LIMIT),
    )(field, third, second)


Y_STEP = 16
Y_STEPS = LANES // Y_STEP
Y_ROWS = Y_STEP * CHANNELS


def relay_kernel(pointed, *refs):
    if pointed:
        point_ref, bias_ref = refs[:2]
        refs = refs[2:]
    outs = 2 if pointed else 1
    field = refs[0]
    out_far = refs[2 : 2 + outs]
    near_field = refs[2 + outs]
    out_near = refs[3 + outs : 3 + 2 * outs]
    rows_ref, in_sem, out_sem = refs[3 + 2 * outs :]

    def coming(step):
        x = step // Y_STEPS
        cut = pl.ds(pl.multiple_of((step % Y_STEPS) * Y_STEP, Y_STEP), Y_STEP)
        return pltpu.make_async_copy(
            field.at[0, :, x, cut], near_field.at[:, x, cut], in_sem.at[step]
        )

    def going(index, step):
        cut = pl.ds(pl.multiple_of(step * Y_ROWS, Y_ROWS), Y_ROWS)
        return pltpu.make_async_copy(
            out_near[index].at[cut], out_far[index].at[cut], out_sem.at[index, step]
        )

    for step in range(2 * Y_STEPS):
        coming(step).start()
    if pointed:
        point = point_ref[...]
        shift = jnp.concatenate([bias_ref[...], bias_ref[...]], axis=1)

    def some(step, carry):
        coming(step).wait()
        at = pl.multiple_of((step % Y_STEPS) * Y_STEP, Y_STEP)
        rows_ref[...] = (
            near_field[:, step // Y_STEPS, pl.ds(at, Y_STEP), :].astype(F32).reshape(Y_ROWS, LANES)
        )
        for y in range(0, Y_STEP, 2):
            pair = [rows_ref[pl.ds(y + e, CHANNELS, stride=Y_STEP), :] for e in range(2)]
            tile = step * (Y_STEP // 2) + y // 2
            out_near[0][tile_at(tile), :] = jnp.concatenate(pair, axis=0).astype(BF16)
            if pointed:
                wide = jnp.concatenate(pair, axis=1).astype(BF16)
                store_wide(out_near[1], tile, mm(point, wide) + shift)
        for index in range(outs):
            going(index, step).start()
        return carry

    lax.fori_loop(0, 2 * Y_STEPS, some, 0)
    for step in range(2 * Y_STEPS):
        for index in range(outs):
            going(index, step).wait()


def relay(field, *operands, token):
    far = pl.BlockSpec(memory_space=pl.ANY)
    pointed = bool(operands)
    outs = 2 if pointed else 1
    return pl.pallas_call(
        functools.partial(relay_kernel, pointed),
        out_shape=[pltpu.HBM((ROWS, LANES), BF16)] * outs,
        in_specs=[VM] * len(operands) + [far] * 2,
        out_specs=[far] * outs,
        scratch_shapes=[pltpu.VMEM(field.shape[1:], BF16)]
        + [pltpu.VMEM((ROWS, LANES), BF16)] * outs
        + [
            pltpu.VMEM((Y_ROWS, LANES), F32),
            pltpu.SemaphoreType.DMA((2 * Y_STEPS,)),
            pltpu.SemaphoreType.DMA((outs, 2 * Y_STEPS)),
        ],
        cost_estimate=pl.CostEstimate(
            flops=600_000_000, bytes_accessed=12 << 20, transcendentals=0
        ),
        compiler_params=pltpu.CompilerParams(vmem_limit_bytes=VMEM_LIMIT),
    )(*[near(operand) for operand in operands], field, token)


def own_spectrum(wide, table, place, block=8):
    real = wide[pl.ds(place, 64, stride=block), :]
    imag = wide[pl.ds(4 + place, 64, stride=block), :]
    both = mm(table, jnp.concatenate([real, imag], axis=0).astype(BF16))
    return both[:32, :CHANNELS] + both[32:, CHANNELS:]


def send_field(mixed, table, place, sent, block=8):
    twin = jnp.concatenate([mixed, mixed], axis=1)
    left = side(32)
    both = jnp.concatenate([jnp.where(left, twin, 0.0), jnp.where(left, 0.0, twin)], axis=0)
    out = mm(table, both.astype(BF16))
    sent[pl.ds(place, 64, stride=block), :] = out[:64]
    sent[pl.ds(4 + place, 64, stride=block), :] = out[64:]


def mode_lanes(modes):
    row = lax.broadcasted_iota(jnp.int32, (32, LANES), 0) % modes
    half = lax.broadcasted_iota(jnp.int32, (32, LANES), 1) // CHANNELS
    return row, half


def mix_kernel(small, _, outs, __, ___, scratch, loop):
    got_ref, weight_ref, forward_ref, inverse_ref = small
    out_ref, spec_ref = outs
    wide, sent = scratch
    wide[...] = got_ref[...].astype(F32)
    forward = forward_ref[...]
    inverse = inverse_ref[...]
    modes = weight_ref.shape[1]
    row, half = mode_lanes(modes)
    for p in range(4):
        spec = own_spectrum(wide, forward, p).astype(BF16)
        spec_ref[:, p * CHANNELS : (p + 1) * CHANNELS] = spec
        spec = spec.astype(F32)
        other = jnp.concatenate([-spec[modes:], spec[:modes]], axis=0)
        pieces = []
        for part in (spec, other):
            twin = jnp.concatenate([part, part], axis=1)
            for pair in range(modes // 2):
                pieces.append(jnp.where(row == 2 * pair + half, twin, 0.0).astype(BF16))
        spread = jnp.concatenate(pieces, axis=1)
        weights = weight_ref[:, :, p].reshape(2 * modes * CHANNELS, CHANNELS)
        mixed = mm(spread, weights).astype(BF16).astype(F32)
        send_field(mixed, inverse, p, sent)
    out_ref[...] = sent[...].astype(BF16)


def high_low(values):
    high = values.astype(BF16).astype(F32)
    return jnp.concatenate([high, values - high], axis=1)


def unmix_kernel(small, _, outs, __, ___, scratch, loop):
    got_ref, weight_ref, forward_ref, inverse_ref, term_ref, one_ref, two_ref = small
    out_ref, spec_ref = outs
    wide, sent = scratch
    wide[...] = got_ref[...].astype(F32)
    forward = forward_ref[...]
    inverse = inverse_ref[...]
    modes = weight_ref.shape[1]
    row, half = mode_lanes(modes)
    spec_ref[0:32, :] = one_ref[...]
    spec_ref[32:64, :] = two_ref[...]
    sent[...] = jnp.zeros_like(sent)
    terms = high_low(term_ref[...])
    sent[pl.ds(8, 64, stride=16), :] = terms[:CHANNELS]
    sent[pl.ds(9, 64, stride=16), :] = jnp.broadcast_to(
        terms[CHANNELS : CHANNELS + 1], (CHANNELS, LANES)
    )
    for p in range(4):
        spec = own_spectrum(wide, forward, p).astype(BF16)
        spec_ref[64:96, p * CHANNELS : (p + 1) * CHANNELS] = spec
        other = jnp.concatenate([spec[modes:].astype(F32), -spec[:modes].astype(F32)], axis=0)
        products = nt(spec, weight_ref[0, :, p].reshape(modes * CHANNELS, CHANNELS)) + nt(
            other.astype(BF16), weight_ref[1, :, p].reshape(modes * CHANNELS, CHANNELS)
        )
        total = jnp.zeros((32, LANES), F32)
        for pair in range(modes // 2):
            piece = products[:, pair * LANES : (pair + 1) * LANES]
            total = total + jnp.where(row == 2 * pair + half, piece, 0.0)
        mixed = (total + turned(total))[:, :CHANNELS].astype(BF16).astype(F32)
        send_field(mixed, inverse, p, sent, 16)
    out_ref[...] = sent[...].astype(BF16)


def last_kernel(small, _, outs, __, ___, scratch, loop):
    got_ref, forward_ref = small
    (out_ref,) = outs
    (wide,) = scratch
    for d in range(64):
        wide[d * 48 : (d + 1) * 48, :] = got_ref[d * 48 : (d + 1) * 48, :].astype(F32)
    forward = forward_ref[...]
    for p in range(4):
        out_ref[0:32, p * CHANNELS : (p + 1) * CHANNELS] = own_spectrum(
            wide, forward, p, 48
        ).astype(BF16)
    total = jnp.zeros((40, LANES), F32)
    for d in range(64):
        total = total + wide[d * 48 + 8 : (d + 1) * 48, :]
    high = total.astype(BF16)
    low = (total - high.astype(F32)).astype(BF16)
    out_ref[32:64, :] = jnp.concatenate([high[:32], low[:32]], axis=1)
    rows = wide[pl.ds(41, 64, stride=48), :]
    out_ref[64:96, :] = jnp.concatenate([rows[:32], rows[32:]], axis=1).astype(BF16)
    biases = jnp.concatenate(
        [
            high_low(total[32:40, :CHANNELS]),
            jnp.broadcast_to(wide[42:43, :], (8, LANES)),
        ],
        axis=1,
    )
    out_ref[96:112, :] = jnp.concatenate([biases, biases], axis=0).astype(BF16)


CHUNK = ((512, LANES), BF16)
SPECTRUM = ((32, 4 * CHANNELS), BF16)
WIDE = pltpu.VMEM((512, LANES), F32)


def mixing(got, weights, forward, inverse, token):
    return call(
        mix_kernel,
        [CHUNK, SPECTRUM],
        [WIDE, WIDE],
        200_000_000,
        3 << 20,
        got,
        weights,
        forward,
        inverse,
        token=token,
    )


def outer_products(spec, grad, out_ref):
    modes = out_ref.shape[1]
    depth = spec.shape[0]
    lane = lax.broadcasted_iota(jnp.int32, (CHANNELS, depth), 1) % modes
    other = []
    for n in range(depth // (2 * modes)):
        at = n * 2 * modes
        other += [grad[at + modes : at + 2 * modes], -grad[at : at + modes]]
    other = jnp.concatenate(other, axis=0)
    for p in range(4):
        cut = slice(p * CHANNELS, (p + 1) * CHANNELS)
        both = jnp.concatenate([grad[:, cut], other[:, cut]], axis=1).astype(BF16)
        tall = spec[:, cut].T
        for m in range(modes):
            out = mm(jnp.where(lane == m, tall, 0.0).astype(BF16), both).astype(BF16)
            out_ref[0, m, p] = out[:, :CHANNELS]
            out_ref[1, m, p] = out[:, CHANNELS:]


def rows_of(ref, step, at):
    count = ref.shape[0] // step
    return jnp.concatenate(
        [ref[n * step + at : n * step + at + 32, :] for n in range(count)], axis=0
    ).astype(F32)


def weight_two_kernel(small, _, __, ___, plain, scratch, loop):
    (all_ref,) = small
    (out_ref,) = plain
    outer_products(rows_of(all_ref, 96, 32), rows_of(all_ref, 96, 64), out_ref)


def weight_one_kernel(factor, small, _, __, ___, plain, scratch, loop):
    early_ref, all_ref = small
    out_ref, one_ref, two_ref, bias_ref = plain
    sums = all_ref[32:112, :].astype(F32)
    for n in range(1, all_ref.shape[0] // 112):
        sums = sums + all_ref[n * 112 + 32 : (n + 1) * 112, :].astype(F32)
    sums = sums * factor
    one = sums[:32, :LANES] + sums[:32, LANES:]
    one_ref[0:32, :] = one[:, :CHANNELS]
    one_ref[32:64, :] = one[:, CHANNELS:]
    two = jnp.concatenate([sums[32:64, :LANES], sums[32:64, LANES:]], axis=0)
    two_ref[...] = (two + turned(two))[:, :CHANNELS]
    bias = jnp.concatenate([sums[64:72, :LANES], sums[64:72, LANES:]], axis=0)
    bias_ref[...] = bias + turned(bias)
    outer_products(rows_of(early_ref, 96, 0), rows_of(all_ref, 112, 0), out_ref)


TILES = 128
PAIRS = TILES // 2
TILE = 2 * CHANNELS


def unpack_modes(got_ref, second_ref, depth, block=8):
    second = second_ref[...]
    left = side(32)
    for k in range(MZ):
        near = jnp.concatenate(
            [got_ref[d * block : d * block + 8, :] for d in range(k * 4, k * 4 + 4)], axis=0
        ) if block > 8 else got_ref[k * 32 : (k + 1) * 32, :].astype(F32)
        far = turned(near)
        top = jnp.concatenate([jnp.where(left, near, 0.0), jnp.where(left, far, 0.0)], axis=1)
        low = jnp.concatenate([jnp.where(left, 0.0, far), jnp.where(left, 0.0, near)], axis=1)
        out = mm(second, jnp.concatenate([top, low], axis=0).astype(BF16))
        for x in range(2):
            cut = slice(x * LANES, (x + 1) * LANES)
            depth[pl.ds(x * 2048 + k, 64, stride=32), :] = out[:64, cut]
            depth[pl.ds(x * 2048 + MZ + k, 64, stride=32), :] = out[64:, cut]


def pack_modes(spec, second_ref, out_ref, block=8):
    second = second_ref[...]
    left = side(32)
    for k in range(MZ):
        planes = [
            jnp.concatenate(
                [
                    spec[pl.ds(x * 2048 + k, 64, stride=32), :],
                    spec[pl.ds(x * 2048 + MZ + k, 64, stride=32), :],
                ],
                axis=0,
            )
            for x in range(2)
        ]
        out = mm(second, jnp.concatenate(planes, axis=1).astype(BF16))
        near, far = out[:, :LANES], out[:, LANES:]
        packed = jnp.where(left, near[:32] + turned(near[32:]), turned(far[:32]) + far[32:])
        if block == 8:
            out_ref[k * 32 : (k + 1) * 32, :] = packed.astype(out_ref.dtype)
        else:
            for d in range(4):
                at = (k * 4 + d) * block
                out_ref[at : at + 8, :] = packed[d * 8 : (d + 1) * 8]


def branch_of(depth, third, pair):
    at = pl.multiple_of(pair * 64, 64)
    wide = tn(depth[pl.ds(at, 64), :].astype(BF16), third)
    return wide[:, :LANES], wide[:, LANES:]


def store_spectrum(spec, third, pair, first, second):
    done = nt(third, jnp.concatenate([first, second], axis=0))
    at = pl.multiple_of(pair * 64, 64)
    spec[pl.ds(at, 32), :] = done[:, :LANES]
    spec[pl.ds(at + 32, 32), :] = done[:, LANES:]


def tile_at(tile):
    return pl.ds(pl.multiple_of(tile * TILE, TILE), TILE)


def gelu(preact):
    inner = preact * (ROOT + (ROOT * CUBIC) * (preact * preact))
    halved = 0.5 * preact
    return halved + halved * jnp.tanh(inner)


def gelu_slope(preact):
    square = preact * preact
    tangent = jnp.tanh(preact * (ROOT + (ROOT * CUBIC) * square))
    steep = (0.5 * preact) * (ROOT + (3.0 * ROOT * CUBIC) * square)
    return 0.5 + 0.5 * tangent + steep * (1.0 - tangent * tangent)


def hidden_kernel(small, big, outs, kinds, _, scratch, loop):
    got, inv2, inv3, fwd3, fwd2 = small
    (base,) = big
    hidden, preact = kinds
    depth, spec = scratch
    unpack_modes(got, inv2, depth)
    third_back = inv3[...]
    third = fwd3[...]

    def body(pair, carry):
        made = []
        for e, branch in enumerate(branch_of(depth, third_back, pair)):
            at = tile_at(2 * pair + e)
            pre = base[at, :].astype(F32) + branch
            preact[at, :] = pre.astype(BF16)
            value = gelu(pre).astype(BF16)
            hidden[at, :] = value
            made.append(value)
        store_spectrum(spec, third, pair, *made)
        return carry

    loop(body)
    pack_modes(spec, fwd2, outs[0])


def grad_two_kernel(small, big, outs, kinds, _, scratch, loop):
    got, inv2, inv3, fwd3, fwd2 = small
    base, cot = big
    (grad,) = kinds
    depth, spec = scratch
    unpack_modes(got, inv2, depth)
    third_back = inv3[...]
    third = fwd3[...]

    def body(pair, carry):
        made = []
        for e, branch in enumerate(branch_of(depth, third_back, pair)):
            at = tile_at(2 * pair + e)
            slope = gelu_slope(base[at, :].astype(F32) + branch)
            value = (cot[at, :].astype(F32) * slope).astype(BF16)
            grad[at, :] = value
            made.append(value)
        store_spectrum(spec, third, pair, *made)
        return carry

    loop(body)
    pack_modes(spec, fwd2, outs[0])


def grad_one_kernel(small, big, outs, _, __, scratch, loop):
    got, inv2, inv3, fwd3, fwd2 = small
    base, slope, values = big
    (out,) = outs
    depth, spec, wide, sent = scratch
    wide[...] = got[...].astype(F32)
    unpack_modes(wide, inv2, depth, 16)
    third_back = inv3[...]
    third = fwd3[...]
    ones = jnp.ones((16, 4 * LANES), BF16)

    def body(pair, total):
        made = []
        for e, branch in enumerate(branch_of(depth, third_back, pair)):
            at = tile_at(2 * pair + e)
            back = base[at, :].astype(F32) + branch
            made.append((back * slope[at, :].astype(F32)).astype(BF16))
        store_spectrum(spec, third, pair, *made)
        left = jnp.concatenate(
            [wide_tile(values, 2 * pair), wide_tile(values, 2 * pair + 1)], axis=1
        )
        right = jnp.concatenate(
            [part for tile in made for part in (tile[:CHANNELS], tile[CHANNELS:])], axis=1
        )
        return total + nt(jnp.concatenate([left, ones], axis=0), right)

    total = loop(body, jnp.zeros((CHANNELS + 16, CHANNELS), F32))
    pack_modes(spec, fwd2, sent, 48)
    left = side(1)

    def arrived_sum(place):
        row = jnp.sum(wide[pl.ds(place, 64, stride=16), :], axis=0, keepdims=True)
        row = row + turned(row)
        high = row.astype(BF16).astype(F32)
        return jnp.where(left, high, row - high)

    bias = jnp.concatenate([total[64:65], total[64:65]], axis=1)
    terms = jnp.concatenate(
        [
            jnp.concatenate([total[:32], total[32:64]], axis=1),
            bias,
            arrived_sum(8),
            arrived_sum(9),
            jnp.zeros((5, LANES), F32),
        ],
        axis=0,
    )
    for d in range(64):
        sent[d * 48 + 8 : (d + 1) * 48, :] = terms
    for d in range(64):
        out[d * 48 : (d + 1) * 48, :] = sent[d * 48 : (d + 1) * 48, :].astype(BF16)


def planes(kernel, kinds, *operands, big, token):
    scratch = [pltpu.VMEM((4096, LANES), F32), pltpu.VMEM((4096, LANES), F32)]
    return call(
        kernel,
        [CHUNK],
        scratch,
        1_000_000_000,
        20 << 20,
        *operands,
        big=big,
        kinds=kinds,
        token=token,
    )


def wide_tile(ref, tile):
    at = pl.multiple_of(tile * TILE, TILE)
    return jnp.concatenate(
        [ref[pl.ds(at, CHANNELS), :], ref[pl.ds(at + CHANNELS, CHANNELS), :]], axis=1
    )


def store_wide(ref, tile, wide):
    at = pl.multiple_of(tile * TILE, TILE)
    ref[pl.ds(at, CHANNELS), :] = wide[:, :LANES].astype(BF16)
    ref[pl.ds(at + CHANNELS, CHANNELS), :] = wide[:, LANES:].astype(BF16)


def layer_two_kernel(small, big, _, kinds, __, scratch, loop):
    point, bias = small
    weights = point[...]
    shift = jnp.concatenate([bias[...], bias[...]], axis=1)

    def body(pair, carry):
        for tile in (2 * pair, 2 * pair + 1):
            store_wide(kinds[0], tile, mm(weights, wide_tile(big[0], tile)) + shift)
        return carry

    loop(body)


def slope_kernel(small, big, _, kinds, __, scratch, loop):
    def body(pair, carry):
        for tile in (2 * pair, 2 * pair + 1):
            at = tile_at(tile)
            kinds[0][at, :] = gelu_slope(big[0][at, :].astype(F32)).astype(BF16)
        return carry

    loop(body, unroll=2)


def point_back_kernel(small, big, outs, kinds, _, scratch, loop):
    weights = small[0][...]
    hidden, grad = big
    ones = jnp.ones((16, 4 * LANES), BF16)

    def body(pair, total):
        right = [wide_tile(grad, 2 * pair + e) for e in range(2)]
        for e in range(2):
            store_wide(kinds[0], 2 * pair + e, mm(weights, right[e]))
        left = jnp.concatenate(
            [wide_tile(hidden, 2 * pair), wide_tile(hidden, 2 * pair + 1)], axis=1
        )
        return total + nt(
            jnp.concatenate([left, ones], axis=0), jnp.concatenate(right, axis=1)
        )

    outs[0][...] = loop(body, jnp.zeros((CHANNELS + 16, CHANNELS), F32))


def body(field_in, cotangent, spectral_one, spectral_two, point_one, point_two, bias_one, bias_two):
    forward_c, inverse_c = complex_tables(LANES, MY)
    forward_z, inverse_z = real_tables(LANES, MZ)
    shape = spectral_one.shape
    const = lambda table: jnp.asarray(np.ascontiguousarray(table))

    natural_second = const(second_natural(forward_c))
    third_forward = const(forward_z.T)
    third_adjoint = const(inverse_z)
    third_inverse = const(twice_diagonal(inverse_z))
    third_back = const(twice_diagonal(forward_z.T))
    second_fwd = const(second_paired(forward_c))
    second_adj = const(second_paired(flipped(inverse_c)))
    second_inv = const(second_inverse(inverse_c))
    second_back = const(second_inverse(flipped(forward_c)))
    first_fwd = const(first_forward(forward_c))
    first_adj = const(first_forward(flipped(inverse_c)))
    first_inv = const(first_inverse(inverse_c))
    first_back = const(first_inverse(flipped(forward_c)))

    def exchange(chunk):
        return lax.all_to_all(chunk, "space", split_axis=0, concat_axis=0, tiled=True)

    def samples(spectrum):
        return lax.all_gather(spectrum, "dp", axis=0, tiled=True)

    spread = lambda bias: jnp.broadcast_to(bias[:, None], (CHANNELS, LANES))

    chunk = first_partial(field_in, third_forward, natural_second)
    got = exchange(chunk)
    values, base = relay(field_in, point_one.T, spread(bias_one), token=chunk)

    chunk, spec_one = mixing(got, spectral_one, first_fwd, first_inv, token=base)
    got = exchange(chunk)
    cot = relay(cotangent, token=chunk)[0]

    chunk, hidden, preact = planes(
        hidden_kernel,
        [BF16, BF16],
        got,
        second_inv,
        third_inverse,
        third_forward,
        second_fwd,
        big=[base],
        token=cot,
    )
    got = exchange(chunk)
    base = call(
        layer_two_kernel,
        [],
        [],
        500_000_000,
        12 << 20,
        point_two.T,
        spread(bias_two),
        big=[hidden],
        kinds=[BF16],
    )[0]

    chunk, spec_two = mixing(got, spectral_two, first_fwd, first_inv, token=base)
    got = exchange(chunk)
    slope = call(
        slope_kernel, [], [], 500_000_000, 12 << 20, big=[preact], kinds=[BF16], token=chunk
    )[0]

    chunk, grad_two = planes(
        grad_two_kernel,
        [BF16],
        got,
        second_inv,
        third_inverse,
        third_adjoint,
        second_adj,
        big=[base, cot],
        token=slope,
    )
    got = exchange(chunk)
    term_two, base = call(
        point_back_kernel,
        [((CHANNELS + 16, CHANNELS), F32)],
        [],
        1_000_000_000,
        12 << 20,
        point_two,
        big=[hidden, grad_two],
        kinds=[BF16],
    )

    chunk, early = call(
        unmix_kernel,
        [((1024, LANES), BF16), ((96, 4 * CHANNELS), BF16)],
        [WIDE, pltpu.VMEM((1024, LANES), F32)],
        200_000_000,
        3 << 20,
        got,
        spectral_two,
        first_adj,
        first_back,
        term_two,
        spec_one,
        spec_two,
    )
    got = exchange(chunk)
    early = samples(early)
    spectral_grad_two = call(
        weight_two_kernel,
        [],
        [],
        200_000_000,
        3 << 20,
        early,
        plain=[jax.ShapeDtypeStruct(shape, BF16)],
        token=chunk,
    )[0]

    chunk = call(
        grad_one_kernel,
        [((3072, LANES), BF16)],
        [
            pltpu.VMEM((4096, LANES), F32),
            pltpu.VMEM((4096, LANES), F32),
            pltpu.VMEM((1024, LANES), F32),
            pltpu.VMEM((3072, LANES), F32),
        ],
        1_500_000_000,
        20 << 20,
        got,
        second_back,
        third_back,
        third_adjoint,
        second_adj,
        big=[base, slope, values],
        token=spectral_grad_two,
    )[0]
    got = exchange(chunk)
    late = call(
        last_kernel,
        [((112, 4 * CHANNELS), BF16)],
        [pltpu.VMEM((3072, LANES), F32)],
        50_000_000,
        1 << 20,
        got,
        first_adj,
    )[0]
    late = samples(late)
    cells = lax.axis_size("dp") * lax.axis_size("space") * 2 * LANES * LANES
    square = jax.ShapeDtypeStruct((CHANNELS, CHANNELS), F32)
    spectral_grad_one, point_grad_one, point_grad_two, biases = call(
        functools.partial(weight_one_kernel, 1.0 / math.sqrt(cells)),
        [],
        [],
        200_000_000,
        3 << 20,
        early,
        late,
        plain=[
            jax.ShapeDtypeStruct(shape, BF16),
            square,
            square,
            jax.ShapeDtypeStruct((16, LANES), F32),
        ],
    )
    return (
        spectral_grad_one,
        spectral_grad_two,
        point_grad_one,
        point_grad_two,
        biases[0, :CHANNELS],
        biases[8, :CHANNELS],
    )


def solution(mesh):
    field = P("dp", None, "space", None, None)
    modes = P(None, None, "space", None, None)
    return jax.shard_map(
        body,
        mesh=mesh,
        in_specs=(field, field, modes, modes, P(), P(), P(), P()),
        out_specs=(modes, modes, P(), P(), P(), P()),
        check_vma=False,
    )
```

time: 361 us -> 270 us (0.75); the launches traced: 354 us -> 269 us
  Pallas kernels: 0 us -> 98 us
  matrix products: 94.5 us -> 0 us
  waiting for transfers between devices: 54 us -> 9.76 us
  blocking collectives: 78.4 us -> 54.5 us
  other arithmetic: 16.4 us -> 0 us
  between operations: 15.2 us -> 1 us
  starting transfers between devices: 56.1 us -> 66.6 us
    pallas_call x0 -> x15, Pallas kernels: none -> 98 us  [the longest x12 80.2 us: call(): pl.pallas_call(whole_kernel, out_shape=shapes + list(plain), in_specs=[VM...]
    dot_general x29 -> x0, matrix products: 94.5 us -> none  [product(): return jnp.einsum(form, left, right, preferred_element_type=jnp.float32)]
    psum x1 -> x0, blocking collectives: 78.4 us -> none  [body(): lax.psum((point_term_one, point_term_two, bias_term_one, bias_term_two),...]
    all_to_all x7 -> x6, waiting for transfers between devices: 46.3 us -> 9.76 us  [exchange(): lax.all_to_all(chunk, 'space', split_axis=0, concat_axis=0, tiled=True)]
    all_to_all x0 -> x1, blocking collectives: none -> 36.2 us  [exchange(): lax.all_to_all(chunk, 'space', split_axis=0, concat_axis=0, tiled=True)]
    all_gather x0 -> x2, blocking collectives: none -> 18.3 us  [samples(): return lax.all_gather(spectrum, 'dp', axis=0, tiled=True)]
    unnamed x42 -> x78, local copies, waits for them, and re-layouts: 20.5 us -> 38.3 us
    reshape x7 -> x0, local copies, waits for them, and re-layouts: 14 us -> none  [the longest x3 12.9 us: partial_field(): second_done.reshape(channels, planes, 2 * modes_third, grid_second)]
  transfers between devices with their start and end apart: 8 -> 6, of which waited for: 8 -> 4; matrix products, arithmetic and copies ran while one was open for 13% -> 0% of each run, Pallas kernels for 0% -> 12%
where the time goes in v1:
time: 270 us; the launch traced here: 269 us
  Pallas kernels  98 us (36%)
  starting transfers between devices  66.6 us (25%)
  blocking collectives  54.5 us (20%)
  local copies, waits for them, and re-layouts  39 us (14%)
  waiting for transfers between devices  9.76 us (4%)
    pallas_call x12, Pallas kernels, call(): pl.pallas_call(whole_kernel, out_shape=shapes + list(plain), in_specs=[VM...  80.2 us
    all_to_all x6, starting transfers between devices, exchange(): lax.all_to_all(chunk, 'space', split_axis=0, concat_axis=0, tiled=True)  66.6 us
    unnamed x78, local copies, waits for them, and re-layouts  38.3 us
    all_to_all x1, blocking collectives, exchange(): lax.all_to_all(chunk, 'space', split_axis=0, concat_axis=0, tiled=True)  36.2 us
    all_gather x2, blocking collectives, samples(): return lax.all_gather(spectrum, 'dp', axis=0, tiled=True)  18.3 us
    pallas_call x2, Pallas kernels, relay(): pl.pallas_call(functools.partial(relay_kernel, pointed), out_shape=[pltpu...  13.2 us
    all_to_all x6, waiting for transfers between devices, exchange(): lax.all_to_all(chunk, 'space', split_axis=0, concat_axis=0, tiled=True)  9.76 us
  transfers between devices with their start and end apart: 6, of which 4 were waited for; matrix products, arithmetic and copies ran while one was open for 0% of the time, Pallas kernels for 12%

profile of v1, /device:TPU:1, one launch (start us, length us, event | category | flops | bytes accessed | tf_op | source)
XLA Modules:
  0.0 268.9 jit_solution(338109760302162665)
XLA Ops:
  4.3 4.6 %shard_map.244.refs_3_ = bf16[512,128]{1,0:T(8,128)(2,1)} custom-call(bf16[1,64,2,128,128]{4,3,2,1,0:T(8,128)(2,1)S(1)} %copy-done.6, bf16[32,128]{1,0:T(8,128)(2,1)S(1)} %copy-done.29, bf16[32,256]{1,0:T(8,128)(2,1)S(1)} %copy-done.34), custom_call_target="tpu_custom_call" | custom-call | flops 600000000 | bytes 6291456 | tf_op jit(solution)/shard_map/pallas_call | solution.py:273
  8.9 15.1 %all-to-all-start = ((bf16[64,8,128]{2,1,0:T(8,128)(2,1)}), bf16[64,8,128]{2,1,0:T(8,128)(2,1)S(1)}, u32[]{:S(2)}, u32[]{:S(2)}) async-start(bf16[64,8,128]{2,1,0:T(8,128)(2,1)} %bitcast.21), calls=%async_computation | async-start | bytes 262144 | tf_op jit(solution)/shard_map/all_to_all | solution.py:829
  27.3 8.1 %shard_map.245 = (bf16[16384,128]{1,0:T(8,128)(2,1)}, bf16[16384,128]{1,0:T(8,128)(2,1)}) custom-call(bf16[64,64]{1,0:T(8,128)(2,1)S(1)} %bitcast.31, f32[64,128]{1,0:T(8,128)S(1)} %broadcast_in_dim.4.refs_1_, bf16[1,64,2,128,128]{4,3,2,1,0:T(8,128)(2,1)S(1)} %copy-done.7, bf16[512,128]{1,0:T(8,128)(2,1)S(1)} %copy-done.17), custom_call_target="tpu_custom_call" | custom-call | flops 600000000 | bytes 12582912 | tf_op jit(solution)/shard_map/pallas_call | solution.py:356
  37.6 3.2 %shard_map.246 = (bf16[512,128]{1,0:T(8,128)(2,1)}, bf16[32,256]{1,0:T(8,128)(2,1)}) custom-call(bf16[512,128]{1,0:T(8,128)(2,1)S(1)} %bitcast.29, bf16[2,16,4,64,64]{4,3,2,1,0:T(8,128)(2,1)S(1)} %copy-done.16, bf16[64,128]{1,0:T(8,128)(2,1)S(1)} %copy-done.23, bf16[128,64]{1,0:T(8,128)(2,1)S(1)} %copy-done.22, bf16[16384,128]{1,0:T(8,128)(2,1)S(1)} %copy-done.4), custom_call_target="tpu_custom_call" | custom-call | flops 200000000 | bytes 3145728 | tf_op jit(solution)/shard_map/pallas_call | solution.py:210
  40.8 12.2 %all-to-all-start.1 = ((bf16[64,8,128]{2,1,0:T(8,128)(2,1)}), bf16[64,8,128]{2,1,0:T(8,128)(2,1)S(1)}, u32[]{:S(2)}, u32[]{:S(2)}) async-start(bf16[64,8,128]{2,1,0:T(8,128)(2,1)} %bitcast.27), calls=%async_computation.1 | async-start | bytes 262144 | tf_op jit(solution)/shard_map/all_to_all | solution.py:829
  56.1 5.1 %shard_map.247.refs_6_ = bf16[16384,128]{1,0:T(8,128)(2,1)} custom-call(bf16[1,64,2,128,128]{4,3,2,1,0:T(8,128)(2,1)S(1)} %copy-done.12, bf16[512,128]{1,0:T(8,128)(2,1)S(1)} %copy-done.20), custom_call_target="tpu_custom_call" | custom-call | flops 600000000 | bytes 12582912 | tf_op jit(solution)/shard_map/pallas_call | solution.py:356
  61.3 3.1 %all-to-all-done.1 = bf16[64,8,128]{2,1,0:T(8,128)(2,1)S(1)} async-done(((bf16[64,8,128]{2,1,0:T(8,128)(2,1)}), bf16[64,8,128]{2,1,0:T(8,128)(2,1)S(1)}, u32[]{:S(2)}, u32[]{:S(2)}) %all-to-all-start.1) | async-done | bytes 131104 | tf_op jit(solution)/shard_map/all_to_all | solution.py:829
  68.7 12.5 %shard_map.248 = (bf16[512,128]{1,0:T(8,128)(2,1)}, bf16[16384,128]{1,0:T(8,128)(2,1)}, bf16[16384,128]{1,0:T(8,128)(2,1)}) custom-call(bf16[512,128]{1,0:T(8,128)(2,1)S(1)} %bitcast.25, bf16[128,64]{1,0:T(8,128)(2,1)S(1)} %copy-done.21, bf16[64,256]{1,0:T(8,128)(2,1)S(1)} %copy-done.25, bf16[32,128]{1,0:T(8,128)(2,1)S(1)} %copy-done.30, ...), custom_call_target="tpu_custom_call" | custom-call | flops 1000000000 | bytes 20971520 | tf_op jit(solution)/shard_map/pallas_call | solution.py:210
  81.3 9.1 %all-to-all-start.2 = ((bf16[64,8,128]{2,1,0:T(8,128)(2,1)}), bf16[64,8,128]{2,1,0:T(8,128)(2,1)S(1)}, u32[]{:S(2)}, u32[]{:S(2)}) async-start(bf16[64,8,128]{2,1,0:T(8,128)(2,1)} %bitcast.34), calls=%async_computation.2 | async-start | bytes 262144 | tf_op jit(solution)/shard_map/all_to_all | solution.py:829
  92.8 4.7 %shard_map.249.refs_4_.refs_5_ = bf16[16384,128]{1,0:T(8,128)(2,1)} custom-call(bf16[64,64]{1,0:T(8,128)(2,1)S(1)} %bitcast.32, f32[64,128]{1,0:T(8,128)S(1)} %broadcast_in_dim.5.refs_1_, bf16[16384,128]{1,0:T(8,128)(2,1)S(1)} %copy-done.8), custom_call_target="tpu_custom_call" | custom-call | flops 500000000 | bytes 12582912 | tf_op jit(solution)/shard_map/pallas_call | solution.py:210
  97.5 4.3 %all-to-all-done.2 = bf16[64,8,128]{2,1,0:T(8,128)(2,1)S(1)} async-done(((bf16[64,8,128]{2,1,0:T(8,128)(2,1)}), bf16[64,8,128]{2,1,0:T(8,128)(2,1)S(1)}, u32[]{:S(2)}, u32[]{:S(2)}) %all-to-all-start.2) | async-done | bytes 131104 | tf_op jit(solution)/shard_map/all_to_all | solution.py:829
  104.0 3.2 %shard_map.250 = (bf16[512,128]{1,0:T(8,128)(2,1)}, bf16[32,256]{1,0:T(8,128)(2,1)}) custom-call(bf16[512,128]{1,0:T(8,128)(2,1)S(1)} %bitcast.30, bf16[2,16,4,64,64]{4,3,2,1,0:T(8,128)(2,1)S(1)} %copy-done.10, bf16[64,128]{1,0:T(8,128)(2,1)S(1)} %copy-done.23, bf16[128,64]{1,0:T(8,128)(2,1)S(1)} %copy-done.22, bf16[16384,128]{1,0:T(8,128)(2,1)S(1)} %copy-done.2), custom_call_target="tpu_custom_call" | custom-call | flops 200000000 | bytes 3145728 | tf_op jit(solution)/shard_map/pallas_call | solution.py:210
  107.2 8.1 %all-to-all-start.3 = ((bf16[64,8,128]{2,1,0:T(8,128)(2,1)}), bf16[64,8,128]{2,1,0:T(8,128)(2,1)S(1)}, u32[]{:S(2)}, u32[]{:S(2)}) async-start(bf16[64,8,128]{2,1,0:T(8,128)(2,1)} %bitcast.26), calls=%async_computation.3 | async-start | bytes 262144 | tf_op jit(solution)/shard_map/all_to_all | solution.py:829
  118.4 6.2 %shard_map.251.refs_7_.refs_6_ = bf16[16384,128]{1,0:T(8,128)(2,1)} custom-call(bf16[16384,128]{1,0:T(8,128)(2,1)S(1)} %copy-done.13, bf16[512,128]{1,0:T(8,128)(2,1)S(1)} %copy-done.19), custom_call_target="tpu_custom_call" | custom-call | flops 500000000 | bytes 12582912 | tf_op jit(solution)/shard_map/pallas_call | solution.py:210
  131.0 15.0 %shard_map.252 = (bf16[512,128]{1,0:T(8,128)(2,1)}, bf16[16384,128]{1,0:T(8,128)(2,1)}) custom-call(bf16[512,128]{1,0:T(8,128)(2,1)S(1)} %bitcast.24, bf16[128,64]{1,0:T(8,128)(2,1)S(1)} %copy-done.21, bf16[64,256]{1,0:T(8,128)(2,1)S(1)} %copy-done.25, bf16[32,128]{1,0:T(8,128)(2,1)S(1)} %copy-done.31, bf16[64,128]{1,0:T(8,128)(2,1)S(1)} %copy-done.24, ...), custom_call_target="tpu_custom_call" | custom-call | flops 1000000000 | bytes 20971520 | tf_op jit(solution)/shard_map/pallas_call | solution.py:210
  146.0 10.2 %all-to-all-start.4 = ((bf16[64,8,128]{2,1,0:T(8,128)(2,1)}), bf16[64,8,128]{2,1,0:T(8,128)(2,1)S(1)}, u32[]{:S(2)}, u32[]{:S(2)}) async-start(bf16[64,8,128]{2,1,0:T(8,128)(2,1)} %bitcast.35), calls=%async_computation.4 | async-start | bytes 262144 | tf_op jit(solution)/shard_map/all_to_all | solution.py:829
  160.7 6.6 %shard_map.253 = (f32[80,64]{1,0:T(8,128)}, bf16[16384,128]{1,0:T(8,128)(2,1)}) custom-call(bf16[64,64]{1,0:T(8,128)(2,1)S(1)} %copy-done.26, bf16[16384,128]{1,0:T(8,128)(2,1)S(1)} %copy-done.9, bf16[16384,128]{1,0:T(8,128)(2,1)S(1)} %copy-done.14), custom_call_target="tpu_custom_call" | custom-call | flops 1000000000 | bytes 12582912 | tf_op jit(solution)/shard_map/pallas_call | solution.py:210
  168.4 3.5 %shard_map.254 = (bf16[1024,128]{1,0:T(8,128)(2,1)}, bf16[96,256]{1,0:T(8,128)(2,1)}) custom-call(bf16[512,128]{1,0:T(8,128)(2,1)S(1)} %bitcast.28, bf16[2,16,4,64,64]{4,3,2,1,0:T(8,128)(2,1)S(1)} %copy-done.10, bf16[64,128]{1,0:T(8,128)(2,1)S(1)} %copy-done.23, bf16[128,64]{1,0:T(8,128)(2,1)S(1)} %copy-done.22, f32[80,64]{1,0:T(8,128)S(1)} %copy-done.27, ...), custom_call_target="tpu_custom_call" | custom-call | flops 200000000 | bytes 3145728 | tf_op jit(solution)/shard_map/pallas_call | solution.py:210
  171.9 11.8 %all-to-all-start.5 = ((bf16[64,16,128]{2,1,0:T(8,128)(2,1)}), bf16[64,16,128]{2,1,0:T(8,128)(2,1)S(1)}, u32[]{:S(2)}, u32[]{:S(2)}) async-start(bf16[64,16,128]{2,1,0:T(8,128)(2,1)} %bitcast.23), calls=%async_computation.5 | async-start | bytes 524288 | tf_op jit(solution)/shard_map/all_to_all | solution.py:829
  183.8 10.1 %all_gather.6.refs_0_ = bf16[384,256]{1,0:T(8,128)(2,1)S(1)} all-gather(bf16[96,256]{1,0:T(8,128)(2,1)} %get-tuple-element.36), channel_id=1, replica_groups=mesh['dp'=4,'space'=64] {'dp'}, dimensions={0}, use_global_device_ids=true | all-gather | bytes 245760 | tf_op jit(solution)/shard_map/all_gather | solution.py:832
  201.1 19.2 %shard_map.256 = bf16[3072,128]{1,0:T(8,128)(2,1)} custom-call(bf16[1024,128]{1,0:T(8,128)(2,1)S(1)} %bitcast.22, bf16[128,64]{1,0:T(8,128)(2,1)S(1)} %copy-done.21, bf16[64,256]{1,0:T(8,128)(2,1)S(1)} %copy-done.28, bf16[32,128]{1,0:T(8,128)(2,1)S(1)} %copy-done.31, bf16[64,128]{1,0:T(8,128)(2,1)S(1)} %copy-done.24, bf16[16384,128]{1,0:T(8,128)(2,1)S(1)} %copy-done.15, ...), custom_call_target="tpu_custom_call" | custom-call | flops 1500000000 | bytes 20971520 | tf_op jit(solution)/shard_map/pallas_call | solution.py:210
  220.3 36.2 %all_to_all.77 = bf16[64,48,128]{2,1,0:T(8,128)(2,1)S(1)} all-to-all(bf16[64,48,128]{2,1,0:T(8,128)(2,1)} %bitcast.33), channel_id=1, replica_groups=mesh['dp'=4,'space'=64] {'space'}, dimensions={0} | all-to-all | bytes 1572864 | tf_op jit(solution)/shard_map/all_to_all | solution.py:829
  257.7 8.2 %all_gather.7.refs_1_ = bf16[448,256]{1,0:T(8,128)(2,1)S(1)} all-gather(bf16[112,256]{1,0:T(8,128)(2,1)} %shard_map.257), channel_id=1, replica_groups=mesh['dp'=4,'space'=64] {'dp'}, dimensions={0}, use_global_device_ids=true | all-gather | bytes 286720 | tf_op jit(solution)/shard_map/all_gather | solution.py:832
  265.8 2.5 shard_map.258
  (87 shorter events, 44.9 us)
Async XLA Ops:
  4.2 19.8 %copy-start.35 = (bf16[64,64]{1,0:T(8,128)(2,1)S(1)}, bf16[64,64]{1,0:T(8,128)(2,1)}, u32[]{:S(2)}) copy-start(bf16[64,64]{1,0:T(8,128)(2,1)} %param.25) | copy-start | bytes 24580
  4.2 19.9 %copy-start.36 = (f32[64]{0:T(128)S(1)}, f32[64]{0:T(128)}, u32[]{:S(2)}) copy-start(f32[64]{0:T(128)} %param.27) | copy-start | bytes 772
  4.2 31.2 %copy-start.16 = (bf16[2,16,4,64,64]{4,3,2,1,0:T(8,128)(2,1)S(1)}, bf16[2,16,4,64,64]{4,3,2,1,0:T(8,128)(2,1)}, u32[]{:S(2)}) copy-start(bf16[2,16,4,64,64]{4,3,2,1,0:T(8,128)(2,1)} %refs_1_.7) | copy-start | bytes 3145732
  4.2 31.2 %copy-start.22 = (bf16[128,64]{1,0:T(8,128)(2,1)S(1)}, bf16[128,64]{1,0:T(8,128)(2,1)}, u32[]{:S(2)}) copy-start(bf16[128,64]{1,0:T(8,128)(2,1)} %constant.26.clone.refs_3_) | copy-start | bytes 49156
  4.2 31.2 %copy-start.23 = (bf16[64,128]{1,0:T(8,128)(2,1)S(1)}, bf16[64,128]{1,0:T(8,128)(2,1)}, u32[]{:S(2)}) copy-start(bf16[64,128]{1,0:T(8,128)(2,1)} %constant.25.clone.refs_2_.refs_1_) | copy-start | bytes 49156
  8.9 26.5 %all-to-all-start = ((bf16[64,8,128]{2,1,0:T(8,128)(2,1)}), bf16[64,8,128]{2,1,0:T(8,128)(2,1)S(1)}, u32[]{:S(2)}, u32[]{:S(2)}) async-start(bf16[64,8,128]{2,1,0:T(8,128)(2,1)} %bitcast.21), calls=%async_computation | async-start | bytes 262144 | tf_op jit(solution)/shard_map/all_to_all | solution.py:829
  24.2 2.2 copy-start.7
  40.8 23.5 %all-to-all-start.1 = ((bf16[64,8,128]{2,1,0:T(8,128)(2,1)}), bf16[64,8,128]{2,1,0:T(8,128)(2,1)S(1)}, u32[]{:S(2)}, u32[]{:S(2)}) async-start(bf16[64,8,128]{2,1,0:T(8,128)(2,1)} %bitcast.27), calls=%async_computation.1 | async-start | bytes 262144 | tf_op jit(solution)/shard_map/all_to_all | solution.py:829
  56.1 8.2 %copy-start.21 = (bf16[128,64]{1,0:T(8,128)(2,1)S(1)}, bf16[128,64]{1,0:T(8,128)(2,1)}, u32[]{:S(2)}) copy-start(bf16[128,64]{1,0:T(8,128)(2,1)} %constant.24.clone.refs_1_) | copy-start | bytes 49156
  56.1 8.2 %copy-start.24 = (bf16[64,128]{1,0:T(8,128)(2,1)S(1)}, bf16[64,128]{1,0:T(8,128)(2,1)}, u32[]{:S(2)}) copy-start(bf16[64,128]{1,0:T(8,128)(2,1)} %constant.23.clone.refs_4_) | copy-start | bytes 49156
  56.1 8.2 %copy-start.25 = (bf16[64,256]{1,0:T(8,128)(2,1)S(1)}, bf16[64,256]{1,0:T(8,128)(2,1)}, u32[]{:S(2)}) copy-start(bf16[64,256]{1,0:T(8,128)(2,1)} %constant.21.clone.refs_2_) | copy-start | bytes 98308
  56.1 8.2 %copy-start.30 = (bf16[32,128]{1,0:T(8,128)(2,1)S(1)}, bf16[32,128]{1,0:T(8,128)(2,1)}, u32[]{:S(2)}) copy-start(bf16[32,128]{1,0:T(8,128)(2,1)} %constant.19.clone.third_far.refs_3_) | copy-start | bytes 24580
  68.7 21.7 %copy-start.26 = (bf16[64,64]{1,0:T(8,128)(2,1)S(1)}, bf16[64,64]{1,0:T(8,128)(2,1)}, u32[]{:S(2)}) copy-start(bf16[64,64]{1,0:T(8,128)(2,1)} %refs_0_.3) | copy-start | bytes 24580
  68.7 21.8 %copy-start.37 = (f32[64]{0:T(128)S(1)}, f32[64]{0:T(128)}, u32[]{:S(2)}) copy-start(f32[64]{0:T(128)} %param.28) | copy-start | bytes 772
  81.3 20.6 %all-to-all-start.2 = ((bf16[64,8,128]{2,1,0:T(8,128)(2,1)}), bf16[64,8,128]{2,1,0:T(8,128)(2,1)S(1)}, u32[]{:S(2)}, u32[]{:S(2)}) async-start(bf16[64,8,128]{2,1,0:T(8,128)(2,1)} %bitcast.34), calls=%async_computation.2 | async-start | bytes 262144 | tf_op jit(solution)/shard_map/all_to_all | solution.py:829
  90.6 2.2 copy-start.8
  92.8 9.0 %copy-start.10 = (bf16[2,16,4,64,64]{4,3,2,1,0:T(8,128)(2,1)S(1)}, bf16[2,16,4,64,64]{4,3,2,1,0:T(8,128)(2,1)}, u32[]{:S(2)}) copy-start(bf16[2,16,4,64,64]{4,3,2,1,0:T(8,128)(2,1)} %refs_1_.9) | copy-start | bytes 3145732
  107.2 19.4 %all-to-all-start.3 = ((bf16[64,8,128]{2,1,0:T(8,128)(2,1)}), bf16[64,8,128]{2,1,0:T(8,128)(2,1)S(1)}, u32[]{:S(2)}, u32[]{:S(2)}) async-start(bf16[64,8,128]{2,1,0:T(8,128)(2,1)} %bitcast.26), calls=%async_computation.3 | async-start | bytes 262144 | tf_op jit(solution)/shard_map/all_to_all | solution.py:829
  118.4 8.2 %copy-start.31 = (bf16[32,128]{1,0:T(8,128)(2,1)S(1)}, bf16[32,128]{1,0:T(8,128)(2,1)}, u32[]{:S(2)}) copy-start(bf16[32,128]{1,0:T(8,128)(2,1)} %constant.20.clone.refs_3_) | copy-start | bytes 24580
  146.0 21.6 %all-to-all-start.4 = ((bf16[64,8,128]{2,1,0:T(8,128)(2,1)}), bf16[64,8,128]{2,1,0:T(8,128)(2,1)S(1)}, u32[]{:S(2)}, u32[]{:S(2)}) async-start(bf16[64,8,128]{2,1,0:T(8,128)(2,1)} %bitcast.35), calls=%async_computation.4 | async-start | bytes 262144 | tf_op jit(solution)/shard_map/all_to_all | solution.py:829
  160.7 7.0 %copy-start.32 = (bf16[32,256]{1,0:T(8,128)(2,1)S(1)}, bf16[32,256]{1,0:T(8,128)(2,1)}, u32[]{:S(2)}) copy-start(bf16[32,256]{1,0:T(8,128)(2,1)} %get-tuple-element.34.refs_5_) | copy-start | bytes 49156
  160.7 7.0 %copy-start.33 = (bf16[32,256]{1,0:T(8,128)(2,1)S(1)}, bf16[32,256]{1,0:T(8,128)(2,1)}, u32[]{:S(2)}) copy-start(bf16[32,256]{1,0:T(8,128)(2,1)} %get-tuple-element.35.refs_6_) | copy-start | bytes 49156
  160.7 36.6 %copy-start.28 = (bf16[64,256]{1,0:T(8,128)(2,1)S(1)}, bf16[64,256]{1,0:T(8,128)(2,1)}, u32[]{:S(2)}) copy-start(bf16[64,256]{1,0:T(8,128)(2,1)} %constant.22.clone.refs_2_) | copy-start | bytes 98308
  171.9 25.4 %all-to-all-start.5 = ((bf16[64,16,128]{2,1,0:T(8,128)(2,1)}), bf16[64,16,128]{2,1,0:T(8,128)(2,1)S(1)}, u32[]{:S(2)}, u32[]{:S(2)}) async-start(bf16[64,16,128]{2,1,0:T(8,128)(2,1)} %bitcast.23), calls=%async_computation.5 | async-start | bytes 524288 | tf_op jit(solution)/shard_map/all_to_all | solution.py:829
  (20 other events, 33.7 us)

commit v2 on v1

--- a/solution.py
+++ b/solution.py
@@ -126,6 +126,10 @@
 
 def near(value):
     return pltpu.with_memory_space_constraint(value, pltpu.VMEM)
+
+
+def afar(value):
+    return pltpu.with_memory_space_constraint(value, pltpu.HBM)
 
 
 def call(
@@ -223,7 +227,7 @@
         ],
         cost_estimate=pl.CostEstimate(flops=flops, bytes_accessed=moved, transcendentals=0),
         compiler_params=pltpu.CompilerParams(vmem_limit_bytes=VMEM_LIMIT),
-    )(*operands, *big, *extra)
+    )(*operands, *[afar(array) for array in (*big, *extra)])
 
 
 C_STEP = 8
@@ -288,7 +292,7 @@
             flops=600_000_000, bytes_accessed=6 << 20, transcendentals=0
         ),
         compiler_params=pltpu.CompilerParams(vmem_limit_bytes=VMEM_LIMIT),
-    )(field, third, second)
+    )(afar(field), afar(third), afar(second))
 
 
 Y_STEP = 16
@@ -369,7 +373,7 @@
             flops=600_000_000, bytes_accessed=12 << 20, transcendentals=0
         ),
         compiler_params=pltpu.CompilerParams(vmem_limit_bytes=VMEM_LIMIT),
-    )(*[near(operand) for operand in operands], field, token)
+    )(*[near(operand) for operand in operands], afar(field), afar(token))
 
 
 def own_spectrum(wide, table, place, block=8):

time: 270 us -> 235 us (0.87)
  local copies, waits for them, and re-layouts: 39 us -> 1.72 us
  starting transfers between devices: 66.6 us -> 53.2 us
  waiting for transfers between devices: 9.76 us -> 23 us
  Pallas kernels: 98 us -> 101 us
    unnamed x78 -> x36, local copies, waits for them, and re-layouts: 38.3 us -> 1.06 us
    all_to_all x6, starting transfers between devices: 66.6 us -> 53.2 us  [exchange(): lax.all_to_all(chunk, 'space', split_axis=0, concat_axis=0, tiled=True)]
    all_to_all x6, waiting for transfers between devices: 9.76 us -> 23 us  [exchange(): lax.all_to_all(chunk, 'space', split_axis=0, concat_axis=0, tiled=True)]
  transfers between devices with their start and end apart: 6 -> 6, of which waited for: 4 -> 5; matrix products, arithmetic and copies ran while one was open for 0% -> 0% of each run, Pallas kernels for 12% -> 15%
where the time goes in v2:
time: 235 us
  Pallas kernels  101 us (43%)
  blocking collectives  54.5 us (23%)
  starting transfers between devices  53.2 us (23%)
  waiting for transfers between devices  23 us (10%)
    pallas_call x12, Pallas kernels, call(): pl.pallas_call(whole_kernel, out_shape=shapes + list(plain), in_specs=[VM...  82 us
    all_to_all x6, starting transfers between devices, exchange(): lax.all_to_all(chunk, 'space', split_axis=0, concat_axis=0, tiled=True)  53.2 us
    all_to_all x1, blocking collectives, exchange(): lax.all_to_all(chunk, 'space', split_axis=0, concat_axis=0, tiled=True)  36.2 us
    all_to_all x6, waiting for transfers between devices, exchange(): lax.all_to_all(chunk, 'space', split_axis=0, concat_axis=0, tiled=True)  23 us
    all_gather x2, blocking collectives, samples(): return lax.all_gather(spectrum, 'dp', axis=0, tiled=True)  18.3 us
    pallas_call x2, Pallas kernels, relay(): pl.pallas_call(functools.partial(relay_kernel, pointed), out_shape=[pltpu...  13.1 us
    pallas_call x1, Pallas kernels, first_partial(): pl.pallas_call(spectrum_kernel, out_shape=pltpu.HBM((512, LANES), BF16),...  6.29 us
  transfers between devices with their start and end apart: 6, of which 5 were waited for; matrix products, arithmetic and copies ran while one was open for 0% of the time, Pallas kernels for 15%

profile of v2, /device:TPU:1, one launch (start us, length us, event | category | flops | bytes accessed | tf_op | source)
XLA Modules:
  0.0 234.9 jit_solution(9367268894810988319)
XLA Ops:
  0.7 6.3 %shard_map.244.refs_3_ = bf16[512,128]{1,0:T(8,128)(2,1)} custom-call(bf16[1,64,2,128,128]{4,3,2,1,0:T(8,128)(2,1)} %refs_2_.7, bf16[32,128]{1,0:T(8,128)(2,1)} %constant.19.clone.third_far.refs_3_, bf16[32,256]{1,0:T(8,128)(2,1)} %constant.18.clone.second_far), custom_call_target="tpu_custom_call" | custom-call | flops 600000000 | bytes 6291456 | tf_op jit(solution)/shard_map/pallas_call | solution.py:277
  7.0 15.1 %all-to-all-start = ((bf16[64,8,128]{2,1,0:T(8,128)(2,1)}), bf16[64,8,128]{2,1,0:T(8,128)(2,1)S(1)}, u32[]{:S(2)}, u32[]{:S(2)}) async-start(bf16[64,8,128]{2,1,0:T(8,128)(2,1)} %bitcast.30), calls=%async_computation | async-start | bytes 262144 | tf_op jit(solution)/shard_map/all_to_all | solution.py:833
  22.3 8.0 %shard_map.245 = (bf16[16384,128]{1,0:T(8,128)(2,1)}, bf16[16384,128]{1,0:T(8,128)(2,1)}) custom-call(bf16[64,64]{1,0:T(8,128)(2,1)S(1)} %bitcast.27, f32[64,128]{1,0:T(8,128)S(1)} %broadcast_in_dim.4.refs_1_, bf16[1,64,2,128,128]{4,3,2,1,0:T(8,128)(2,1)} %refs_2_.7, bf16[512,128]{1,0:T(8,128)(2,1)} %shard_map.244.refs_3_), custom_call_target="tpu_custom_call" | custom-call | flops 600000000 | bytes 12582912 | tf_op jit(solution)/shard_map/pallas_call | solution.py:360
  36.5 9.2 %all-to-all-start.1 = ((bf16[64,8,128]{2,1,0:T(8,128)(2,1)}), bf16[64,8,128]{2,1,0:T(8,128)(2,1)S(1)}, u32[]{:S(2)}, u32[]{:S(2)}) async-start(bf16[64,8,128]{2,1,0:T(8,128)(2,1)} %bitcast.33), calls=%async_computation.1 | async-start | bytes 262144 | tf_op jit(solution)/shard_map/all_to_all | solution.py:833
  45.8 5.1 %shard_map.247.refs_6_ = bf16[16384,128]{1,0:T(8,128)(2,1)} custom-call(bf16[1,64,2,128,128]{4,3,2,1,0:T(8,128)(2,1)} %refs_0_.2, bf16[512,128]{1,0:T(8,128)(2,1)} %get-tuple-element.26.refs_1_), custom_call_target="tpu_custom_call" | custom-call | flops 600000000 | bytes 12582912 | tf_op jit(solution)/shard_map/pallas_call | solution.py:360
  50.9 6.2 %all-to-all-done.1 = bf16[64,8,128]{2,1,0:T(8,128)(2,1)S(1)} async-done(((bf16[64,8,128]{2,1,0:T(8,128)(2,1)}), bf16[64,8,128]{2,1,0:T(8,128)(2,1)S(1)}, u32[]{:S(2)}, u32[]{:S(2)}) %all-to-all-start.1) | async-done | bytes 131104 | tf_op jit(solution)/shard_map/all_to_all | solution.py:833
  57.1 12.3 %shard_map.248 = (bf16[512,128]{1,0:T(8,128)(2,1)}, bf16[16384,128]{1,0:T(8,128)(2,1)}, bf16[16384,128]{1,0:T(8,128)(2,1)}) custom-call(bf16[512,128]{1,0:T(8,128)(2,1)S(1)} %bitcast.23, bf16[128,64]{1,0:T(8,128)(2,1)S(1)} %copy-done.2, bf16[64,256]{1,0:T(8,128)(2,1)S(1)} %copy-done.6, bf16[32,128]{1,0:T(8,128)(2,1)S(1)} %copy-done.10, ...), custom_call_target="tpu_custom_call" | custom-call | flops 1000000000 | bytes 20971520 | tf_op jit(solution)/shard_map/pallas_call | solution.py:214
  69.5 6.0 %all-to-all-start.2 = ((bf16[64,8,128]{2,1,0:T(8,128)(2,1)}), bf16[64,8,128]{2,1,0:T(8,128)(2,1)S(1)}, u32[]{:S(2)}, u32[]{:S(2)}) async-start(bf16[64,8,128]{2,1,0:T(8,128)(2,1)} %bitcast.34), calls=%async_computation.2 | async-start | bytes 262144 | tf_op jit(solution)/shard_map/all_to_all | solution.py:833
  75.7 5.6 %shard_map.249.refs_4_.refs_5_ = bf16[16384,128]{1,0:T(8,128)(2,1)} custom-call(bf16[64,64]{1,0:T(8,128)(2,1)S(1)} %bitcast.28, f32[64,128]{1,0:T(8,128)S(1)} %broadcast_in_dim.5.refs_1_, bf16[16384,128]{1,0:T(8,128)(2,1)} %get-tuple-element.28.refs_2_.refs_1_), custom_call_target="tpu_custom_call" | custom-call | flops 500000000 | bytes 12582912 | tf_op jit(solution)/shard_map/pallas_call | solution.py:214
  81.3 5.5 %all-to-all-done.2 = bf16[64,8,128]{2,1,0:T(8,128)(2,1)S(1)} async-done(((bf16[64,8,128]{2,1,0:T(8,128)(2,1)}), bf16[64,8,128]{2,1,0:T(8,128)(2,1)S(1)}, u32[]{:S(2)}, u32[]{:S(2)}) %all-to-all-start.2) | async-done | bytes 131104 | tf_op jit(solution)/shard_map/all_to_all | solution.py:833
  86.8 3.2 %shard_map.250 = (bf16[512,128]{1,0:T(8,128)(2,1)}, bf16[32,256]{1,0:T(8,128)(2,1)}) custom-call(bf16[512,128]{1,0:T(8,128)(2,1)S(1)} %bitcast.26, bf16[2,16,4,64,64]{4,3,2,1,0:T(8,128)(2,1)S(1)} %copy-done, bf16[64,128]{1,0:T(8,128)(2,1)S(1)} %copy-done.4, bf16[128,64]{1,0:T(8,128)(2,1)S(1)} %copy-done.3, bf16[16384,128]{1,0:T(8,128)(2,1)} %shard_map.249.refs_4_.refs_5_), custom_call_target="tpu_custom_call" | custom-call | flops 200000000 | bytes 3145728 | tf_op jit(solution)/shard_map/pallas_call | solution.py:214
  90.0 6.9 %all-to-all-start.3 = ((bf16[64,8,128]{2,1,0:T(8,128)(2,1)}), bf16[64,8,128]{2,1,0:T(8,128)(2,1)S(1)}, u32[]{:S(2)}, u32[]{:S(2)}) async-start(bf16[64,8,128]{2,1,0:T(8,128)(2,1)} %bitcast.32), calls=%async_computation.3 | async-start | bytes 262144 | tf_op jit(solution)/shard_map/all_to_all | solution.py:833
  96.9 7.0 %shard_map.251.refs_7_.refs_6_ = bf16[16384,128]{1,0:T(8,128)(2,1)} custom-call(bf16[16384,128]{1,0:T(8,128)(2,1)} %get-tuple-element.30.refs_0_, bf16[512,128]{1,0:T(8,128)(2,1)} %get-tuple-element.29.refs_1_), custom_call_target="tpu_custom_call" | custom-call | flops 500000000 | bytes 12582912 | tf_op jit(solution)/shard_map/pallas_call | solution.py:214
  103.9 4.2 %all-to-all-done.3 = bf16[64,8,128]{2,1,0:T(8,128)(2,1)S(1)} async-done(((bf16[64,8,128]{2,1,0:T(8,128)(2,1)}), bf16[64,8,128]{2,1,0:T(8,128)(2,1)S(1)}, u32[]{:S(2)}, u32[]{:S(2)}) %all-to-all-start.3) | async-done | bytes 131104 | tf_op jit(solution)/shard_map/all_to_all | solution.py:833
  108.0 14.7 %shard_map.252 = (bf16[512,128]{1,0:T(8,128)(2,1)}, bf16[16384,128]{1,0:T(8,128)(2,1)}) custom-call(bf16[512,128]{1,0:T(8,128)(2,1)S(1)} %bitcast.22, bf16[128,64]{1,0:T(8,128)(2,1)S(1)} %copy-done.2, bf16[64,256]{1,0:T(8,128)(2,1)S(1)} %copy-done.6, bf16[32,128]{1,0:T(8,128)(2,1)S(1)} %copy-done.11, bf16[64,128]{1,0:T(8,128)(2,1)S(1)} %copy-done.5, ...), custom_call_target="tpu_custom_call" | custom-call | flops 1000000000 | bytes 20971520 | tf_op jit(solution)/shard_map/pallas_call | solution.py:214
  122.8 7.9 %all-to-all-start.4 = ((bf16[64,8,128]{2,1,0:T(8,128)(2,1)}), bf16[64,8,128]{2,1,0:T(8,128)(2,1)S(1)}, u32[]{:S(2)}, u32[]{:S(2)}) async-start(bf16[64,8,128]{2,1,0:T(8,128)(2,1)} %bitcast.35), calls=%async_computation.4 | async-start | bytes 262144 | tf_op jit(solution)/shard_map/all_to_all | solution.py:833
  130.7 7.1 %shard_map.253 = (f32[80,64]{1,0:T(8,128)}, bf16[16384,128]{1,0:T(8,128)(2,1)}) custom-call(bf16[64,64]{1,0:T(8,128)(2,1)S(1)} %copy-done.7, bf16[16384,128]{1,0:T(8,128)(2,1)} %get-tuple-element.28.refs_2_.refs_1_, bf16[16384,128]{1,0:T(8,128)(2,1)} %get-tuple-element.32.refs_2_), custom_call_target="tpu_custom_call" | custom-call | flops 1000000000 | bytes 12582912 | tf_op jit(solution)/shard_map/pallas_call | solution.py:214
  137.8 4.2 %all-to-all-done.4 = bf16[64,8,128]{2,1,0:T(8,128)(2,1)S(1)} async-done(((bf16[64,8,128]{2,1,0:T(8,128)(2,1)}), bf16[64,8,128]{2,1,0:T(8,128)(2,1)S(1)}, u32[]{:S(2)}, u32[]{:S(2)}) %all-to-all-start.4) | async-done | bytes 131104 | tf_op jit(solution)/shard_map/all_to_all | solution.py:833
  142.8 3.5 %shard_map.254 = (bf16[1024,128]{1,0:T(8,128)(2,1)}, bf16[96,256]{1,0:T(8,128)(2,1)}) custom-call(bf16[512,128]{1,0:T(8,128)(2,1)S(1)} %bitcast.24, bf16[2,16,4,64,64]{4,3,2,1,0:T(8,128)(2,1)S(1)} %copy-done, bf16[64,128]{1,0:T(8,128)(2,1)S(1)} %copy-done.4, bf16[128,64]{1,0:T(8,128)(2,1)S(1)} %copy-done.3, f32[80,64]{1,0:T(8,128)S(1)} %copy-done.8, ...), custom_call_target="tpu_custom_call" | custom-call | flops 200000000 | bytes 3145728 | tf_op jit(solution)/shard_map/pallas_call | solution.py:214
  146.3 8.1 %all-to-all-start.5 = ((bf16[64,16,128]{2,1,0:T(8,128)(2,1)}), bf16[64,16,128]{2,1,0:T(8,128)(2,1)S(1)}, u32[]{:S(2)}, u32[]{:S(2)}) async-start(bf16[64,16,128]{2,1,0:T(8,128)(2,1)} %bitcast.31), calls=%async_computation.5 | async-start | bytes 524288 | tf_op jit(solution)/shard_map/all_to_all | solution.py:833
  154.4 10.1 %all_gather.6.refs_0_ = bf16[384,256]{1,0:T(8,128)(2,1)S(1)} all-gather(bf16[96,256]{1,0:T(8,128)(2,1)} %get-tuple-element.36), channel_id=1, replica_groups=mesh['dp'=4,'space'=64] {'dp'}, dimensions={0}, use_global_device_ids=true | all-gather | bytes 245760 | tf_op jit(solution)/shard_map/all_gather | solution.py:836
  167.0 19.3 %shard_map.256 = bf16[3072,128]{1,0:T(8,128)(2,1)} custom-call(bf16[1024,128]{1,0:T(8,128)(2,1)S(1)} %bitcast.21, bf16[128,64]{1,0:T(8,128)(2,1)S(1)} %copy-done.2, bf16[64,256]{1,0:T(8,128)(2,1)S(1)} %copy-done.9, bf16[32,128]{1,0:T(8,128)(2,1)S(1)} %copy-done.11, bf16[64,128]{1,0:T(8,128)(2,1)S(1)} %copy-done.5, ...), custom_call_target="tpu_custom_call" | custom-call | flops 1500000000 | bytes 20971520 | tf_op jit(solution)/shard_map/pallas_call | solution.py:214
  186.3 36.2 %all_to_all.77 = bf16[64,48,128]{2,1,0:T(8,128)(2,1)S(1)} all-to-all(bf16[64,48,128]{2,1,0:T(8,128)(2,1)} %bitcast.29), channel_id=1, replica_groups=mesh['dp'=4,'space'=64] {'space'}, dimensions={0} | all-to-all | bytes 1572864 | tf_op jit(solution)/shard_map/all_to_all | solution.py:833
  223.7 8.2 %all_gather.7.refs_1_ = bf16[448,256]{1,0:T(8,128)(2,1)S(1)} all-gather(bf16[112,256]{1,0:T(8,128)(2,1)} %shard_map.257), channel_id=1, replica_groups=mesh['dp'=4,'space'=64] {'dp'}, dimensions={0}, use_global_device_ids=true | all-gather | bytes 286720 | tf_op jit(solution)/shard_map/all_gather | solution.py:836
  (45 shorter events, 14.0 us)
Async XLA Ops:
  0.6 32.7 %copy-start.3 = (bf16[128,64]{1,0:T(8,128)(2,1)S(1)}, bf16[128,64]{1,0:T(8,128)(2,1)}, u32[]{:S(2)}) copy-start(bf16[128,64]{1,0:T(8,128)(2,1)} %constant.26.clone.refs_3_) | copy-start | bytes 49156
  0.6 32.7 %copy-start.4 = (bf16[64,128]{1,0:T(8,128)(2,1)S(1)}, bf16[64,128]{1,0:T(8,128)(2,1)}, u32[]{:S(2)}) copy-start(bf16[64,128]{1,0:T(8,128)(2,1)} %constant.25.clone.refs_2_.refs_1_) | copy-start | bytes 49156
  0.7 21.5 %copy-start.14 = (bf16[64,64]{1,0:T(8,128)(2,1)S(1)}, bf16[64,64]{1,0:T(8,128)(2,1)}, u32[]{:S(2)}) copy-start(bf16[64,64]{1,0:T(8,128)(2,1)} %param.25) | copy-start | bytes 24580
  0.7 21.6 %copy-start.15 = (f32[64]{0:T(128)S(1)}, f32[64]{0:T(128)}, u32[]{:S(2)}) copy-start(f32[64]{0:T(128)} %param.27) | copy-start | bytes 772
  0.7 32.7 %copy-start.1 = (bf16[2,16,4,64,64]{4,3,2,1,0:T(8,128)(2,1)S(1)}, bf16[2,16,4,64,64]{4,3,2,1,0:T(8,128)(2,1)}, u32[]{:S(2)}) copy-start(bf16[2,16,4,64,64]{4,3,2,1,0:T(8,128)(2,1)} %refs_1_.7) | copy-start | bytes 3145732
  7.0 26.4 %all-to-all-start = ((bf16[64,8,128]{2,1,0:T(8,128)(2,1)}), bf16[64,8,128]{2,1,0:T(8,128)(2,1)S(1)}, u32[]{:S(2)}, u32[]{:S(2)}) async-start(bf16[64,8,128]{2,1,0:T(8,128)(2,1)} %bitcast.30), calls=%async_computation | async-start | bytes 262144 | tf_op jit(solution)/shard_map/all_to_all | solution.py:833
  36.5 20.5 %all-to-all-start.1 = ((bf16[64,8,128]{2,1,0:T(8,128)(2,1)}), bf16[64,8,128]{2,1,0:T(8,128)(2,1)S(1)}, u32[]{:S(2)}, u32[]{:S(2)}) async-start(bf16[64,8,128]{2,1,0:T(8,128)(2,1)} %bitcast.33), calls=%async_computation.1 | async-start | bytes 262144 | tf_op jit(solution)/shard_map/all_to_all | solution.py:833
  45.8 11.3 %copy-start.2 = (bf16[128,64]{1,0:T(8,128)(2,1)S(1)}, bf16[128,64]{1,0:T(8,128)(2,1)}, u32[]{:S(2)}) copy-start(bf16[128,64]{1,0:T(8,128)(2,1)} %constant.24.clone.refs_1_) | copy-start | bytes 49156
  45.8 11.3 %copy-start.5 = (bf16[64,128]{1,0:T(8,128)(2,1)S(1)}, bf16[64,128]{1,0:T(8,128)(2,1)}, u32[]{:S(2)}) copy-start(bf16[64,128]{1,0:T(8,128)(2,1)} %constant.23.clone.refs_4_) | copy-start | bytes 49156
  45.8 11.3 %copy-start.6 = (bf16[64,256]{1,0:T(8,128)(2,1)S(1)}, bf16[64,256]{1,0:T(8,128)(2,1)}, u32[]{:S(2)}) copy-start(bf16[64,256]{1,0:T(8,128)(2,1)} %constant.21.clone.refs_2_) | copy-start | bytes 98308
  45.8 11.3 %copy-start.10 = (bf16[32,128]{1,0:T(8,128)(2,1)S(1)}, bf16[32,128]{1,0:T(8,128)(2,1)}, u32[]{:S(2)}) copy-start(bf16[32,128]{1,0:T(8,128)(2,1)} %constant.19.clone.third_far.refs_3_) | copy-start | bytes 24580
  57.1 18.4 %copy-start.7 = (bf16[64,64]{1,0:T(8,128)(2,1)S(1)}, bf16[64,64]{1,0:T(8,128)(2,1)}, u32[]{:S(2)}) copy-start(bf16[64,64]{1,0:T(8,128)(2,1)} %refs_0_.3) | copy-start | bytes 24580
  57.1 18.5 %copy-start.16 = (f32[64]{0:T(128)S(1)}, f32[64]{0:T(128)}, u32[]{:S(2)}) copy-start(f32[64]{0:T(128)} %param.28) | copy-start | bytes 772
  69.5 17.4 %all-to-all-start.2 = ((bf16[64,8,128]{2,1,0:T(8,128)(2,1)}), bf16[64,8,128]{2,1,0:T(8,128)(2,1)S(1)}, u32[]{:S(2)}, u32[]{:S(2)}) async-start(bf16[64,8,128]{2,1,0:T(8,128)(2,1)} %bitcast.34), calls=%async_computation.2 | async-start | bytes 262144 | tf_op jit(solution)/shard_map/all_to_all | solution.py:833
  75.7 11.2 %copy-start = (bf16[2,16,4,64,64]{4,3,2,1,0:T(8,128)(2,1)S(1)}, bf16[2,16,4,64,64]{4,3,2,1,0:T(8,128)(2,1)}, u32[]{:S(2)}) copy-start(bf16[2,16,4,64,64]{4,3,2,1,0:T(8,128)(2,1)} %refs_1_.9) | copy-start | bytes 3145732
  90.0 18.0 %all-to-all-start.3 = ((bf16[64,8,128]{2,1,0:T(8,128)(2,1)}), bf16[64,8,128]{2,1,0:T(8,128)(2,1)S(1)}, u32[]{:S(2)}, u32[]{:S(2)}) async-start(bf16[64,8,128]{2,1,0:T(8,128)(2,1)} %bitcast.32), calls=%async_computation.3 | async-start | bytes 262144 | tf_op jit(solution)/shard_map/all_to_all | solution.py:833
  96.9 11.2 %copy-start.11 = (bf16[32,128]{1,0:T(8,128)(2,1)S(1)}, bf16[32,128]{1,0:T(8,128)(2,1)}, u32[]{:S(2)}) copy-start(bf16[32,128]{1,0:T(8,128)(2,1)} %constant.20.clone.refs_3_) | copy-start | bytes 24580
  122.8 19.2 %all-to-all-start.4 = ((bf16[64,8,128]{2,1,0:T(8,128)(2,1)}), bf16[64,8,128]{2,1,0:T(8,128)(2,1)S(1)}, u32[]{:S(2)}, u32[]{:S(2)}) async-start(bf16[64,8,128]{2,1,0:T(8,128)(2,1)} %bitcast.35), calls=%async_computation.4 | async-start | bytes 262144 | tf_op jit(solution)/shard_map/all_to_all | solution.py:833
  130.6 11.3 %copy-start.12 = (bf16[32,256]{1,0:T(8,128)(2,1)S(1)}, bf16[32,256]{1,0:T(8,128)(2,1)}, u32[]{:S(2)}) copy-start(bf16[32,256]{1,0:T(8,128)(2,1)} %get-tuple-element.34.refs_5_) | copy-start | bytes 49156
  130.7 11.3 %copy-start.13 = (bf16[32,256]{1,0:T(8,128)(2,1)S(1)}, bf16[32,256]{1,0:T(8,128)(2,1)}, u32[]{:S(2)}) copy-start(bf16[32,256]{1,0:T(8,128)(2,1)} %get-tuple-element.35.refs_6_) | copy-start | bytes 49156
  130.7 36.3 %copy-start.9 = (bf16[64,256]{1,0:T(8,128)(2,1)S(1)}, bf16[64,256]{1,0:T(8,128)(2,1)}, u32[]{:S(2)}) copy-start(bf16[64,256]{1,0:T(8,128)(2,1)} %constant.22.clone.refs_2_) | copy-start | bytes 98308
  142.0 0.8 copy-start.8
  146.3 20.7 %all-to-all-start.5 = ((bf16[64,16,128]{2,1,0:T(8,128)(2,1)}), bf16[64,16,128]{2,1,0:T(8,128)(2,1)S(1)}, u32[]{:S(2)}, u32[]{:S(2)}) async-start(bf16[64,16,128]{2,1,0:T(8,128)(2,1)} %bitcast.31), calls=%async_computation.5 | async-start | bytes 524288 | tf_op jit(solution)/shard_map/all_to_all | solution.py:833

commit v3 on v2

--- a/solution.py
+++ b/solution.py
@@ -120,7 +120,7 @@
 VM = pl.BlockSpec(memory_space=pltpu.VMEM)
 
 
-GROUPS = 8
+GROUPS = 4
 ROWS = 2 * LANES * CHANNELS
 
 
@@ -174,7 +174,7 @@
             for index in range(len(big)):
                 coming(index, group).start()
 
-        def loop(body, carry=0, unroll=4):
+        def loop(body, carry=0, unroll=PAIRS // GROUPS):
             per = PAIRS // GROUPS
 
             def some(i, carry):
@@ -300,17 +300,7 @@
 Y_ROWS = Y_STEP * CHANNELS
 
 
-def relay_kernel(pointed, *refs):
-    if pointed:
-        point_ref, bias_ref = refs[:2]
-        refs = refs[2:]
-    outs = 2 if pointed else 1
-    field = refs[0]
-    out_far = refs[2 : 2 + outs]
-    near_field = refs[2 + outs]
-    out_near = refs[3 + outs : 3 + 2 * outs]
-    rows_ref, in_sem, out_sem = refs[3 + 2 * outs :]
-
+def relay_kernel(field, _, out_far, near_field, out_near, rows_ref, in_sem, out_sem):
     def coming(step):
         x = step // Y_STEPS
         cut = pl.ds(pl.multiple_of((step % Y_STEPS) * Y_STEP, Y_STEP), Y_STEP)
@@ -318,17 +308,12 @@
             field.at[0, :, x, cut], near_field.at[:, x, cut], in_sem.at[step]
         )
 
-    def going(index, step):
+    def going(step):
         cut = pl.ds(pl.multiple_of(step * Y_ROWS, Y_ROWS), Y_ROWS)
-        return pltpu.make_async_copy(
-            out_near[index].at[cut], out_far[index].at[cut], out_sem.at[index, step]
-        )
+        return pltpu.make_async_copy(out_near.at[cut], out_far.at[cut], out_sem.at[step])
 
     for step in range(2 * Y_STEPS):
         coming(step).start()
-    if pointed:
-        point = point_ref[...]
-        shift = jnp.concatenate([bias_ref[...], bias_ref[...]], axis=1)
 
     def some(step, carry):
         coming(step).wait()
@@ -339,41 +324,34 @@
         for y in range(0, Y_STEP, 2):
             pair = [rows_ref[pl.ds(y + e, CHANNELS, stride=Y_STEP), :] for e in range(2)]
             tile = step * (Y_STEP // 2) + y // 2
-            out_near[0][tile_at(tile), :] = jnp.concatenate(pair, axis=0).astype(BF16)
-            if pointed:
-                wide = jnp.concatenate(pair, axis=1).astype(BF16)
-                store_wide(out_near[1], tile, mm(point, wide) + shift)
-        for index in range(outs):
-            going(index, step).start()
+            out_near[tile_at(tile), :] = jnp.concatenate(pair, axis=0).astype(BF16)
+        going(step).start()
         return carry
 
     lax.fori_loop(0, 2 * Y_STEPS, some, 0)
     for step in range(2 * Y_STEPS):
-        for index in range(outs):
-            going(index, step).wait()
-
-
-def relay(field, *operands, token):
+        going(step).wait()
+
+
+def relay(field, token):
     far = pl.BlockSpec(memory_space=pl.ANY)
-    pointed = bool(operands)
-    outs = 2 if pointed else 1
     return pl.pallas_call(
-        functools.partial(relay_kernel, pointed),
-        out_shape=[pltpu.HBM((ROWS, LANES), BF16)] * outs,
-        in_specs=[VM] * len(operands) + [far] * 2,
-        out_specs=[far] * outs,
-        scratch_shapes=[pltpu.VMEM(field.shape[1:], BF16)]
-        + [pltpu.VMEM((ROWS, LANES), BF16)] * outs
-        + [
+        relay_kernel,
+        out_shape=pltpu.HBM((ROWS, LANES), BF16),
+        in_specs=[far] * 2,
+        out_specs=far,
+        scratch_shapes=[
+            pltpu.VMEM(field.shape[1:], BF16),
+            pltpu.VMEM((ROWS, LANES), BF16),
             pltpu.VMEM((Y_ROWS, LANES), F32),
             pltpu.SemaphoreType.DMA((2 * Y_STEPS,)),
-            pltpu.SemaphoreType.DMA((outs, 2 * Y_STEPS)),
+            pltpu.SemaphoreType.DMA((2 * Y_STEPS,)),
         ],
         cost_estimate=pl.CostEstimate(
             flops=600_000_000, bytes_accessed=12 << 20, transcendentals=0
         ),
         compiler_params=pltpu.CompilerParams(vmem_limit_bytes=VMEM_LIMIT),
-    )(*[near(operand) for operand in operands], afar(field), afar(token))
+    )(afar(field), afar(token))
 
 
 def own_spectrum(wide, table, place, block=8):
@@ -545,7 +523,7 @@
 
 def weight_one_kernel(factor, small, _, __, ___, plain, scratch, loop):
     early_ref, all_ref = small
-    out_ref, one_ref, two_ref, bias_ref = plain
+    out_ref, one_ref, two_ref, bias_one_ref, bias_two_ref = plain
     sums = all_ref[32:112, :].astype(F32)
     for n in range(1, all_ref.shape[0] // 112):
         sums = sums + all_ref[n * 112 + 32 : (n + 1) * 112, :].astype(F32)
@@ -556,7 +534,9 @@
     two = jnp.concatenate([sums[32:64, :LANES], sums[32:64, LANES:]], axis=0)
     two_ref[...] = (two + turned(two))[:, :CHANNELS]
     bias = jnp.concatenate([sums[64:72, :LANES], sums[64:72, LANES:]], axis=0)
-    bias_ref[...] = bias + turned(bias)
+    bias = bias + turned(bias)
+    bias_one_ref[...] = bias[0:1, :CHANNELS]
+    bias_two_ref[...] = bias[8:9, :CHANNELS]
     outer_products(rows_of(early_ref, 96, 0), rows_of(all_ref, 112, 0), out_ref)
 
 
@@ -767,7 +747,7 @@
     ref[pl.ds(at + CHANNELS, CHANNELS), :] = wide[:, LANES:].astype(BF16)
 
 
-def layer_two_kernel(small, big, _, kinds, __, scratch, loop):
+def point_kernel(small, big, _, kinds, __, scratch, loop):
     point, bias = small
     weights = point[...]
     shift = jnp.concatenate([bias[...], bias[...]], axis=1)
@@ -787,7 +767,7 @@
             kinds[0][at, :] = gelu_slope(big[0][at, :].astype(F32)).astype(BF16)
         return carry
 
-    loop(body, unroll=2)
+    loop(body)
 
 
 def point_back_kernel(small, big, outs, kinds, _, scratch, loop):
@@ -832,6 +812,20 @@
     def exchange(chunk):
         return lax.all_to_all(chunk, "space", split_axis=0, concat_axis=0, tiled=True)
 
+    def point_map(values, point, bias, token):
+        return call(
+            point_kernel,
+            [],
+            [],
+            500_000_000,
+            12 << 20,
+            point.T,
+            spread(bias),
+            big=[values],
+            kinds=[BF16],
+            token=token,
+        )[0]
+
     def samples(spectrum):
         return lax.all_gather(spectrum, "dp", axis=0, tiled=True)
 
@@ -839,11 +833,11 @@
 
     chunk = first_partial(field_in, third_forward, natural_second)
     got = exchange(chunk)
-    values, base = relay(field_in, point_one.T, spread(bias_one), token=chunk)
-
-    chunk, spec_one = mixing(got, spectral_one, first_fwd, first_inv, token=base)
+    values = relay(field_in, chunk)
+
+    chunk, spec_one = mixing(got, spectral_one, first_fwd, first_inv, token=values)
     got = exchange(chunk)
-    cot = relay(cotangent, token=chunk)[0]
+    base = point_map(values, point_one, bias_one, chunk)
 
     chunk, hidden, preact = planes(
         hidden_kernel,
@@ -854,26 +848,14 @@
         third_forward,
         second_fwd,
         big=[base],
-        token=cot,
+        token=spec_one,
     )
     got = exchange(chunk)
-    base = call(
-        layer_two_kernel,
-        [],
-        [],
-        500_000_000,
-        12 << 20,
-        point_two.T,
-        spread(bias_two),
-        big=[hidden],
-        kinds=[BF16],
-    )[0]
+    base = point_map(hidden, point_two, bias_two, chunk)
 
     chunk, spec_two = mixing(got, spectral_two, first_fwd, first_inv, token=base)
     got = exchange(chunk)
-    slope = call(
-        slope_kernel, [], [], 500_000_000, 12 << 20, big=[preact], kinds=[BF16], token=chunk
-    )[0]
+    cot = relay(cotangent, chunk)
 
     chunk, grad_two = planes(
         grad_two_kernel,
@@ -884,7 +866,7 @@
         third_adjoint,
         second_adj,
         big=[base, cot],
-        token=slope,
+        token=spec_two,
     )
     got = exchange(chunk)
     term_two, base = call(
@@ -914,15 +896,8 @@
     )
     got = exchange(chunk)
     early = samples(early)
-    spectral_grad_two = call(
-        weight_two_kernel,
-        [],
-        [],
-        200_000_000,
-        3 << 20,
-        early,
-        plain=[jax.ShapeDtypeStruct(shape, BF16)],
-        token=chunk,
+    slope = call(
+        slope_kernel, [], [], 500_000_000, 12 << 20, big=[preact], kinds=[BF16], token=chunk
     )[0]
 
     chunk = call(
@@ -942,7 +917,7 @@
         third_adjoint,
         second_adj,
         big=[base, slope, values],
-        token=spectral_grad_two,
+        token=early,
     )[0]
     got = exchange(chunk)
     late = call(
@@ -954,10 +929,21 @@
         got,
         first_adj,
     )[0]
+    spectral_grad_two = call(
+        weight_two_kernel,
+        [],
+        [],
+        200_000_000,
+        3 << 20,
+        early,
+        plain=[jax.ShapeDtypeStruct(shape, BF16)],
+        token=late,
+    )[0]
     late = samples(late)
     cells = lax.axis_size("dp") * lax.axis_size("space") * 2 * LANES * LANES
     square = jax.ShapeDtypeStruct((CHANNELS, CHANNELS), F32)
-    spectral_grad_one, point_grad_one, point_grad_two, biases = call(
+    line = jax.ShapeDtypeStruct((1, CHANNELS), F32)
+    spectral_grad_one, point_grad_one, point_grad_two, bias_grad_one, bias_grad_two = call(
         functools.partial(weight_one_kernel, 1.0 / math.sqrt(cells)),
         [],
         [],
@@ -969,16 +955,18 @@
             jax.ShapeDtypeStruct(shape, BF16),
             square,
             square,
-            jax.ShapeDtypeStruct((16, LANES), F32),
+            line,
+            line,
         ],
+        token=spectral_grad_two,
     )
     return (
         spectral_grad_one,
         spectral_grad_two,
         point_grad_one,
         point_grad_two,
-        biases[0, :CHANNELS],
-        biases[8, :CHANNELS],
+        bias_grad_one.reshape(CHANNELS),
+        bias_grad_two.reshape(CHANNELS),
     )
 
 

time: 235 us -> 224 us (0.953)
  Pallas kernels: 101 us -> 90.6 us
  starting transfers between devices: 53.2 us -> 44.6 us
  waiting for transfers between devices: 23 us -> 31.6 us
    all_to_all x6, starting transfers between devices: 53.2 us -> 44.6 us  [exchange(): lax.all_to_all(chunk, 'space', split_axis=0, concat_axis=0, tiled=True)]
    all_to_all x6, waiting for transfers between devices: 23 us -> 31.6 us  [exchange(): lax.all_to_all(chunk, 'space', split_axis=0, concat_axis=0, tiled=True)]
    pallas_call x12 -> x13, Pallas kernels: 82 us -> 74.2 us  [call(): pl.pallas_call(whole_kernel, out_shape=shapes + list(plain), in_specs=[VM...]
    pallas_call x2, Pallas kernels: 13.1 us -> 10.3 us  [relay(): pl.pallas_call(relay_kernel, out_shape=pltpu.HBM((ROWS, LANES), BF16), in...]
  transfers between devices with their start and end apart: 6 -> 6, of which waited for: 5 -> 5; matrix products, arithmetic and copies ran while one was open for 0% -> 0% of each run, Pallas kernels for 15% -> 14%
where the time goes in v3:
time: 224 us; the launch traced here: 223 us
  Pallas kernels  90.6 us (40%)
  blocking collectives  53.7 us (24%)
  starting transfers between devices  44.6 us (20%)
  waiting for transfers between devices  31.6 us (14%)
    pallas_call x13, Pallas kernels, call(): pl.pallas_call(whole_kernel, out_shape=shapes + list(plain), in_specs=[VM...  74.2 us
    all_to_all x6, starting transfers between devices, exchange(): lax.all_to_all(chunk, 'space', split_axis=0, concat_axis=0, tiled=True)  44.6 us
    all_to_all x1, blocking collectives, exchange(): lax.all_to_all(chunk, 'space', split_axis=0, concat_axis=0, tiled=True)  34.9 us
    all_to_all x6, waiting for transfers between devices, exchange(): lax.all_to_all(chunk, 'space', split_axis=0, concat_axis=0, tiled=True)  31.6 us
    all_gather x2, blocking collectives, samples(): return lax.all_gather(spectrum, 'dp', axis=0, tiled=True)  18.9 us
    pallas_call x2, Pallas kernels, relay(): pl.pallas_call(relay_kernel, out_shape=pltpu.HBM((ROWS, LANES), BF16), in...  10.3 us
    pallas_call x1, Pallas kernels, first_partial(): pl.pallas_call(spectrum_kernel, out_shape=pltpu.HBM((512, LANES), BF16),...  6.16 us
  transfers between devices with their start and end apart: 6, of which 5 were waited for; matrix products, arithmetic and copies ran while one was open for 0% of the time, Pallas kernels for 14%

profile of v3, /device:TPU:1, one launch (start us, length us, event | category | flops | bytes accessed | tf_op | source)
XLA Modules:
  0.0 223.0 jit_solution(3975449985673653844)
XLA Ops:
  0.6 6.2 %shard_map.244._ = bf16[512,128]{1,0:T(8,128)(2,1)} custom-call(bf16[1,64,2,128,128]{4,3,2,1,0:T(8,128)(2,1)} %field.4, bf16[32,128]{1,0:T(8,128)(2,1)} %constant.19.clone.third_far.refs_3_, bf16[32,256]{1,0:T(8,128)(2,1)} %constant.18.clone.second_far), custom_call_target="tpu_custom_call" | custom-call | flops 600000000 | bytes 6291456 | tf_op jit(solution)/shard_map/pallas_call | solution.py:277
  6.8 15.1 %all-to-all-start = ((bf16[64,8,128]{2,1,0:T(8,128)(2,1)}), bf16[64,8,128]{2,1,0:T(8,128)(2,1)S(1)}, u32[]{:S(2)}, u32[]{:S(2)}) async-start(bf16[64,8,128]{2,1,0:T(8,128)(2,1)} %bitcast.28), calls=%async_computation | async-start | bytes 262144 | tf_op jit(solution)/shard_map/all_to_all | solution.py:813
  22.0 5.2 %shard_map.245.refs_4_.refs_2_.refs_7_ = bf16[16384,128]{1,0:T(8,128)(2,1)} custom-call(bf16[1,64,2,128,128]{4,3,2,1,0:T(8,128)(2,1)} %field.4, bf16[512,128]{1,0:T(8,128)(2,1)} %shard_map.244._), custom_call_target="tpu_custom_call" | custom-call | flops 600000000 | bytes 12582912 | tf_op jit(solution)/shard_map/pallas_call | solution.py:338
  27.2 5.9 %all-to-all-done = bf16[64,8,128]{2,1,0:T(8,128)(2,1)S(1)} async-done(((bf16[64,8,128]{2,1,0:T(8,128)(2,1)}), bf16[64,8,128]{2,1,0:T(8,128)(2,1)S(1)}, u32[]{:S(2)}, u32[]{:S(2)}) %all-to-all-start) | async-done | bytes 131104 | tf_op jit(solution)/shard_map/all_to_all | solution.py:813
  36.3 6.3 %all-to-all-start.1 = ((bf16[64,8,128]{2,1,0:T(8,128)(2,1)}), bf16[64,8,128]{2,1,0:T(8,128)(2,1)S(1)}, u32[]{:S(2)}, u32[]{:S(2)}) async-start(bf16[64,8,128]{2,1,0:T(8,128)(2,1)} %bitcast.31), calls=%async_computation.1 | async-start | bytes 262144 | tf_op jit(solution)/shard_map/all_to_all | solution.py:813
  42.8 4.0 %shard_map.247.refs_5_ = bf16[16384,128]{1,0:T(8,128)(2,1)} custom-call(bf16[64,64]{1,0:T(8,128)(2,1)S(1)} %bitcast.25, f32[64,128]{1,0:T(8,128)S(1)} %broadcast_in_dim.4.refs_1_, bf16[16384,128]{1,0:T(8,128)(2,1)} %shard_map.245.refs_4_.refs_2_.refs_7_, bf16[512,128]{1,0:T(8,128)(2,1)} %get-tuple-element.24.refs_3_), custom_call_target="tpu_custom_call" | custom-call | flops 500000000 | bytes 12582912 | tf_op jit(solution)/shard_map/pallas_call | solution.py:214
  46.8 7.1 %all-to-all-done.1 = bf16[64,8,128]{2,1,0:T(8,128)(2,1)S(1)} async-done(((bf16[64,8,128]{2,1,0:T(8,128)(2,1)}), bf16[64,8,128]{2,1,0:T(8,128)(2,1)S(1)}, u32[]{:S(2)}, u32[]{:S(2)}) %all-to-all-start.1) | async-done | bytes 131104 | tf_op jit(solution)/shard_map/all_to_all | solution.py:813
  53.9 9.1 %shard_map.248 = (bf16[512,128]{1,0:T(8,128)(2,1)}, bf16[16384,128]{1,0:T(8,128)(2,1)}, bf16[16384,128]{1,0:T(8,128)(2,1)}) custom-call(bf16[512,128]{1,0:T(8,128)(2,1)S(1)} %bitcast.22, bf16[128,64]{1,0:T(8,128)(2,1)S(1)} %copy-done.3, bf16[64,256]{1,0:T(8,128)(2,1)S(1)} %copy-done.7, bf16[32,128]{1,0:T(8,128)(2,1)S(1)} %copy-done.14, ...), custom_call_target="tpu_custom_call" | custom-call | flops 1000000000 | bytes 20971520 | tf_op jit(solution)/shard_map/pallas_call | solution.py:214
  63.0 5.2 %all-to-all-start.2 = ((bf16[64,8,128]{2,1,0:T(8,128)(2,1)}), bf16[64,8,128]{2,1,0:T(8,128)(2,1)S(1)}, u32[]{:S(2)}, u32[]{:S(2)}) async-start(bf16[64,8,128]{2,1,0:T(8,128)(2,1)} %bitcast.30), calls=%async_computation.2 | async-start | bytes 262144 | tf_op jit(solution)/shard_map/all_to_all | solution.py:813
  68.4 4.2 %shard_map.249.refs_4_.refs_5_ = bf16[16384,128]{1,0:T(8,128)(2,1)} custom-call(bf16[64,64]{1,0:T(8,128)(2,1)S(1)} %bitcast.26, f32[64,128]{1,0:T(8,128)S(1)} %broadcast_in_dim.5.refs_1_, bf16[16384,128]{1,0:T(8,128)(2,1)} %get-tuple-element.27.refs_2_.refs_1_, bf16[512,128]{1,0:T(8,128)(2,1)} %get-tuple-element.26.refs_3_), custom_call_target="tpu_custom_call" | custom-call | flops 500000000 | bytes 12582912 | tf_op jit(solution)/shard_map/pallas_call | solution.py:214
  72.5 7.0 %all-to-all-done.2 = bf16[64,8,128]{2,1,0:T(8,128)(2,1)S(1)} async-done(((bf16[64,8,128]{2,1,0:T(8,128)(2,1)}), bf16[64,8,128]{2,1,0:T(8,128)(2,1)S(1)}, u32[]{:S(2)}, u32[]{:S(2)}) %all-to-all-start.2) | async-done | bytes 131104 | tf_op jit(solution)/shard_map/all_to_all | solution.py:813
  82.6 5.4 %all-to-all-start.3 = ((bf16[64,8,128]{2,1,0:T(8,128)(2,1)}), bf16[64,8,128]{2,1,0:T(8,128)(2,1)S(1)}, u32[]{:S(2)}, u32[]{:S(2)}) async-start(bf16[64,8,128]{2,1,0:T(8,128)(2,1)} %bitcast.32), calls=%async_computation.3 | async-start | bytes 262144 | tf_op jit(solution)/shard_map/all_to_all | solution.py:813
  88.0 5.1 %shard_map.251.refs_6_ = bf16[16384,128]{1,0:T(8,128)(2,1)} custom-call(bf16[1,64,2,128,128]{4,3,2,1,0:T(8,128)(2,1)} %field.5, bf16[512,128]{1,0:T(8,128)(2,1)} %get-tuple-element.28._), custom_call_target="tpu_custom_call" | custom-call | flops 600000000 | bytes 12582912 | tf_op jit(solution)/shard_map/pallas_call | solution.py:338
  93.1 6.1 %all-to-all-done.3 = bf16[64,8,128]{2,1,0:T(8,128)(2,1)S(1)} async-done(((bf16[64,8,128]{2,1,0:T(8,128)(2,1)}), bf16[64,8,128]{2,1,0:T(8,128)(2,1)S(1)}, u32[]{:S(2)}, u32[]{:S(2)}) %all-to-all-start.3) | async-done | bytes 131104 | tf_op jit(solution)/shard_map/all_to_all | solution.py:813
  99.2 11.3 %shard_map.252 = (bf16[512,128]{1,0:T(8,128)(2,1)}, bf16[16384,128]{1,0:T(8,128)(2,1)}) custom-call(bf16[512,128]{1,0:T(8,128)(2,1)S(1)} %bitcast.20, bf16[128,64]{1,0:T(8,128)(2,1)S(1)} %copy-done.3, bf16[64,256]{1,0:T(8,128)(2,1)S(1)} %copy-done.7, bf16[32,128]{1,0:T(8,128)(2,1)S(1)} %copy-done.13, bf16[64,128]{1,0:T(8,128)(2,1)S(1)} %copy-done.6, ...), custom_call_target="tpu_custom_call" | custom-call | flops 1000000000 | bytes 20971520 | tf_op jit(solution)/shard_map/pallas_call | solution.py:214
  110.5 6.0 %all-to-all-start.4 = ((bf16[64,8,128]{2,1,0:T(8,128)(2,1)}), bf16[64,8,128]{2,1,0:T(8,128)(2,1)S(1)}, u32[]{:S(2)}, u32[]{:S(2)}) async-start(bf16[64,8,128]{2,1,0:T(8,128)(2,1)} %bitcast.33), calls=%async_computation.4 | async-start | bytes 262144 | tf_op jit(solution)/shard_map/all_to_all | solution.py:813
  116.5 5.7 %shard_map.253 = (f32[80,64]{1,0:T(8,128)}, bf16[16384,128]{1,0:T(8,128)(2,1)}) custom-call(bf16[64,64]{1,0:T(8,128)(2,1)S(1)} %copy-done.10, bf16[16384,128]{1,0:T(8,128)(2,1)} %get-tuple-element.27.refs_2_.refs_1_, bf16[16384,128]{1,0:T(8,128)(2,1)} %get-tuple-element.31.refs_2_), custom_call_target="tpu_custom_call" | custom-call | flops 1000000000 | bytes 12582912 | tf_op jit(solution)/shard_map/pallas_call | solution.py:214
  122.2 5.6 %all-to-all-done.4 = bf16[64,8,128]{2,1,0:T(8,128)(2,1)S(1)} async-done(((bf16[64,8,128]{2,1,0:T(8,128)(2,1)}), bf16[64,8,128]{2,1,0:T(8,128)(2,1)S(1)}, u32[]{:S(2)}, u32[]{:S(2)}) %all-to-all-start.4) | async-done | bytes 131104 | tf_op jit(solution)/shard_map/all_to_all | solution.py:813
  132.0 6.7 %all-to-all-start.5 = ((bf16[64,16,128]{2,1,0:T(8,128)(2,1)}), bf16[64,16,128]{2,1,0:T(8,128)(2,1)S(1)}, u32[]{:S(2)}, u32[]{:S(2)}) async-start(bf16[64,16,128]{2,1,0:T(8,128)(2,1)} %bitcast.29), calls=%async_computation.5 | async-start | bytes 524288 | tf_op jit(solution)/shard_map/all_to_all | solution.py:813
  138.7 7.2 %shard_map.255.refs_6_ = bf16[16384,128]{1,0:T(8,128)(2,1)} custom-call(bf16[16384,128]{1,0:T(8,128)(2,1)} %get-tuple-element.36.refs_0_, bf16[1024,128]{1,0:T(8,128)(2,1)} %get-tuple-element.34.refs_1_), custom_call_target="tpu_custom_call" | custom-call | flops 500000000 | bytes 12582912 | tf_op jit(solution)/shard_map/pallas_call | solution.py:214
  146.0 9.9 %all_gather.6.refs_8_.refs_0_ = bf16[384,256]{1,0:T(8,128)(2,1)} all-gather(bf16[96,256]{1,0:T(8,128)(2,1)S(1)} %copy-done.15), channel_id=1, replica_groups=mesh['dp'=4,'space'=64] {'dp'}, dimensions={0}, use_global_device_ids=true | all-gather | bytes 245760 | tf_op jit(solution)/shard_map/all_gather | solution.py:830
  155.9 17.1 %shard_map.256 = bf16[3072,128]{1,0:T(8,128)(2,1)} custom-call(bf16[1024,128]{1,0:T(8,128)(2,1)S(1)} %bitcast.19, bf16[128,64]{1,0:T(8,128)(2,1)S(1)} %copy-done.3, bf16[64,256]{1,0:T(8,128)(2,1)S(1)} %copy-done.12, bf16[32,128]{1,0:T(8,128)(2,1)S(1)} %copy-done.13, bf16[64,128]{1,0:T(8,128)(2,1)S(1)} %copy-done.6, ...), custom_call_target="tpu_custom_call" | custom-call | flops 1500000000 | bytes 20971520 | tf_op jit(solution)/shard_map/pallas_call | solution.py:214
  173.1 34.9 %all_to_all.77 = bf16[64,48,128]{2,1,0:T(8,128)(2,1)S(1)} all-to-all(bf16[64,48,128]{2,1,0:T(8,128)(2,1)} %bitcast.27), channel_id=1, replica_groups=mesh['dp'=4,'space'=64] {'space'}, dimensions={0} | all-to-all | bytes 1572864 | tf_op jit(solution)/shard_map/all_to_all | solution.py:813
  209.0 9.0 %all_gather.7.refs_1_ = bf16[448,256]{1,0:T(8,128)(2,1)S(1)} all-gather(bf16[112,256]{1,0:T(8,128)(2,1)} %shard_map.257.refs_1_), channel_id=1, replica_groups=mesh['dp'=4,'space'=64] {'dp'}, dimensions={0}, use_global_device_ids=true | all-gather | bytes 286720 | tf_op jit(solution)/shard_map/all_gather | solution.py:830
  (49 shorter events, 16.7 us)
Async XLA Ops:
  6.8 26.4 %all-to-all-start = ((bf16[64,8,128]{2,1,0:T(8,128)(2,1)}), bf16[64,8,128]{2,1,0:T(8,128)(2,1)S(1)}, u32[]{:S(2)}, u32[]{:S(2)}) async-start(bf16[64,8,128]{2,1,0:T(8,128)(2,1)} %bitcast.28), calls=%async_computation | async-start | bytes 262144 | tf_op jit(solution)/shard_map/all_to_all | solution.py:813
  21.9 11.2 %copy-start.2 = (bf16[2,16,4,64,64]{4,3,2,1,0:T(8,128)(2,1)S(1)}, bf16[2,16,4,64,64]{4,3,2,1,0:T(8,128)(2,1)}, u32[]{:S(2)}) copy-start(bf16[2,16,4,64,64]{4,3,2,1,0:T(8,128)(2,1)} %refs_1_.7) | copy-start | bytes 3145732
  21.9 11.2 %copy-start.4 = (bf16[128,64]{1,0:T(8,128)(2,1)S(1)}, bf16[128,64]{1,0:T(8,128)(2,1)}, u32[]{:S(2)}) copy-start(bf16[128,64]{1,0:T(8,128)(2,1)} %constant.26.clone.refs_3_) | copy-start | bytes 49156
  22.0 11.2 %copy-start.5 = (bf16[64,128]{1,0:T(8,128)(2,1)S(1)}, bf16[64,128]{1,0:T(8,128)(2,1)}, u32[]{:S(2)}) copy-start(bf16[64,128]{1,0:T(8,128)(2,1)} %constant.25.clone.refs_2_.refs_1_) | copy-start | bytes 49156
  27.2 15.4 %copy-start.16 = (bf16[64,64]{1,0:T(8,128)(2,1)S(1)}, bf16[64,64]{1,0:T(8,128)(2,1)}, u32[]{:S(2)}) copy-start(bf16[64,64]{1,0:T(8,128)(2,1)} %param.25) | copy-start | bytes 24580
  27.2 15.5 %copy-start.17 = (f32[64]{0:T(128)S(1)}, f32[64]{0:T(128)}, u32[]{:S(2)}) copy-start(f32[64]{0:T(128)} %param.27) | copy-start | bytes 772
  36.3 17.6 %all-to-all-start.1 = ((bf16[64,8,128]{2,1,0:T(8,128)(2,1)}), bf16[64,8,128]{2,1,0:T(8,128)(2,1)S(1)}, u32[]{:S(2)}, u32[]{:S(2)}) async-start(bf16[64,8,128]{2,1,0:T(8,128)(2,1)} %bitcast.31), calls=%async_computation.1 | async-start | bytes 262144 | tf_op jit(solution)/shard_map/all_to_all | solution.py:813
  42.8 11.2 %copy-start.3 = (bf16[128,64]{1,0:T(8,128)(2,1)S(1)}, bf16[128,64]{1,0:T(8,128)(2,1)}, u32[]{:S(2)}) copy-start(bf16[128,64]{1,0:T(8,128)(2,1)} %constant.24.clone.refs_1_) | copy-start | bytes 49156
  42.8 11.2 %copy-start.6 = (bf16[64,128]{1,0:T(8,128)(2,1)S(1)}, bf16[64,128]{1,0:T(8,128)(2,1)}, u32[]{:S(2)}) copy-start(bf16[64,128]{1,0:T(8,128)(2,1)} %constant.23.clone.refs_4_) | copy-start | bytes 49156
  42.8 11.2 %copy-start.7 = (bf16[64,256]{1,0:T(8,128)(2,1)S(1)}, bf16[64,256]{1,0:T(8,128)(2,1)}, u32[]{:S(2)}) copy-start(bf16[64,256]{1,0:T(8,128)(2,1)} %constant.21.clone.refs_2_) | copy-start | bytes 98308
  42.8 11.2 %copy-start.14 = (bf16[32,128]{1,0:T(8,128)(2,1)S(1)}, bf16[32,128]{1,0:T(8,128)(2,1)}, u32[]{:S(2)}) copy-start(bf16[32,128]{1,0:T(8,128)(2,1)} %constant.19.clone.third_far.refs_3_) | copy-start | bytes 24580
  46.8 21.3 %copy-start.10 = (bf16[64,64]{1,0:T(8,128)(2,1)S(1)}, bf16[64,64]{1,0:T(8,128)(2,1)}, u32[]{:S(2)}) copy-start(bf16[64,64]{1,0:T(8,128)(2,1)} %refs_0_.1) | copy-start | bytes 24580
  46.8 21.4 %copy-start.18 = (f32[64]{0:T(128)S(1)}, f32[64]{0:T(128)}, u32[]{:S(2)}) copy-start(f32[64]{0:T(128)} %param.28) | copy-start | bytes 772
  63.0 16.5 %all-to-all-start.2 = ((bf16[64,8,128]{2,1,0:T(8,128)(2,1)}), bf16[64,8,128]{2,1,0:T(8,128)(2,1)S(1)}, u32[]{:S(2)}, u32[]{:S(2)}) async-start(bf16[64,8,128]{2,1,0:T(8,128)(2,1)} %bitcast.30), calls=%async_computation.2 | async-start | bytes 262144 | tf_op jit(solution)/shard_map/all_to_all | solution.py:813
  68.4 11.2 %copy-start = (bf16[2,16,4,64,64]{4,3,2,1,0:T(8,128)(2,1)S(1)}, bf16[2,16,4,64,64]{4,3,2,1,0:T(8,128)(2,1)}, u32[]{:S(2)}) copy-start(bf16[2,16,4,64,64]{4,3,2,1,0:T(8,128)(2,1)} %refs_1_.9) | copy-start | bytes 3145732
  82.6 16.6 %all-to-all-start.3 = ((bf16[64,8,128]{2,1,0:T(8,128)(2,1)}), bf16[64,8,128]{2,1,0:T(8,128)(2,1)S(1)}, u32[]{:S(2)}, u32[]{:S(2)}) async-start(bf16[64,8,128]{2,1,0:T(8,128)(2,1)} %bitcast.32), calls=%async_computation.3 | async-start | bytes 262144 | tf_op jit(solution)/shard_map/all_to_all | solution.py:813
  88.0 11.2 %copy-start.13 = (bf16[32,128]{1,0:T(8,128)(2,1)S(1)}, bf16[32,128]{1,0:T(8,128)(2,1)}, u32[]{:S(2)}) copy-start(bf16[32,128]{1,0:T(8,128)(2,1)} %constant.20.clone.refs_3_) | copy-start | bytes 24580
  110.5 17.3 %all-to-all-start.4 = ((bf16[64,8,128]{2,1,0:T(8,128)(2,1)}), bf16[64,8,128]{2,1,0:T(8,128)(2,1)S(1)}, u32[]{:S(2)}, u32[]{:S(2)}) async-start(bf16[64,8,128]{2,1,0:T(8,128)(2,1)} %bitcast.33), calls=%async_computation.4 | async-start | bytes 262144 | tf_op jit(solution)/shard_map/all_to_all | solution.py:813
  116.5 11.3 %copy-start.8 = (bf16[32,256]{1,0:T(8,128)(2,1)S(1)}, bf16[32,256]{1,0:T(8,128)(2,1)}, u32[]{:S(2)}) copy-start(bf16[32,256]{1,0:T(8,128)(2,1)} %get-tuple-element.25.refs_6_.refs_5_) | copy-start | bytes 49156
  116.5 11.3 %copy-start.9 = (bf16[32,256]{1,0:T(8,128)(2,1)S(1)}, bf16[32,256]{1,0:T(8,128)(2,1)}, u32[]{:S(2)}) copy-start(bf16[32,256]{1,0:T(8,128)(2,1)} %get-tuple-element.29.refs_7_.refs_6_) | copy-start | bytes 49156
  132.0 23.9 %all-to-all-start.5 = ((bf16[64,16,128]{2,1,0:T(8,128)(2,1)}), bf16[64,16,128]{2,1,0:T(8,128)(2,1)S(1)}, u32[]{:S(2)}, u32[]{:S(2)}) async-start(bf16[64,16,128]{2,1,0:T(8,128)(2,1)} %bitcast.29), calls=%async_computation.5 | async-start | bytes 524288 | tf_op jit(solution)/shard_map/all_to_all | solution.py:813
  138.7 7.3 %copy-start.15 = (bf16[96,256]{1,0:T(8,128)(2,1)S(1)}, bf16[96,256]{1,0:T(8,128)(2,1)}, u32[]{:S(2)}) copy-start(bf16[96,256]{1,0:T(8,128)(2,1)} %get-tuple-element.33) | copy-start | bytes 147460
  138.7 17.2 %copy-start.12 = (bf16[64,256]{1,0:T(8,128)(2,1)S(1)}, bf16[64,256]{1,0:T(8,128)(2,1)}, u32[]{:S(2)}) copy-start(bf16[64,256]{1,0:T(8,128)(2,1)} %constant.22.clone.refs_2_) | copy-start | bytes 98308
  155.9 62.1 %copy-start.1 = (bf16[384,256]{1,0:T(8,128)(2,1)S(1)}, bf16[384,256]{1,0:T(8,128)(2,1)}, u32[]{:S(2)}) copy-start(bf16[384,256]{1,0:T(8,128)(2,1)} %all_gather.6.refs_8_.refs_0_) | copy-start | bytes 589828
  (1 other events, 0.8 us)

commit v4 on v3

--- a/solution.py
+++ b/solution.py
@@ -136,10 +136,11 @@
     kernel, outs, scratch, flops, moved, *operands, big=(), kinds=(), plain=(), token=None
 ):
     cut = ROWS // GROUPS
+    extra = [] if token is None else list(token) if isinstance(token, list) else [token]
     counts = [
         len(operands),
         len(big),
-        0 if token is None else 1,
+        len(extra),
         len(outs),
         len(kinds),
         len(plain),
@@ -208,7 +209,6 @@
 
     operands = [near(operand) for operand in operands]
     far = pl.BlockSpec(memory_space=pl.ANY)
-    extra = [] if token is None else [token]
     shapes = [pltpu.HBM(shape, kind) for shape, kind in outs]
     shapes += [pltpu.HBM((ROWS, LANES), kind) for kind in kinds]
     return pl.pallas_call(
@@ -515,18 +515,27 @@
     ).astype(F32)
 
 
-def weight_two_kernel(small, _, __, ___, plain, scratch, loop):
-    (all_ref,) = small
-    (out_ref,) = plain
-    outer_products(rows_of(all_ref, 96, 32), rows_of(all_ref, 96, 64), out_ref)
-
-
-def weight_one_kernel(factor, small, _, __, ___, plain, scratch, loop):
-    early_ref, all_ref = small
-    out_ref, one_ref, two_ref, bias_one_ref, bias_two_ref = plain
-    sums = all_ref[32:112, :].astype(F32)
-    for n in range(1, all_ref.shape[0] // 112):
-        sums = sums + all_ref[n * 112 + 32 : (n + 1) * 112, :].astype(F32)
+def in_order(index, parts, ordered):
+    rows = parts[0].shape[0]
+    for k, part in enumerate(parts):
+        at = pl.multiple_of((index ^ k) * rows, 16)
+        ordered[pl.ds(at, rows), :] = part[...].astype(F32)
+
+
+def weight_two_kernel(index_ref, *refs):
+    early, _, out_ref, ordered = refs[:4], refs[4], refs[5], refs[6]
+    in_order(index_ref[0], early, ordered)
+    outer_products(rows_of(ordered, 96, 32), rows_of(ordered, 96, 64), out_ref)
+
+
+def weight_one_kernel(factor, index_ref, *refs):
+    early, late = refs[:4], refs[4:8]
+    out_ref, one_ref, two_ref, bias_one_ref, bias_two_ref, early_all, late_all = refs[9:]
+    in_order(index_ref[0], early, early_all)
+    in_order(index_ref[0], late, late_all)
+    sums = late_all[32:112, :]
+    for n in range(1, 4):
+        sums = sums + late_all[n * 112 + 32 : (n + 1) * 112, :]
     sums = sums * factor
     one = sums[:32, :LANES] + sums[:32, LANES:]
     one_ref[0:32, :] = one[:, :CHANNELS]
@@ -537,7 +546,25 @@
     bias = bias + turned(bias)
     bias_one_ref[...] = bias[0:1, :CHANNELS]
     bias_two_ref[...] = bias[8:9, :CHANNELS]
-    outer_products(rows_of(early_ref, 96, 0), rows_of(all_ref, 112, 0), out_ref)
+    outer_products(rows_of(early_all, 96, 0), rows_of(late_all, 112, 0), out_ref)
+
+
+def weight_call(kernel, outs, index, parts, token):
+    wide = 4 * CHANNELS
+    heights = [4 * part.shape[0] for part in parts[::4]]
+    return pl.pallas_call(
+        kernel,
+        out_shape=outs,
+        in_specs=[pl.BlockSpec(memory_space=pltpu.SMEM)]
+        + [VM] * len(parts)
+        + [pl.BlockSpec(memory_space=pl.ANY)],
+        out_specs=[VM] * len(outs),
+        scratch_shapes=[pltpu.VMEM((height, wide), F32) for height in heights],
+        cost_estimate=pl.CostEstimate(
+            flops=200_000_000, bytes_accessed=3 << 20, transcendentals=0
+        ),
+        compiler_params=pltpu.CompilerParams(vmem_limit_bytes=VMEM_LIMIT),
+    )(index, *[near(part) for part in parts], token)
 
 
 TILES = 128
@@ -827,7 +854,11 @@
         )[0]
 
     def samples(spectrum):
-        return lax.all_gather(spectrum, "dp", axis=0, tiled=True)
+        size = 4
+        return [spectrum] + [
+            lax.ppermute(spectrum, "dp", [(i, i ^ k) for i in range(size)])
+            for k in range(1, size)
+        ]
 
     spread = lambda bias: jnp.broadcast_to(bias[:, None], (CHANNELS, LANES))
 
@@ -917,7 +948,7 @@
         third_adjoint,
         second_adj,
         big=[base, slope, values],
-        token=early,
+        token=early[1:],
     )[0]
     got = exchange(chunk)
     late = call(
@@ -929,36 +960,19 @@
         got,
         first_adj,
     )[0]
-    spectral_grad_two = call(
-        weight_two_kernel,
-        [],
-        [],
-        200_000_000,
-        3 << 20,
-        early,
-        plain=[jax.ShapeDtypeStruct(shape, BF16)],
-        token=late,
-    )[0]
+    index = lax.axis_index("dp").astype(jnp.int32).reshape(1)
+    weights = jax.ShapeDtypeStruct(shape, BF16)
+    spectral_grad_two = weight_call(weight_two_kernel, [weights], index, early, late)[0]
     late = samples(late)
     cells = lax.axis_size("dp") * lax.axis_size("space") * 2 * LANES * LANES
     square = jax.ShapeDtypeStruct((CHANNELS, CHANNELS), F32)
     line = jax.ShapeDtypeStruct((1, CHANNELS), F32)
-    spectral_grad_one, point_grad_one, point_grad_two, bias_grad_one, bias_grad_two = call(
+    spectral_grad_one, point_grad_one, point_grad_two, bias_grad_one, bias_grad_two = weight_call(
         functools.partial(weight_one_kernel, 1.0 / math.sqrt(cells)),
-        [],
-        [],
-        200_000_000,
-        3 << 20,
-        early,
-        late,
-        plain=[
-            jax.ShapeDtypeStruct(shape, BF16),
-            square,
-            square,
-            line,
-            line,
-        ],
-        token=spectral_grad_two,
+        [weights, square, square, line, line],
+        index,
+        early + late,
+        spectral_grad_two,
     )
     return (
         spectral_grad_one,

time: 224 us -> 222 us (level)
  blocking collectives: 53.7 us -> 35 us
  starting transfers between devices: 44.6 us -> 55.2 us
  local copies, waits for them, and re-layouts: 1.21 us -> 7.47 us
    all_gather x2 -> x0, blocking collectives: 18.9 us -> none  [samples(): return lax.all_gather(spectrum, 'dp', axis=0, tiled=True)]
    ppermute x0 -> x6, starting transfers between devices: none -> 10.6 us  [samples(): lax.ppermute(spectrum, 'dp', [(i, i ^ k) for i in range(size)])]
    unnamed x40 -> x62, local copies, waits for them, and re-layouts: 1.06 us -> 7.32 us
    pallas_call x13 -> x11, Pallas kernels: 74.2 us -> 69.4 us  [call(): pl.pallas_call(whole_kernel, out_shape=shapes + list(plain), in_specs=[VM...]
    pallas_call x0 -> x2, Pallas kernels: none -> 4.7 us  [weight_call(): pl.pallas_call(kernel, out_shape=outs, in_specs=[pl.BlockSpec(memory_spac...]
  transfers between devices with their start and end apart: 6 -> 12, of which waited for: 5 -> 5; matrix products, arithmetic and copies ran while one was open for 0% -> 0% of each run, Pallas kernels for 14% -> 15%
where the time goes in v4:
time: 222 us; the launch traced here: 221 us
  Pallas kernels  90.5 us (41%)
  starting transfers between devices  55.2 us (25%)
  blocking collectives  35 us (16%)
  waiting for transfers between devices  31.6 us (14%)
  local copies, waits for them, and re-layouts  7.47 us (3%)
    pallas_call x11, Pallas kernels, call(): pl.pallas_call(whole_kernel, out_shape=shapes + list(plain), in_specs=[VM...  69.4 us
    all_to_all x6, starting transfers between devices, exchange(): lax.all_to_all(chunk, 'space', split_axis=0, concat_axis=0, tiled=True)  44.6 us
    all_to_all x1, blocking collectives, exchange(): lax.all_to_all(chunk, 'space', split_axis=0, concat_axis=0, tiled=True)  35 us
    all_to_all x6, waiting for transfers between devices, exchange(): lax.all_to_all(chunk, 'space', split_axis=0, concat_axis=0, tiled=True)  31.6 us
    ppermute x6, starting transfers between devices, samples(): lax.ppermute(spectrum, 'dp', [(i, i ^ k) for i in range(size)])  10.6 us
    pallas_call x2, Pallas kernels, relay(): pl.pallas_call(relay_kernel, out_shape=pltpu.HBM((ROWS, LANES), BF16), in...  10.3 us
    unnamed x62, local copies, waits for them, and re-layouts  7.32 us
    pallas_call x1, Pallas kernels, first_partial(): pl.pallas_call(spectrum_kernel, out_shape=pltpu.HBM((512, LANES), BF16),...  6.14 us
  transfers between devices with their start and end apart: 12, of which 5 were waited for; matrix products, arithmetic and copies ran while one was open for 0% of the time, Pallas kernels for 15%

profile of v4, /device:TPU:1, one launch (start us, length us, event | category | flops | bytes accessed | tf_op | source)
XLA Modules:
  0.0 220.9 jit_solution(6302205205717853140)
XLA Ops:
  0.6 6.1 %shard_map.244._ = bf16[512,128]{1,0:T(8,128)(2,1)} custom-call(bf16[1,64,2,128,128]{4,3,2,1,0:T(8,128)(2,1)} %field.4, bf16[32,128]{1,0:T(8,128)(2,1)} %constant.25.clone.third_far.refs_3_, bf16[32,256]{1,0:T(8,128)(2,1)} %constant.24.clone.second_far), custom_call_target="tpu_custom_call" | custom-call | flops 600000000 | bytes 6291456 | tf_op jit(solution)/shard_map/pallas_call | solution.py:277
  6.8 15.1 %all-to-all-start = ((bf16[64,8,128]{2,1,0:T(8,128)(2,1)}), bf16[64,8,128]{2,1,0:T(8,128)(2,1)S(1)}, u32[]{:S(2)}, u32[]{:S(2)}) async-start(bf16[64,8,128]{2,1,0:T(8,128)(2,1)} %bitcast.29), calls=%async_computation | async-start | bytes 262144 | tf_op jit(solution)/shard_map/all_to_all | solution.py:840
  21.9 5.2 %shard_map.245.refs_4_.refs_2_.refs_7_ = bf16[16384,128]{1,0:T(8,128)(2,1)} custom-call(bf16[1,64,2,128,128]{4,3,2,1,0:T(8,128)(2,1)} %field.4, bf16[512,128]{1,0:T(8,128)(2,1)} %shard_map.244._), custom_call_target="tpu_custom_call" | custom-call | flops 600000000 | bytes 12582912 | tf_op jit(solution)/shard_map/pallas_call | solution.py:338
  27.2 5.9 %all-to-all-done = bf16[64,8,128]{2,1,0:T(8,128)(2,1)S(1)} async-done(((bf16[64,8,128]{2,1,0:T(8,128)(2,1)}), bf16[64,8,128]{2,1,0:T(8,128)(2,1)S(1)}, u32[]{:S(2)}, u32[]{:S(2)}) %all-to-all-start) | async-done | bytes 131104 | tf_op jit(solution)/shard_map/all_to_all | solution.py:840
  36.3 6.3 %all-to-all-start.1 = ((bf16[64,8,128]{2,1,0:T(8,128)(2,1)}), bf16[64,8,128]{2,1,0:T(8,128)(2,1)S(1)}, u32[]{:S(2)}, u32[]{:S(2)}) async-start(bf16[64,8,128]{2,1,0:T(8,128)(2,1)} %bitcast.32), calls=%async_computation.1 | async-start | bytes 262144 | tf_op jit(solution)/shard_map/all_to_all | solution.py:840
  42.8 4.0 %shard_map.247.refs_5_ = bf16[16384,128]{1,0:T(8,128)(2,1)} custom-call(bf16[64,64]{1,0:T(8,128)(2,1)S(1)} %bitcast.26, f32[64,128]{1,0:T(8,128)S(1)} %broadcast_in_dim.4.refs_1_, bf16[16384,128]{1,0:T(8,128)(2,1)} %shard_map.245.refs_4_.refs_2_.refs_7_, bf16[512,128]{1,0:T(8,128)(2,1)} %get-tuple-element.24.refs_3_), custom_call_target="tpu_custom_call" | custom-call | flops 500000000 | bytes 12582912 | tf_op jit(solution)/shard_map/pallas_call | solution.py:214
  46.8 7.1 %all-to-all-done.1 = bf16[64,8,128]{2,1,0:T(8,128)(2,1)S(1)} async-done(((bf16[64,8,128]{2,1,0:T(8,128)(2,1)}), bf16[64,8,128]{2,1,0:T(8,128)(2,1)S(1)}, u32[]{:S(2)}, u32[]{:S(2)}) %all-to-all-start.1) | async-done | bytes 131104 | tf_op jit(solution)/shard_map/all_to_all | solution.py:840
  53.9 9.1 %shard_map.248 = (bf16[512,128]{1,0:T(8,128)(2,1)}, bf16[16384,128]{1,0:T(8,128)(2,1)}, bf16[16384,128]{1,0:T(8,128)(2,1)}) custom-call(bf16[512,128]{1,0:T(8,128)(2,1)S(1)} %bitcast.23, bf16[128,64]{1,0:T(8,128)(2,1)S(1)} %copy-done.14, bf16[64,256]{1,0:T(8,128)(2,1)S(1)} %copy-done.19, bf16[32,128]{1,0:T(8,128)(2,1)S(1)} %copy-done.26, ...), custom_call_target="tpu_custom_call" | custom-call | flops 1000000000 | bytes 20971520 | tf_op jit(solution)/shard_map/pallas_call | solution.py:214
  63.0 5.2 %all-to-all-start.2 = ((bf16[64,8,128]{2,1,0:T(8,128)(2,1)}), bf16[64,8,128]{2,1,0:T(8,128)(2,1)S(1)}, u32[]{:S(2)}, u32[]{:S(2)}) async-start(bf16[64,8,128]{2,1,0:T(8,128)(2,1)} %bitcast.31), calls=%async_computation.2 | async-start | bytes 262144 | tf_op jit(solution)/shard_map/all_to_all | solution.py:840
  68.3 4.2 %shard_map.249.refs_4_.refs_5_ = bf16[16384,128]{1,0:T(8,128)(2,1)} custom-call(bf16[64,64]{1,0:T(8,128)(2,1)S(1)} %bitcast.27, f32[64,128]{1,0:T(8,128)S(1)} %broadcast_in_dim.5.refs_1_, bf16[16384,128]{1,0:T(8,128)(2,1)} %get-tuple-element.27.refs_2_.refs_1_, bf16[512,128]{1,0:T(8,128)(2,1)} %get-tuple-element.26.refs_3_), custom_call_target="tpu_custom_call" | custom-call | flops 500000000 | bytes 12582912 | tf_op jit(solution)/shard_map/pallas_call | solution.py:214
  72.5 7.0 %all-to-all-done.2 = bf16[64,8,128]{2,1,0:T(8,128)(2,1)S(1)} async-done(((bf16[64,8,128]{2,1,0:T(8,128)(2,1)}), bf16[64,8,128]{2,1,0:T(8,128)(2,1)S(1)}, u32[]{:S(2)}, u32[]{:S(2)}) %all-to-all-start.2) | async-done | bytes 131104 | tf_op jit(solution)/shard_map/all_to_all | solution.py:840
  82.6 5.4 %all-to-all-start.3 = ((bf16[64,8,128]{2,1,0:T(8,128)(2,1)}), bf16[64,8,128]{2,1,0:T(8,128)(2,1)S(1)}, u32[]{:S(2)}, u32[]{:S(2)}) async-start(bf16[64,8,128]{2,1,0:T(8,128)(2,1)} %bitcast.33), calls=%async_computation.3 | async-start | bytes 262144 | tf_op jit(solution)/shard_map/all_to_all | solution.py:840
  88.0 5.1 %shard_map.251.refs_6_ = bf16[16384,128]{1,0:T(8,128)(2,1)} custom-call(bf16[1,64,2,128,128]{4,3,2,1,0:T(8,128)(2,1)} %field.5, bf16[512,128]{1,0:T(8,128)(2,1)} %get-tuple-element.28._), custom_call_target="tpu_custom_call" | custom-call | flops 600000000 | bytes 12582912 | tf_op jit(solution)/shard_map/pallas_call | solution.py:338
  93.1 6.0 %all-to-all-done.3 = bf16[64,8,128]{2,1,0:T(8,128)(2,1)S(1)} async-done(((bf16[64,8,128]{2,1,0:T(8,128)(2,1)}), bf16[64,8,128]{2,1,0:T(8,128)(2,1)S(1)}, u32[]{:S(2)}, u32[]{:S(2)}) %all-to-all-start.3) | async-done | bytes 131104 | tf_op jit(solution)/shard_map/all_to_all | solution.py:840
  99.2 11.3 %shard_map.252 = (bf16[512,128]{1,0:T(8,128)(2,1)}, bf16[16384,128]{1,0:T(8,128)(2,1)}) custom-call(bf16[512,128]{1,0:T(8,128)(2,1)S(1)} %bitcast.21, bf16[128,64]{1,0:T(8,128)(2,1)S(1)} %copy-done.14, bf16[64,256]{1,0:T(8,128)(2,1)S(1)} %copy-done.19, bf16[32,128]{1,0:T(8,128)(2,1)S(1)} %copy-done.25, bf16[64,128]{1,0:T(8,128)(2,1)S(1)} %copy-done.18, ...), custom_call_target="tpu_custom_call" | custom-call | flops 1000000000 | bytes 20971520 | tf_op jit(solution)/shard_map/pallas_call | solution.py:214
  110.5 6.0 %all-to-all-start.4 = ((bf16[64,8,128]{2,1,0:T(8,128)(2,1)}), bf16[64,8,128]{2,1,0:T(8,128)(2,1)S(1)}, u32[]{:S(2)}, u32[]{:S(2)}) async-start(bf16[64,8,128]{2,1,0:T(8,128)(2,1)} %bitcast.34), calls=%async_computation.4 | async-start | bytes 262144 | tf_op jit(solution)/shard_map/all_to_all | solution.py:840
  116.5 5.7 %shard_map.253 = (f32[80,64]{1,0:T(8,128)}, bf16[16384,128]{1,0:T(8,128)(2,1)}) custom-call(bf16[64,64]{1,0:T(8,128)(2,1)S(1)} %copy-done.22, bf16[16384,128]{1,0:T(8,128)(2,1)} %get-tuple-element.27.refs_2_.refs_1_, bf16[16384,128]{1,0:T(8,128)(2,1)} %get-tuple-element.31.refs_2_), custom_call_target="tpu_custom_call" | custom-call | flops 1000000000 | bytes 12582912 | tf_op jit(solution)/shard_map/pallas_call | solution.py:214
  122.2 5.6 %all-to-all-done.4 = bf16[64,8,128]{2,1,0:T(8,128)(2,1)S(1)} async-done(((bf16[64,8,128]{2,1,0:T(8,128)(2,1)}), bf16[64,8,128]{2,1,0:T(8,128)(2,1)S(1)}, u32[]{:S(2)}, u32[]{:S(2)}) %all-to-all-start.4) | async-done | bytes 131104 | tf_op jit(solution)/shard_map/all_to_all | solution.py:840
  128.6 3.4 %shard_map.254 = (bf16[1024,128]{1,0:T(8,128)(2,1)}, bf16[96,256]{1,0:T(8,128)(2,1)}) custom-call(bf16[512,128]{1,0:T(8,128)(2,1)S(1)} %bitcast.22, bf16[2,16,4,64,64]{4,3,2,1,0:T(8,128)(2,1)S(1)} %copy-done, bf16[64,128]{1,0:T(8,128)(2,1)S(1)} %copy-done.16, bf16[128,64]{1,0:T(8,128)(2,1)S(1)} %copy-done.15, f32[80,64]{1,0:T(8,128)S(1)} %copy-done.23, ...), custom_call_target="tpu_custom_call" | custom-call | flops 200000000 | bytes 3145728 | tf_op jit(solution)/shard_map/pallas_call | solution.py:214
  132.0 6.7 %all-to-all-start.5 = ((bf16[64,16,128]{2,1,0:T(8,128)(2,1)}), bf16[64,16,128]{2,1,0:T(8,128)(2,1)S(1)}, u32[]{:S(2)}, u32[]{:S(2)}) async-start(bf16[64,16,128]{2,1,0:T(8,128)(2,1)} %bitcast.30), calls=%async_computation.5 | async-start | bytes 524288 | tf_op jit(solution)/shard_map/all_to_all | solution.py:840
  138.7 3.9 %collective-permute-start = (bf16[96,256]{1,0:T(8,128)(2,1)}, bf16[96,256]{1,0:T(8,128)(2,1)S(1)}, u32[]{:S(2)}, u32[]{:S(2)}) collective-permute-start(bf16[96,256]{1,0:T(8,128)(2,1)} %get-tuple-element.33.refs_0_), channel_id=1, source_target_pairs={{0,64},{64,0},{128,192},{192,128},{1,65},{65,1},{129,193},{193,129... | collective-permute-start | bytes 147464 | tf_op jit(solution)/shard_map/ppermute | solution.py:859
  144.3 7.3 %shard_map.255.refs_6_ = bf16[16384,128]{1,0:T(8,128)(2,1)} custom-call(bf16[16384,128]{1,0:T(8,128)(2,1)} %get-tuple-element.36.refs_0_, bf16[1024,128]{1,0:T(8,128)(2,1)} %get-tuple-element.34.refs_1_), custom_call_target="tpu_custom_call" | custom-call | flops 500000000 | bytes 12582912 | tf_op jit(solution)/shard_map/pallas_call | solution.py:214
  152.3 17.1 %shard_map.256 = bf16[3072,128]{1,0:T(8,128)(2,1)} custom-call(bf16[1024,128]{1,0:T(8,128)(2,1)S(1)} %bitcast.20, bf16[128,64]{1,0:T(8,128)(2,1)S(1)} %copy-done.14, bf16[64,256]{1,0:T(8,128)(2,1)S(1)} %copy-done.24, bf16[32,128]{1,0:T(8,128)(2,1)S(1)} %copy-done.25, bf16[64,128]{1,0:T(8,128)(2,1)S(1)} %copy-done.18, ...), custom_call_target="tpu_custom_call" | custom-call | flops 1500000000 | bytes 20971520 | tf_op jit(solution)/shard_map/pallas_call | solution.py:214
  169.4 35.0 %all_to_all.77 = bf16[64,48,128]{2,1,0:T(8,128)(2,1)S(1)} all-to-all(bf16[64,48,128]{2,1,0:T(8,128)(2,1)} %bitcast.28), channel_id=1, replica_groups=mesh['dp'=4,'space'=64] {'space'}, dimensions={0} | all-to-all | bytes 1572864 | tf_op jit(solution)/shard_map/all_to_all | solution.py:840
  (81 shorter events, 26.2 us)
Async XLA Ops:
  6.8 26.4 %all-to-all-start = ((bf16[64,8,128]{2,1,0:T(8,128)(2,1)}), bf16[64,8,128]{2,1,0:T(8,128)(2,1)S(1)}, u32[]{:S(2)}, u32[]{:S(2)}) async-start(bf16[64,8,128]{2,1,0:T(8,128)(2,1)} %bitcast.29), calls=%async_computation | async-start | bytes 262144 | tf_op jit(solution)/shard_map/all_to_all | solution.py:840
  21.9 11.2 %copy-start.2 = (bf16[2,16,4,64,64]{4,3,2,1,0:T(8,128)(2,1)S(1)}, bf16[2,16,4,64,64]{4,3,2,1,0:T(8,128)(2,1)}, u32[]{:S(2)}) copy-start(bf16[2,16,4,64,64]{4,3,2,1,0:T(8,128)(2,1)} %refs_1_.7) | copy-start | bytes 3145732
  21.9 11.2 %copy-start.15 = (bf16[128,64]{1,0:T(8,128)(2,1)S(1)}, bf16[128,64]{1,0:T(8,128)(2,1)}, u32[]{:S(2)}) copy-start(bf16[128,64]{1,0:T(8,128)(2,1)} %constant.32.clone.refs_3_) | copy-start | bytes 49156
  27.2 15.4 %copy-start.27 = (bf16[64,64]{1,0:T(8,128)(2,1)S(1)}, bf16[64,64]{1,0:T(8,128)(2,1)}, u32[]{:S(2)}) copy-start(bf16[64,64]{1,0:T(8,128)(2,1)} %param.25) | copy-start | bytes 24580
  27.2 15.5 %copy-start.28 = (f32[64]{0:T(128)S(1)}, f32[64]{0:T(128)}, u32[]{:S(2)}) copy-start(f32[64]{0:T(128)} %param.27) | copy-start | bytes 772
  36.3 17.6 %all-to-all-start.1 = ((bf16[64,8,128]{2,1,0:T(8,128)(2,1)}), bf16[64,8,128]{2,1,0:T(8,128)(2,1)S(1)}, u32[]{:S(2)}, u32[]{:S(2)}) async-start(bf16[64,8,128]{2,1,0:T(8,128)(2,1)} %bitcast.32), calls=%async_computation.1 | async-start | bytes 262144 | tf_op jit(solution)/shard_map/all_to_all | solution.py:840
  46.8 21.3 %copy-start.22 = (bf16[64,64]{1,0:T(8,128)(2,1)S(1)}, bf16[64,64]{1,0:T(8,128)(2,1)}, u32[]{:S(2)}) copy-start(bf16[64,64]{1,0:T(8,128)(2,1)} %refs_0_.1) | copy-start | bytes 24580
  46.8 21.4 %copy-start.29 = (f32[64]{0:T(128)S(1)}, f32[64]{0:T(128)}, u32[]{:S(2)}) copy-start(f32[64]{0:T(128)} %param.28) | copy-start | bytes 772
  63.0 16.5 %all-to-all-start.2 = ((bf16[64,8,128]{2,1,0:T(8,128)(2,1)}), bf16[64,8,128]{2,1,0:T(8,128)(2,1)S(1)}, u32[]{:S(2)}, u32[]{:S(2)}) async-start(bf16[64,8,128]{2,1,0:T(8,128)(2,1)} %bitcast.31), calls=%async_computation.2 | async-start | bytes 262144 | tf_op jit(solution)/shard_map/all_to_all | solution.py:840
  82.6 16.6 %all-to-all-start.3 = ((bf16[64,8,128]{2,1,0:T(8,128)(2,1)}), bf16[64,8,128]{2,1,0:T(8,128)(2,1)S(1)}, u32[]{:S(2)}, u32[]{:S(2)}) async-start(bf16[64,8,128]{2,1,0:T(8,128)(2,1)} %bitcast.33), calls=%async_computation.3 | async-start | bytes 262144 | tf_op jit(solution)/shard_map/all_to_all | solution.py:840
  110.5 17.3 %all-to-all-start.4 = ((bf16[64,8,128]{2,1,0:T(8,128)(2,1)}), bf16[64,8,128]{2,1,0:T(8,128)(2,1)S(1)}, u32[]{:S(2)}, u32[]{:S(2)}) async-start(bf16[64,8,128]{2,1,0:T(8,128)(2,1)} %bitcast.34), calls=%async_computation.4 | async-start | bytes 262144 | tf_op jit(solution)/shard_map/all_to_all | solution.py:840
  116.5 11.3 %copy-start.20 = (bf16[32,256]{1,0:T(8,128)(2,1)S(1)}, bf16[32,256]{1,0:T(8,128)(2,1)}, u32[]{:S(2)}) copy-start(bf16[32,256]{1,0:T(8,128)(2,1)} %get-tuple-element.25.refs_6_.refs_5_) | copy-start | bytes 49156
  116.5 11.3 %copy-start.21 = (bf16[32,256]{1,0:T(8,128)(2,1)S(1)}, bf16[32,256]{1,0:T(8,128)(2,1)}, u32[]{:S(2)}) copy-start(bf16[32,256]{1,0:T(8,128)(2,1)} %get-tuple-element.29.refs_7_.refs_6_) | copy-start | bytes 49156
  132.0 19.6 %all-to-all-start.5 = ((bf16[64,16,128]{2,1,0:T(8,128)(2,1)}), bf16[64,16,128]{2,1,0:T(8,128)(2,1)S(1)}, u32[]{:S(2)}, u32[]{:S(2)}) async-start(bf16[64,16,128]{2,1,0:T(8,128)(2,1)} %bitcast.30), calls=%async_computation.5 | async-start | bytes 524288 | tf_op jit(solution)/shard_map/all_to_all | solution.py:840
  138.7 12.9 %collective-permute-start = (bf16[96,256]{1,0:T(8,128)(2,1)}, bf16[96,256]{1,0:T(8,128)(2,1)S(1)}, u32[]{:S(2)}, u32[]{:S(2)}) collective-permute-start(bf16[96,256]{1,0:T(8,128)(2,1)} %get-tuple-element.33.refs_0_), channel_id=1, source_target_pairs={{0,64},{64,0},{128,192},{192,128},{1,65},{65,1},{129,193},{193,129... | collective-permute-start | bytes 147464 | tf_op jit(solution)/shard_map/ppermute | solution.py:859
  142.6 9.0 %collective-permute-start.1 = (bf16[96,256]{1,0:T(8,128)(2,1)}, bf16[96,256]{1,0:T(8,128)(2,1)S(1)}, u32[]{:S(2)}, u32[]{:S(2)}) collective-permute-start(bf16[96,256]{1,0:T(8,128)(2,1)} %get-tuple-element.33.refs_0_), channel_id=1, source_target_pairs={{0,128},{64,192},{128,0},{192,64},{1,129},{65,193},{129,1},{193,65... | collective-permute-start | bytes 147464 | tf_op jit(solution)/shard_map/ppermute | solution.py:859
  143.3 8.3 %collective-permute-start.2 = (bf16[96,256]{1,0:T(8,128)(2,1)}, bf16[96,256]{1,0:T(8,128)(2,1)S(1)}, u32[]{:S(2)}, u32[]{:S(2)}) collective-permute-start(bf16[96,256]{1,0:T(8,128)(2,1)} %get-tuple-element.33.refs_0_), channel_id=1, source_target_pairs={{0,192},{64,128},{128,64},{192,0},{1,193},{65,129},{129,65},{193,1... | collective-permute-start | bytes 147464 | tf_op jit(solution)/shard_map/ppermute | solution.py:859
  152.3 58.2 %copy-start.17 = (bf16[96,256]{1,0:T(8,128)(2,1)S(1)}, bf16[96,256]{1,0:T(8,128)(2,1)}, u32[]{:S(2)}) copy-start(bf16[96,256]{1,0:T(8,128)(2,1)} %get-tuple-element.33.refs_0_) | copy-start | bytes 147460
  169.4 46.7 %copy-start.7 = (bf16[96,256]{1,0:T(8,128)(2,1)S(1)}, bf16[96,256]{1,0:T(8,128)(2,1)}, u32[]{:S(2)}) copy-start(bf16[96,256]{1,0:T(8,128)(2,1)} %copy-done.5) | copy-start | bytes 147460
  169.4 46.7 %copy-start.10 = (bf16[96,256]{1,0:T(8,128)(2,1)S(1)}, bf16[96,256]{1,0:T(8,128)(2,1)}, u32[]{:S(2)}) copy-start(bf16[96,256]{1,0:T(8,128)(2,1)} %copy-done.8) | copy-start | bytes 147460
  169.4 46.7 %copy-start.13 = (bf16[96,256]{1,0:T(8,128)(2,1)S(1)}, bf16[96,256]{1,0:T(8,128)(2,1)}, u32[]{:S(2)}) copy-start(bf16[96,256]{1,0:T(8,128)(2,1)} %copy-done.11) | copy-start | bytes 147460
  205.5 10.6 %collective-permute-start.3 = (bf16[112,256]{1,0:T(8,128)(2,1)}, bf16[112,256]{1,0:T(8,128)(2,1)S(1)}, u32[]{:S(2)}, u32[]{:S(2)}) collective-permute-start(bf16[112,256]{1,0:T(8,128)(2,1)} %shard_map.257.refs_4_), channel_id=1, source_target_pairs={{0,64},{64,0},{128,192},{192,128},{1,65},{65,1},{129,193},{193,129... | collective-permute-start | bytes 172040 | tf_op jit(solution)/shard_map/ppermute | solution.py:859
  208.8 7.3 %collective-permute-start.4 = (bf16[112,256]{1,0:T(8,128)(2,1)}, bf16[112,256]{1,0:T(8,128)(2,1)S(1)}, u32[]{:S(2)}, u32[]{:S(2)}) collective-permute-start(bf16[112,256]{1,0:T(8,128)(2,1)} %shard_map.257.refs_4_), channel_id=1, source_target_pairs={{0,128},{64,192},{128,0},{192,64},{1,129},{65,193},{129,1},{193,65... | collective-permute-start | bytes 172040 | tf_op jit(solution)/shard_map/ppermute | solution.py:859
  210.2 5.9 %collective-permute-start.5 = (bf16[112,256]{1,0:T(8,128)(2,1)}, bf16[112,256]{1,0:T(8,128)(2,1)S(1)}, u32[]{:S(2)}, u32[]{:S(2)}) collective-permute-start(bf16[112,256]{1,0:T(8,128)(2,1)} %shard_map.257.refs_4_), channel_id=1, source_target_pairs={{0,192},{64,128},{128,64},{192,0},{1,193},{65,129},{129,65},{193,1... | collective-permute-start | bytes 172040 | tf_op jit(solution)/shard_map/ppermute | solution.py:859
  (18 other events, 94.4 us)

commit v5 on v4

--- a/solution.py
+++ b/solution.py
@@ -564,7 +564,7 @@
             flops=200_000_000, bytes_accessed=3 << 20, transcendentals=0
         ),
         compiler_params=pltpu.CompilerParams(vmem_limit_bytes=VMEM_LIMIT),
-    )(index, *[near(part) for part in parts], token)
+    )(index, *parts[:4], *[near(part) for part in parts[4:]], token)
 
 
 TILES = 128

time: 222 us -> 222 us (level)
  no operation moved by 1% of the time
where the time goes in v5:
time: 222 us; the launch traced here: 221 us
  Pallas kernels  90.5 us (41%)
  starting transfers between devices  55.2 us (25%)
  blocking collectives  35 us (16%)
  waiting for transfers between devices  31.6 us (14%)
  local copies, waits for them, and re-layouts  7.47 us (3%)
    pallas_call x11, Pallas kernels, call(): pl.pallas_call(whole_kernel, out_shape=shapes + list(plain), in_specs=[VM...  69.4 us
    all_to_all x6, starting transfers between devices, exchange(): lax.all_to_all(chunk, 'space', split_axis=0, concat_axis=0, tiled=True)  44.6 us
    all_to_all x1, blocking collectives, exchange(): lax.all_to_all(chunk, 'space', split_axis=0, concat_axis=0, tiled=True)  35 us
    all_to_all x6, waiting for transfers between devices, exchange(): lax.all_to_all(chunk, 'space', split_axis=0, concat_axis=0, tiled=True)  31.6 us
    ppermute x6, starting transfers between devices, samples(): lax.ppermute(spectrum, 'dp', [(i, i ^ k) for i in range(size)])  10.6 us
    pallas_call x2, Pallas kernels, relay(): pl.pallas_call(relay_kernel, out_shape=pltpu.HBM((ROWS, LANES), BF16), in...  10.3 us
    unnamed x62, local copies, waits for them, and re-layouts  7.32 us
    pallas_call x1, Pallas kernels, first_partial(): pl.pallas_call(spectrum_kernel, out_shape=pltpu.HBM((512, LANES), BF16),...  6.14 us
  transfers between devices with their start and end apart: 12, of which 5 were waited for; matrix products, arithmetic and copies ran while one was open for 0% of the time, Pallas kernels for 15%

profile of v5, /device:TPU:1, one launch (start us, length us, event | category | flops | bytes accessed | tf_op | source)
XLA Modules:
  0.0 220.9 jit_solution(6302205205717853140)
XLA Ops:
  0.6 6.1 %shard_map.244._ = bf16[512,128]{1,0:T(8,128)(2,1)} custom-call(bf16[1,64,2,128,128]{4,3,2,1,0:T(8,128)(2,1)} %field.4, bf16[32,128]{1,0:T(8,128)(2,1)} %constant.25.clone.third_far.refs_3_, bf16[32,256]{1,0:T(8,128)(2,1)} %constant.24.clone.second_far), custom_call_target="tpu_custom_call" | custom-call | flops 600000000 | bytes 6291456 | tf_op jit(solution)/shard_map/pallas_call | solution.py:277
  6.8 15.1 %all-to-all-start = ((bf16[64,8,128]{2,1,0:T(8,128)(2,1)}), bf16[64,8,128]{2,1,0:T(8,128)(2,1)S(1)}, u32[]{:S(2)}, u32[]{:S(2)}) async-start(bf16[64,8,128]{2,1,0:T(8,128)(2,1)} %bitcast.29), calls=%async_computation | async-start | bytes 262144 | tf_op jit(solution)/shard_map/all_to_all | solution.py:840
  21.9 5.2 %shard_map.245.refs_4_.refs_2_.refs_7_ = bf16[16384,128]{1,0:T(8,128)(2,1)} custom-call(bf16[1,64,2,128,128]{4,3,2,1,0:T(8,128)(2,1)} %field.4, bf16[512,128]{1,0:T(8,128)(2,1)} %shard_map.244._), custom_call_target="tpu_custom_call" | custom-call | flops 600000000 | bytes 12582912 | tf_op jit(solution)/shard_map/pallas_call | solution.py:338
  27.2 5.9 %all-to-all-done = bf16[64,8,128]{2,1,0:T(8,128)(2,1)S(1)} async-done(((bf16[64,8,128]{2,1,0:T(8,128)(2,1)}), bf16[64,8,128]{2,1,0:T(8,128)(2,1)S(1)}, u32[]{:S(2)}, u32[]{:S(2)}) %all-to-all-start) | async-done | bytes 131104 | tf_op jit(solution)/shard_map/all_to_all | solution.py:840
  36.3 6.3 %all-to-all-start.1 = ((bf16[64,8,128]{2,1,0:T(8,128)(2,1)}), bf16[64,8,128]{2,1,0:T(8,128)(2,1)S(1)}, u32[]{:S(2)}, u32[]{:S(2)}) async-start(bf16[64,8,128]{2,1,0:T(8,128)(2,1)} %bitcast.32), calls=%async_computation.1 | async-start | bytes 262144 | tf_op jit(solution)/shard_map/all_to_all | solution.py:840
  42.8 4.0 %shard_map.247.refs_5_ = bf16[16384,128]{1,0:T(8,128)(2,1)} custom-call(bf16[64,64]{1,0:T(8,128)(2,1)S(1)} %bitcast.26, f32[64,128]{1,0:T(8,128)S(1)} %broadcast_in_dim.4.refs_1_, bf16[16384,128]{1,0:T(8,128)(2,1)} %shard_map.245.refs_4_.refs_2_.refs_7_, bf16[512,128]{1,0:T(8,128)(2,1)} %get-tuple-element.24.refs_3_), custom_call_target="tpu_custom_call" | custom-call | flops 500000000 | bytes 12582912 | tf_op jit(solution)/shard_map/pallas_call | solution.py:214
  46.8 7.1 %all-to-all-done.1 = bf16[64,8,128]{2,1,0:T(8,128)(2,1)S(1)} async-done(((bf16[64,8,128]{2,1,0:T(8,128)(2,1)}), bf16[64,8,128]{2,1,0:T(8,128)(2,1)S(1)}, u32[]{:S(2)}, u32[]{:S(2)}) %all-to-all-start.1) | async-done | bytes 131104 | tf_op jit(solution)/shard_map/all_to_all | solution.py:840
  53.9 9.1 %shard_map.248 = (bf16[512,128]{1,0:T(8,128)(2,1)}, bf16[16384,128]{1,0:T(8,128)(2,1)}, bf16[16384,128]{1,0:T(8,128)(2,1)}) custom-call(bf16[512,128]{1,0:T(8,128)(2,1)S(1)} %bitcast.23, bf16[128,64]{1,0:T(8,128)(2,1)S(1)} %copy-done.14, bf16[64,256]{1,0:T(8,128)(2,1)S(1)} %copy-done.19, bf16[32,128]{1,0:T(8,128)(2,1)S(1)} %copy-done.26, ...), custom_call_target="tpu_custom_call" | custom-call | flops 1000000000 | bytes 20971520 | tf_op jit(solution)/shard_map/pallas_call | solution.py:214
  63.0 5.2 %all-to-all-start.2 = ((bf16[64,8,128]{2,1,0:T(8,128)(2,1)}), bf16[64,8,128]{2,1,0:T(8,128)(2,1)S(1)}, u32[]{:S(2)}, u32[]{:S(2)}) async-start(bf16[64,8,128]{2,1,0:T(8,128)(2,1)} %bitcast.31), calls=%async_computation.2 | async-start | bytes 262144 | tf_op jit(solution)/shard_map/all_to_all | solution.py:840
  68.3 4.2 %shard_map.249.refs_4_.refs_5_ = bf16[16384,128]{1,0:T(8,128)(2,1)} custom-call(bf16[64,64]{1,0:T(8,128)(2,1)S(1)} %bitcast.27, f32[64,128]{1,0:T(8,128)S(1)} %broadcast_in_dim.5.refs_1_, bf16[16384,128]{1,0:T(8,128)(2,1)} %get-tuple-element.27.refs_2_.refs_1_, bf16[512,128]{1,0:T(8,128)(2,1)} %get-tuple-element.26.refs_3_), custom_call_target="tpu_custom_call" | custom-call | flops 500000000 | bytes 12582912 | tf_op jit(solution)/shard_map/pallas_call | solution.py:214
  72.5 7.0 %all-to-all-done.2 = bf16[64,8,128]{2,1,0:T(8,128)(2,1)S(1)} async-done(((bf16[64,8,128]{2,1,0:T(8,128)(2,1)}), bf16[64,8,128]{2,1,0:T(8,128)(2,1)S(1)}, u32[]{:S(2)}, u32[]{:S(2)}) %all-to-all-start.2) | async-done | bytes 131104 | tf_op jit(solution)/shard_map/all_to_all | solution.py:840
  82.6 5.4 %all-to-all-start.3 = ((bf16[64,8,128]{2,1,0:T(8,128)(2,1)}), bf16[64,8,128]{2,1,0:T(8,128)(2,1)S(1)}, u32[]{:S(2)}, u32[]{:S(2)}) async-start(bf16[64,8,128]{2,1,0:T(8,128)(2,1)} %bitcast.33), calls=%async_computation.3 | async-start | bytes 262144 | tf_op jit(solution)/shard_map/all_to_all | solution.py:840
  88.0 5.1 %shard_map.251.refs_6_ = bf16[16384,128]{1,0:T(8,128)(2,1)} custom-call(bf16[1,64,2,128,128]{4,3,2,1,0:T(8,128)(2,1)} %field.5, bf16[512,128]{1,0:T(8,128)(2,1)} %get-tuple-element.28._), custom_call_target="tpu_custom_call" | custom-call | flops 600000000 | bytes 12582912 | tf_op jit(solution)/shard_map/pallas_call | solution.py:338
  93.1 6.0 %all-to-all-done.3 = bf16[64,8,128]{2,1,0:T(8,128)(2,1)S(1)} async-done(((bf16[64,8,128]{2,1,0:T(8,128)(2,1)}), bf16[64,8,128]{2,1,0:T(8,128)(2,1)S(1)}, u32[]{:S(2)}, u32[]{:S(2)}) %all-to-all-start.3) | async-done | bytes 131104 | tf_op jit(solution)/shard_map/all_to_all | solution.py:840
  99.2 11.3 %shard_map.252 = (bf16[512,128]{1,0:T(8,128)(2,1)}, bf16[16384,128]{1,0:T(8,128)(2,1)}) custom-call(bf16[512,128]{1,0:T(8,128)(2,1)S(1)} %bitcast.21, bf16[128,64]{1,0:T(8,128)(2,1)S(1)} %copy-done.14, bf16[64,256]{1,0:T(8,128)(2,1)S(1)} %copy-done.19, bf16[32,128]{1,0:T(8,128)(2,1)S(1)} %copy-done.25, bf16[64,128]{1,0:T(8,128)(2,1)S(1)} %copy-done.18, ...), custom_call_target="tpu_custom_call" | custom-call | flops 1000000000 | bytes 20971520 | tf_op jit(solution)/shard_map/pallas_call | solution.py:214
  110.5 6.0 %all-to-all-start.4 = ((bf16[64,8,128]{2,1,0:T(8,128)(2,1)}), bf16[64,8,128]{2,1,0:T(8,128)(2,1)S(1)}, u32[]{:S(2)}, u32[]{:S(2)}) async-start(bf16[64,8,128]{2,1,0:T(8,128)(2,1)} %bitcast.34), calls=%async_computation.4 | async-start | bytes 262144 | tf_op jit(solution)/shard_map/all_to_all | solution.py:840
  116.5 5.7 %shard_map.253 = (f32[80,64]{1,0:T(8,128)}, bf16[16384,128]{1,0:T(8,128)(2,1)}) custom-call(bf16[64,64]{1,0:T(8,128)(2,1)S(1)} %copy-done.22, bf16[16384,128]{1,0:T(8,128)(2,1)} %get-tuple-element.27.refs_2_.refs_1_, bf16[16384,128]{1,0:T(8,128)(2,1)} %get-tuple-element.31.refs_2_), custom_call_target="tpu_custom_call" | custom-call | flops 1000000000 | bytes 12582912 | tf_op jit(solution)/shard_map/pallas_call | solution.py:214
  122.2 5.6 %all-to-all-done.4 = bf16[64,8,128]{2,1,0:T(8,128)(2,1)S(1)} async-done(((bf16[64,8,128]{2,1,0:T(8,128)(2,1)}), bf16[64,8,128]{2,1,0:T(8,128)(2,1)S(1)}, u32[]{:S(2)}, u32[]{:S(2)}) %all-to-all-start.4) | async-done | bytes 131104 | tf_op jit(solution)/shard_map/all_to_all | solution.py:840
  128.6 3.4 %shard_map.254 = (bf16[1024,128]{1,0:T(8,128)(2,1)}, bf16[96,256]{1,0:T(8,128)(2,1)}) custom-call(bf16[512,128]{1,0:T(8,128)(2,1)S(1)} %bitcast.22, bf16[2,16,4,64,64]{4,3,2,1,0:T(8,128)(2,1)S(1)} %copy-done, bf16[64,128]{1,0:T(8,128)(2,1)S(1)} %copy-done.16, bf16[128,64]{1,0:T(8,128)(2,1)S(1)} %copy-done.15, f32[80,64]{1,0:T(8,128)S(1)} %copy-done.23, ...), custom_call_target="tpu_custom_call" | custom-call | flops 200000000 | bytes 3145728 | tf_op jit(solution)/shard_map/pallas_call | solution.py:214
  132.0 6.7 %all-to-all-start.5 = ((bf16[64,16,128]{2,1,0:T(8,128)(2,1)}), bf16[64,16,128]{2,1,0:T(8,128)(2,1)S(1)}, u32[]{:S(2)}, u32[]{:S(2)}) async-start(bf16[64,16,128]{2,1,0:T(8,128)(2,1)} %bitcast.30), calls=%async_computation.5 | async-start | bytes 524288 | tf_op jit(solution)/shard_map/all_to_all | solution.py:840
  138.7 3.9 %collective-permute-start = (bf16[96,256]{1,0:T(8,128)(2,1)}, bf16[96,256]{1,0:T(8,128)(2,1)S(1)}, u32[]{:S(2)}, u32[]{:S(2)}) collective-permute-start(bf16[96,256]{1,0:T(8,128)(2,1)} %get-tuple-element.33.refs_0_), channel_id=1, source_target_pairs={{0,64},{64,0},{128,192},{192,128},{1,65},{65,1},{129,193},{193,129... | collective-permute-start | bytes 147464 | tf_op jit(solution)/shard_map/ppermute | solution.py:859
  144.3 7.3 %shard_map.255.refs_6_ = bf16[16384,128]{1,0:T(8,128)(2,1)} custom-call(bf16[16384,128]{1,0:T(8,128)(2,1)} %get-tuple-element.36.refs_0_, bf16[1024,128]{1,0:T(8,128)(2,1)} %get-tuple-element.34.refs_1_), custom_call_target="tpu_custom_call" | custom-call | flops 500000000 | bytes 12582912 | tf_op jit(solution)/shard_map/pallas_call | solution.py:214
  152.3 17.1 %shard_map.256 = bf16[3072,128]{1,0:T(8,128)(2,1)} custom-call(bf16[1024,128]{1,0:T(8,128)(2,1)S(1)} %bitcast.20, bf16[128,64]{1,0:T(8,128)(2,1)S(1)} %copy-done.14, bf16[64,256]{1,0:T(8,128)(2,1)S(1)} %copy-done.24, bf16[32,128]{1,0:T(8,128)(2,1)S(1)} %copy-done.25, bf16[64,128]{1,0:T(8,128)(2,1)S(1)} %copy-done.18, ...), custom_call_target="tpu_custom_call" | custom-call | flops 1500000000 | bytes 20971520 | tf_op jit(solution)/shard_map/pallas_call | solution.py:214
  169.4 35.0 %all_to_all.77 = bf16[64,48,128]{2,1,0:T(8,128)(2,1)S(1)} all-to-all(bf16[64,48,128]{2,1,0:T(8,128)(2,1)} %bitcast.28), channel_id=1, replica_groups=mesh['dp'=4,'space'=64] {'space'}, dimensions={0} | all-to-all | bytes 1572864 | tf_op jit(solution)/shard_map/all_to_all | solution.py:840
  (81 shorter events, 26.2 us)
Async XLA Ops:
  6.8 26.4 %all-to-all-start = ((bf16[64,8,128]{2,1,0:T(8,128)(2,1)}), bf16[64,8,128]{2,1,0:T(8,128)(2,1)S(1)}, u32[]{:S(2)}, u32[]{:S(2)}) async-start(bf16[64,8,128]{2,1,0:T(8,128)(2,1)} %bitcast.29), calls=%async_computation | async-start | bytes 262144 | tf_op jit(solution)/shard_map/all_to_all | solution.py:840
  21.9 11.2 %copy-start.2 = (bf16[2,16,4,64,64]{4,3,2,1,0:T(8,128)(2,1)S(1)}, bf16[2,16,4,64,64]{4,3,2,1,0:T(8,128)(2,1)}, u32[]{:S(2)}) copy-start(bf16[2,16,4,64,64]{4,3,2,1,0:T(8,128)(2,1)} %refs_1_.7) | copy-start | bytes 3145732
  21.9 11.2 %copy-start.15 = (bf16[128,64]{1,0:T(8,128)(2,1)S(1)}, bf16[128,64]{1,0:T(8,128)(2,1)}, u32[]{:S(2)}) copy-start(bf16[128,64]{1,0:T(8,128)(2,1)} %constant.32.clone.refs_3_) | copy-start | bytes 49156
  27.2 15.4 %copy-start.27 = (bf16[64,64]{1,0:T(8,128)(2,1)S(1)}, bf16[64,64]{1,0:T(8,128)(2,1)}, u32[]{:S(2)}) copy-start(bf16[64,64]{1,0:T(8,128)(2,1)} %param.25) | copy-start | bytes 24580
  27.2 15.5 %copy-start.28 = (f32[64]{0:T(128)S(1)}, f32[64]{0:T(128)}, u32[]{:S(2)}) copy-start(f32[64]{0:T(128)} %param.27) | copy-start | bytes 772
  36.3 17.6 %all-to-all-start.1 = ((bf16[64,8,128]{2,1,0:T(8,128)(2,1)}), bf16[64,8,128]{2,1,0:T(8,128)(2,1)S(1)}, u32[]{:S(2)}, u32[]{:S(2)}) async-start(bf16[64,8,128]{2,1,0:T(8,128)(2,1)} %bitcast.32), calls=%async_computation.1 | async-start | bytes 262144 | tf_op jit(solution)/shard_map/all_to_all | solution.py:840
  46.8 21.3 %copy-start.22 = (bf16[64,64]{1,0:T(8,128)(2,1)S(1)}, bf16[64,64]{1,0:T(8,128)(2,1)}, u32[]{:S(2)}) copy-start(bf16[64,64]{1,0:T(8,128)(2,1)} %refs_0_.1) | copy-start | bytes 24580
  46.8 21.4 %copy-start.29 = (f32[64]{0:T(128)S(1)}, f32[64]{0:T(128)}, u32[]{:S(2)}) copy-start(f32[64]{0:T(128)} %param.28) | copy-start | bytes 772
  63.0 16.5 %all-to-all-start.2 = ((bf16[64,8,128]{2,1,0:T(8,128)(2,1)}), bf16[64,8,128]{2,1,0:T(8,128)(2,1)S(1)}, u32[]{:S(2)}, u32[]{:S(2)}) async-start(bf16[64,8,128]{2,1,0:T(8,128)(2,1)} %bitcast.31), calls=%async_computation.2 | async-start | bytes 262144 | tf_op jit(solution)/shard_map/all_to_all | solution.py:840
  82.6 16.6 %all-to-all-start.3 = ((bf16[64,8,128]{2,1,0:T(8,128)(2,1)}), bf16[64,8,128]{2,1,0:T(8,128)(2,1)S(1)}, u32[]{:S(2)}, u32[]{:S(2)}) async-start(bf16[64,8,128]{2,1,0:T(8,128)(2,1)} %bitcast.33), calls=%async_computation.3 | async-start | bytes 262144 | tf_op jit(solution)/shard_map/all_to_all | solution.py:840
  110.5 17.3 %all-to-all-start.4 = ((bf16[64,8,128]{2,1,0:T(8,128)(2,1)}), bf16[64,8,128]{2,1,0:T(8,128)(2,1)S(1)}, u32[]{:S(2)}, u32[]{:S(2)}) async-start(bf16[64,8,128]{2,1,0:T(8,128)(2,1)} %bitcast.34), calls=%async_computation.4 | async-start | bytes 262144 | tf_op jit(solution)/shard_map/all_to_all | solution.py:840
  116.5 11.3 %copy-start.20 = (bf16[32,256]{1,0:T(8,128)(2,1)S(1)}, bf16[32,256]{1,0:T(8,128)(2,1)}, u32[]{:S(2)}) copy-start(bf16[32,256]{1,0:T(8,128)(2,1)} %get-tuple-element.25.refs_6_.refs_5_) | copy-start | bytes 49156
  116.5 11.3 %copy-start.21 = (bf16[32,256]{1,0:T(8,128)(2,1)S(1)}, bf16[32,256]{1,0:T(8,128)(2,1)}, u32[]{:S(2)}) copy-start(bf16[32,256]{1,0:T(8,128)(2,1)} %get-tuple-element.29.refs_7_.refs_6_) | copy-start | bytes 49156
  132.0 19.6 %all-to-all-start.5 = ((bf16[64,16,128]{2,1,0:T(8,128)(2,1)}), bf16[64,16,128]{2,1,0:T(8,128)(2,1)S(1)}, u32[]{:S(2)}, u32[]{:S(2)}) async-start(bf16[64,16,128]{2,1,0:T(8,128)(2,1)} %bitcast.30), calls=%async_computation.5 | async-start | bytes 524288 | tf_op jit(solution)/shard_map/all_to_all | solution.py:840
  138.7 12.9 %collective-permute-start = (bf16[96,256]{1,0:T(8,128)(2,1)}, bf16[96,256]{1,0:T(8,128)(2,1)S(1)}, u32[]{:S(2)}, u32[]{:S(2)}) collective-permute-start(bf16[96,256]{1,0:T(8,128)(2,1)} %get-tuple-element.33.refs_0_), channel_id=1, source_target_pairs={{0,64},{64,0},{128,192},{192,128},{1,65},{65,1},{129,193},{193,129... | collective-permute-start | bytes 147464 | tf_op jit(solution)/shard_map/ppermute | solution.py:859
  142.6 9.0 %collective-permute-start.1 = (bf16[96,256]{1,0:T(8,128)(2,1)}, bf16[96,256]{1,0:T(8,128)(2,1)S(1)}, u32[]{:S(2)}, u32[]{:S(2)}) collective-permute-start(bf16[96,256]{1,0:T(8,128)(2,1)} %get-tuple-element.33.refs_0_), channel_id=1, source_target_pairs={{0,128},{64,192},{128,0},{192,64},{1,129},{65,193},{129,1},{193,65... | collective-permute-start | bytes 147464 | tf_op jit(solution)/shard_map/ppermute | solution.py:859
  143.3 8.3 %collective-permute-start.2 = (bf16[96,256]{1,0:T(8,128)(2,1)}, bf16[96,256]{1,0:T(8,128)(2,1)S(1)}, u32[]{:S(2)}, u32[]{:S(2)}) collective-permute-start(bf16[96,256]{1,0:T(8,128)(2,1)} %get-tuple-element.33.refs_0_), channel_id=1, source_target_pairs={{0,192},{64,128},{128,64},{192,0},{1,193},{65,129},{129,65},{193,1... | collective-permute-start | bytes 147464 | tf_op jit(solution)/shard_map/ppermute | solution.py:859
  152.3 58.2 %copy-start.17 = (bf16[96,256]{1,0:T(8,128)(2,1)S(1)}, bf16[96,256]{1,0:T(8,128)(2,1)}, u32[]{:S(2)}) copy-start(bf16[96,256]{1,0:T(8,128)(2,1)} %get-tuple-element.33.refs_0_) | copy-start | bytes 147460
  169.4 46.7 %copy-start.7 = (bf16[96,256]{1,0:T(8,128)(2,1)S(1)}, bf16[96,256]{1,0:T(8,128)(2,1)}, u32[]{:S(2)}) copy-start(bf16[96,256]{1,0:T(8,128)(2,1)} %copy-done.5) | copy-start | bytes 147460
  169.4 46.7 %copy-start.10 = (bf16[96,256]{1,0:T(8,128)(2,1)S(1)}, bf16[96,256]{1,0:T(8,128)(2,1)}, u32[]{:S(2)}) copy-start(bf16[96,256]{1,0:T(8,128)(2,1)} %copy-done.8) | copy-start | bytes 147460
  169.4 46.7 %copy-start.13 = (bf16[96,256]{1,0:T(8,128)(2,1)S(1)}, bf16[96,256]{1,0:T(8,128)(2,1)}, u32[]{:S(2)}) copy-start(bf16[96,256]{1,0:T(8,128)(2,1)} %copy-done.11) | copy-start | bytes 147460
  205.5 10.6 %collective-permute-start.3 = (bf16[112,256]{1,0:T(8,128)(2,1)}, bf16[112,256]{1,0:T(8,128)(2,1)S(1)}, u32[]{:S(2)}, u32[]{:S(2)}) collective-permute-start(bf16[112,256]{1,0:T(8,128)(2,1)} %shard_map.257.refs_4_), channel_id=1, source_target_pairs={{0,64},{64,0},{128,192},{192,128},{1,65},{65,1},{129,193},{193,129... | collective-permute-start | bytes 172040 | tf_op jit(solution)/shard_map/ppermute | solution.py:859
  208.8 7.3 %collective-permute-start.4 = (bf16[112,256]{1,0:T(8,128)(2,1)}, bf16[112,256]{1,0:T(8,128)(2,1)S(1)}, u32[]{:S(2)}, u32[]{:S(2)}) collective-permute-start(bf16[112,256]{1,0:T(8,128)(2,1)} %shard_map.257.refs_4_), channel_id=1, source_target_pairs={{0,128},{64,192},{128,0},{192,64},{1,129},{65,193},{129,1},{193,65... | collective-permute-start | bytes 172040 | tf_op jit(solution)/shard_map/ppermute | solution.py:859
  210.2 5.9 %collective-permute-start.5 = (bf16[112,256]{1,0:T(8,128)(2,1)}, bf16[112,256]{1,0:T(8,128)(2,1)S(1)}, u32[]{:S(2)}, u32[]{:S(2)}) collective-permute-start(bf16[112,256]{1,0:T(8,128)(2,1)} %shard_map.257.refs_4_), channel_id=1, source_target_pairs={{0,192},{64,128},{128,64},{192,0},{1,193},{65,129},{129,65},{193,1... | collective-permute-start | bytes 172040 | tf_op jit(solution)/shard_map/ppermute | solution.py:859
  (18 other events, 94.4 us)

commit v6 on v5

--- a/solution.py
+++ b/solution.py
@@ -515,27 +515,35 @@
     ).astype(F32)
 
 
-def in_order(index, parts, ordered):
+def in_order(index, parts, ordered, sems):
     rows = parts[0].shape[0]
+    copies = []
     for k, part in enumerate(parts):
         at = pl.multiple_of((index ^ k) * rows, 16)
-        ordered[pl.ds(at, rows), :] = part[...].astype(F32)
+        copies.append(pltpu.make_async_copy(part, ordered.at[pl.ds(at, rows)], sems.at[k]))
+    for copy in copies:
+        copy.start()
+    return copies
 
 
 def weight_two_kernel(index_ref, *refs):
-    early, _, out_ref, ordered = refs[:4], refs[4], refs[5], refs[6]
-    in_order(index_ref[0], early, ordered)
+    early, _, out_ref, ordered, sems = refs[:4], refs[4], refs[5], refs[6], refs[7]
+    for copy in in_order(index_ref[0], early, ordered, sems):
+        copy.wait()
     outer_products(rows_of(ordered, 96, 32), rows_of(ordered, 96, 64), out_ref)
 
 
 def weight_one_kernel(factor, index_ref, *refs):
     early, late = refs[:4], refs[4:8]
-    out_ref, one_ref, two_ref, bias_one_ref, bias_two_ref, early_all, late_all = refs[9:]
-    in_order(index_ref[0], early, early_all)
-    in_order(index_ref[0], late, late_all)
-    sums = late_all[32:112, :]
+    out_ref, one_ref, two_ref, bias_one_ref, bias_two_ref = refs[9:14]
+    early_all, late_all, early_sems, late_sems = refs[14:]
+    copies = in_order(index_ref[0], early, early_all, early_sems)
+    copies += in_order(index_ref[0], late, late_all, late_sems)
+    for copy in copies:
+        copy.wait()
+    sums = late_all[32:112, :].astype(F32)
     for n in range(1, 4):
-        sums = sums + late_all[n * 112 + 32 : (n + 1) * 112, :]
+        sums = sums + late_all[n * 112 + 32 : (n + 1) * 112, :].astype(F32)
     sums = sums * factor
     one = sums[:32, :LANES] + sums[:32, LANES:]
     one_ref[0:32, :] = one[:, :CHANNELS]
@@ -549,22 +557,24 @@
     outer_products(rows_of(early_all, 96, 0), rows_of(late_all, 112, 0), out_ref)
 
 
-def weight_call(kernel, outs, index, parts, token):
-    wide = 4 * CHANNELS
-    heights = [4 * part.shape[0] for part in parts[::4]]
+def weight_call(kernel, outs, index, early, late, token):
+    parts = [afar(part) for part in early + late[:1]] + [near(part) for part in late[1:]]
+    groups = [early, late] if late else [early]
+    far = pl.BlockSpec(memory_space=pl.ANY)
     return pl.pallas_call(
         kernel,
         out_shape=outs,
-        in_specs=[pl.BlockSpec(memory_space=pltpu.SMEM)]
-        + [VM] * len(parts)
-        + [pl.BlockSpec(memory_space=pl.ANY)],
+        in_specs=[pl.BlockSpec(memory_space=pltpu.SMEM)] + [far] * len(early + late[:1]) + [VM] * len(late[1:]) + [far],
         out_specs=[VM] * len(outs),
-        scratch_shapes=[pltpu.VMEM((height, wide), F32) for height in heights],
+        scratch_shapes=[
+            pltpu.VMEM((4 * group[0].shape[0], 4 * CHANNELS), BF16) for group in groups
+        ]
+        + [pltpu.SemaphoreType.DMA((4,)) for _ in groups],
         cost_estimate=pl.CostEstimate(
             flops=200_000_000, bytes_accessed=3 << 20, transcendentals=0
         ),
         compiler_params=pltpu.CompilerParams(vmem_limit_bytes=VMEM_LIMIT),
-    )(index, *parts[:4], *[near(part) for part in parts[4:]], token)
+    )(index, *parts, afar(token))
 
 
 TILES = 128
@@ -962,7 +972,7 @@
     )[0]
     index = lax.axis_index("dp").astype(jnp.int32).reshape(1)
     weights = jax.ShapeDtypeStruct(shape, BF16)
-    spectral_grad_two = weight_call(weight_two_kernel, [weights], index, early, late)[0]
+    spectral_grad_two = weight_call(weight_two_kernel, [weights], index, early, [], late)[0]
     late = samples(late)
     cells = lax.axis_size("dp") * lax.axis_size("space") * 2 * LANES * LANES
     square = jax.ShapeDtypeStruct((CHANNELS, CHANNELS), F32)
@@ -971,7 +981,8 @@
         functools.partial(weight_one_kernel, 1.0 / math.sqrt(cells)),
         [weights, square, square, line, line],
         index,
-        early + late,
+        early,
+        late,
         spectral_grad_two,
     )
     return (

time: 222 us -> 218 us (0.982)
  local copies, waits for them, and re-layouts: 7.47 us -> 1.8 us
    unnamed x62 -> x42, local copies, waits for them, and re-layouts: 7.32 us -> 1.66 us
  transfers between devices with their start and end apart: 12 -> 12, of which waited for: 5 -> 6; matrix products, arithmetic and copies ran while one was open for 0% -> 0% of each run, Pallas kernels for 15% -> 16%
where the time goes in v6:
time: 218 us
  Pallas kernels  92.4 us (42%)
  starting transfers between devices  55.3 us (25%)
  blocking collectives  34.8 us (16%)
  waiting for transfers between devices  32.2 us (15%)
    pallas_call x11, Pallas kernels, call(): pl.pallas_call(whole_kernel, out_shape=shapes + list(plain), in_specs=[VM...  69.4 us
    all_to_all x6, starting transfers between devices, exchange(): lax.all_to_all(chunk, 'space', split_axis=0, concat_axis=0, tiled=True)  44.7 us
    all_to_all x1, blocking collectives, exchange(): lax.all_to_all(chunk, 'space', split_axis=0, concat_axis=0, tiled=True)  34.8 us
    all_to_all x6, waiting for transfers between devices, exchange(): lax.all_to_all(chunk, 'space', split_axis=0, concat_axis=0, tiled=True)  31.5 us
    ppermute x6, starting transfers between devices, samples(): lax.ppermute(spectrum, 'dp', [(i, i ^ k) for i in range(size)])  10.6 us
    pallas_call x2, Pallas kernels, relay(): pl.pallas_call(relay_kernel, out_shape=pltpu.HBM((ROWS, LANES), BF16), in...  10.3 us
    pallas_call x2, Pallas kernels, weight_call(): pl.pallas_call(kernel, out_shape=outs, in_specs=[pl.BlockSpec(memory_spac...  6.53 us
    pallas_call x1, Pallas kernels, first_partial(): pl.pallas_call(spectrum_kernel, out_shape=pltpu.HBM((512, LANES), BF16),...  6.16 us
  transfers between devices with their start and end apart: 12, of which 6 were waited for; matrix products, arithmetic and copies ran while one was open for 0% of the time, Pallas kernels for 16%

profile of v6, /device:TPU:1, one launch (start us, length us, event | category | flops | bytes accessed | tf_op | source)
XLA Modules:
  0.0 217.7 jit_solution(4732249674467734037)
XLA Ops:
  0.6 6.2 %shard_map.244._ = bf16[512,128]{1,0:T(8,128)(2,1)} custom-call(bf16[1,64,2,128,128]{4,3,2,1,0:T(8,128)(2,1)} %field.4, bf16[32,128]{1,0:T(8,128)(2,1)} %constant.25.clone.third_far.refs_3_, bf16[32,256]{1,0:T(8,128)(2,1)} %constant.24.clone.second_far), custom_call_target="tpu_custom_call" | custom-call | flops 600000000 | bytes 6291456 | tf_op jit(solution)/shard_map/pallas_call | solution.py:277
  6.8 15.1 %all-to-all-start = ((bf16[64,8,128]{2,1,0:T(8,128)(2,1)}), bf16[64,8,128]{2,1,0:T(8,128)(2,1)S(1)}, u32[]{:S(2)}, u32[]{:S(2)}) async-start(bf16[64,8,128]{2,1,0:T(8,128)(2,1)} %bitcast.29), calls=%async_computation | async-start | bytes 262144 | tf_op jit(solution)/shard_map/all_to_all | solution.py:850
  22.0 5.2 %shard_map.245.refs_4_.refs_2_.refs_7_ = bf16[16384,128]{1,0:T(8,128)(2,1)} custom-call(bf16[1,64,2,128,128]{4,3,2,1,0:T(8,128)(2,1)} %field.4, bf16[512,128]{1,0:T(8,128)(2,1)} %shard_map.244._), custom_call_target="tpu_custom_call" | custom-call | flops 600000000 | bytes 12582912 | tf_op jit(solution)/shard_map/pallas_call | solution.py:338
  27.2 6.0 %all-to-all-done = bf16[64,8,128]{2,1,0:T(8,128)(2,1)S(1)} async-done(((bf16[64,8,128]{2,1,0:T(8,128)(2,1)}), bf16[64,8,128]{2,1,0:T(8,128)(2,1)S(1)}, u32[]{:S(2)}, u32[]{:S(2)}) %all-to-all-start) | async-done | bytes 131104 | tf_op jit(solution)/shard_map/all_to_all | solution.py:850
  36.3 6.3 %all-to-all-start.1 = ((bf16[64,8,128]{2,1,0:T(8,128)(2,1)}), bf16[64,8,128]{2,1,0:T(8,128)(2,1)S(1)}, u32[]{:S(2)}, u32[]{:S(2)}) async-start(bf16[64,8,128]{2,1,0:T(8,128)(2,1)} %bitcast.32), calls=%async_computation.1 | async-start | bytes 262144 | tf_op jit(solution)/shard_map/all_to_all | solution.py:850
  42.8 4.1 %shard_map.247.refs_5_ = bf16[16384,128]{1,0:T(8,128)(2,1)} custom-call(bf16[64,64]{1,0:T(8,128)(2,1)S(1)} %bitcast.26, f32[64,128]{1,0:T(8,128)S(1)} %broadcast_in_dim.4.refs_1_, bf16[16384,128]{1,0:T(8,128)(2,1)} %shard_map.245.refs_4_.refs_2_.refs_7_, bf16[512,128]{1,0:T(8,128)(2,1)} %get-tuple-element.24.refs_3_), custom_call_target="tpu_custom_call" | custom-call | flops 500000000 | bytes 12582912 | tf_op jit(solution)/shard_map/pallas_call | solution.py:214
  46.9 7.0 %all-to-all-done.1 = bf16[64,8,128]{2,1,0:T(8,128)(2,1)S(1)} async-done(((bf16[64,8,128]{2,1,0:T(8,128)(2,1)}), bf16[64,8,128]{2,1,0:T(8,128)(2,1)S(1)}, u32[]{:S(2)}, u32[]{:S(2)}) %all-to-all-start.1) | async-done | bytes 131104 | tf_op jit(solution)/shard_map/all_to_all | solution.py:850
  53.9 9.1 %shard_map.248 = (bf16[512,128]{1,0:T(8,128)(2,1)}, bf16[16384,128]{1,0:T(8,128)(2,1)}, bf16[16384,128]{1,0:T(8,128)(2,1)}) custom-call(bf16[512,128]{1,0:T(8,128)(2,1)S(1)} %bitcast.23, bf16[128,64]{1,0:T(8,128)(2,1)S(1)} %copy-done.2, bf16[64,256]{1,0:T(8,128)(2,1)S(1)} %copy-done.6, bf16[32,128]{1,0:T(8,128)(2,1)S(1)} %copy-done.13, ...), custom_call_target="tpu_custom_call" | custom-call | flops 1000000000 | bytes 20971520 | tf_op jit(solution)/shard_map/pallas_call | solution.py:214
  63.0 5.2 %all-to-all-start.2 = ((bf16[64,8,128]{2,1,0:T(8,128)(2,1)}), bf16[64,8,128]{2,1,0:T(8,128)(2,1)S(1)}, u32[]{:S(2)}, u32[]{:S(2)}) async-start(bf16[64,8,128]{2,1,0:T(8,128)(2,1)} %bitcast.31), calls=%async_computation.2 | async-start | bytes 262144 | tf_op jit(solution)/shard_map/all_to_all | solution.py:850
  68.4 4.2 %shard_map.249.refs_4_.refs_5_ = bf16[16384,128]{1,0:T(8,128)(2,1)} custom-call(bf16[64,64]{1,0:T(8,128)(2,1)S(1)} %bitcast.27, f32[64,128]{1,0:T(8,128)S(1)} %broadcast_in_dim.5.refs_1_, bf16[16384,128]{1,0:T(8,128)(2,1)} %get-tuple-element.27.refs_2_.refs_1_, bf16[512,128]{1,0:T(8,128)(2,1)} %get-tuple-element.26.refs_3_), custom_call_target="tpu_custom_call" | custom-call | flops 500000000 | bytes 12582912 | tf_op jit(solution)/shard_map/pallas_call | solution.py:214
  72.6 6.9 %all-to-all-done.2 = bf16[64,8,128]{2,1,0:T(8,128)(2,1)S(1)} async-done(((bf16[64,8,128]{2,1,0:T(8,128)(2,1)}), bf16[64,8,128]{2,1,0:T(8,128)(2,1)S(1)}, u32[]{:S(2)}, u32[]{:S(2)}) %all-to-all-start.2) | async-done | bytes 131104 | tf_op jit(solution)/shard_map/all_to_all | solution.py:850
  82.6 5.4 %all-to-all-start.3 = ((bf16[64,8,128]{2,1,0:T(8,128)(2,1)}), bf16[64,8,128]{2,1,0:T(8,128)(2,1)S(1)}, u32[]{:S(2)}, u32[]{:S(2)}) async-start(bf16[64,8,128]{2,1,0:T(8,128)(2,1)} %bitcast.33), calls=%async_computation.3 | async-start | bytes 262144 | tf_op jit(solution)/shard_map/all_to_all | solution.py:850
  88.1 5.1 %shard_map.251.refs_6_ = bf16[16384,128]{1,0:T(8,128)(2,1)} custom-call(bf16[1,64,2,128,128]{4,3,2,1,0:T(8,128)(2,1)} %field.5, bf16[512,128]{1,0:T(8,128)(2,1)} %get-tuple-element.28._), custom_call_target="tpu_custom_call" | custom-call | flops 600000000 | bytes 12582912 | tf_op jit(solution)/shard_map/pallas_call | solution.py:338
  93.2 6.0 %all-to-all-done.3 = bf16[64,8,128]{2,1,0:T(8,128)(2,1)S(1)} async-done(((bf16[64,8,128]{2,1,0:T(8,128)(2,1)}), bf16[64,8,128]{2,1,0:T(8,128)(2,1)S(1)}, u32[]{:S(2)}, u32[]{:S(2)}) %all-to-all-start.3) | async-done | bytes 131104 | tf_op jit(solution)/shard_map/all_to_all | solution.py:850
  99.2 11.3 %shard_map.252 = (bf16[512,128]{1,0:T(8,128)(2,1)}, bf16[16384,128]{1,0:T(8,128)(2,1)}) custom-call(bf16[512,128]{1,0:T(8,128)(2,1)S(1)} %bitcast.21, bf16[128,64]{1,0:T(8,128)(2,1)S(1)} %copy-done.2, bf16[64,256]{1,0:T(8,128)(2,1)S(1)} %copy-done.6, bf16[32,128]{1,0:T(8,128)(2,1)S(1)} %copy-done.12, bf16[64,128]{1,0:T(8,128)(2,1)S(1)} %copy-done.5, ...), custom_call_target="tpu_custom_call" | custom-call | flops 1000000000 | bytes 20971520 | tf_op jit(solution)/shard_map/pallas_call | solution.py:214
  110.6 6.0 %all-to-all-start.4 = ((bf16[64,8,128]{2,1,0:T(8,128)(2,1)}), bf16[64,8,128]{2,1,0:T(8,128)(2,1)S(1)}, u32[]{:S(2)}, u32[]{:S(2)}) async-start(bf16[64,8,128]{2,1,0:T(8,128)(2,1)} %bitcast.34), calls=%async_computation.4 | async-start | bytes 262144 | tf_op jit(solution)/shard_map/all_to_all | solution.py:850
  116.6 5.8 %shard_map.253 = (f32[80,64]{1,0:T(8,128)}, bf16[16384,128]{1,0:T(8,128)(2,1)}) custom-call(bf16[64,64]{1,0:T(8,128)(2,1)S(1)} %copy-done.9, bf16[16384,128]{1,0:T(8,128)(2,1)} %get-tuple-element.27.refs_2_.refs_1_, bf16[16384,128]{1,0:T(8,128)(2,1)} %get-tuple-element.31.refs_2_), custom_call_target="tpu_custom_call" | custom-call | flops 1000000000 | bytes 12582912 | tf_op jit(solution)/shard_map/pallas_call | solution.py:214
  122.4 5.5 %all-to-all-done.4 = bf16[64,8,128]{2,1,0:T(8,128)(2,1)S(1)} async-done(((bf16[64,8,128]{2,1,0:T(8,128)(2,1)}), bf16[64,8,128]{2,1,0:T(8,128)(2,1)S(1)}, u32[]{:S(2)}, u32[]{:S(2)}) %all-to-all-start.4) | async-done | bytes 131104 | tf_op jit(solution)/shard_map/all_to_all | solution.py:850
  128.7 3.4 %shard_map.254 = (bf16[1024,128]{1,0:T(8,128)(2,1)}, bf16[96,256]{1,0:T(8,128)(2,1)}) custom-call(bf16[512,128]{1,0:T(8,128)(2,1)S(1)} %bitcast.22, bf16[2,16,4,64,64]{4,3,2,1,0:T(8,128)(2,1)S(1)} %copy-done, bf16[64,128]{1,0:T(8,128)(2,1)S(1)} %copy-done.4, bf16[128,64]{1,0:T(8,128)(2,1)S(1)} %copy-done.3, f32[80,64]{1,0:T(8,128)S(1)} %copy-done.10, ...), custom_call_target="tpu_custom_call" | custom-call | flops 200000000 | bytes 3145728 | tf_op jit(solution)/shard_map/pallas_call | solution.py:214
  132.1 6.7 %all-to-all-start.5 = ((bf16[64,16,128]{2,1,0:T(8,128)(2,1)}), bf16[64,16,128]{2,1,0:T(8,128)(2,1)S(1)}, u32[]{:S(2)}, u32[]{:S(2)}) async-start(bf16[64,16,128]{2,1,0:T(8,128)(2,1)} %bitcast.30), calls=%async_computation.5 | async-start | bytes 524288 | tf_op jit(solution)/shard_map/all_to_all | solution.py:850
  138.8 3.8 %collective-permute-start = (bf16[96,256]{1,0:T(8,128)(2,1)}, bf16[96,256]{1,0:T(8,128)(2,1)S(1)}, u32[]{:S(2)}, u32[]{:S(2)}) collective-permute-start(bf16[96,256]{1,0:T(8,128)(2,1)} %get-tuple-element.33.refs_0_), channel_id=1, source_target_pairs={{0,64},{64,0},{128,192},{192,128},{1,65},{65,1},{129,193},{193,129... | collective-permute-start | bytes 147464 | tf_op jit(solution)/shard_map/ppermute | solution.py:869
  144.4 7.2 %shard_map.255.refs_6_ = bf16[16384,128]{1,0:T(8,128)(2,1)} custom-call(bf16[16384,128]{1,0:T(8,128)(2,1)} %get-tuple-element.36.refs_0_, bf16[1024,128]{1,0:T(8,128)(2,1)} %get-tuple-element.34.refs_1_), custom_call_target="tpu_custom_call" | custom-call | flops 500000000 | bytes 12582912 | tf_op jit(solution)/shard_map/pallas_call | solution.py:214
  152.3 17.1 %shard_map.256 = bf16[3072,128]{1,0:T(8,128)(2,1)} custom-call(bf16[1024,128]{1,0:T(8,128)(2,1)S(1)} %bitcast.20, bf16[128,64]{1,0:T(8,128)(2,1)S(1)} %copy-done.2, bf16[64,256]{1,0:T(8,128)(2,1)S(1)} %copy-done.11, bf16[32,128]{1,0:T(8,128)(2,1)S(1)} %copy-done.12, bf16[64,128]{1,0:T(8,128)(2,1)S(1)} %copy-done.5, ...), custom_call_target="tpu_custom_call" | custom-call | flops 1500000000 | bytes 20971520 | tf_op jit(solution)/shard_map/pallas_call | solution.py:214
  169.4 34.8 %all_to_all.77 = bf16[64,48,128]{2,1,0:T(8,128)(2,1)S(1)} all-to-all(bf16[64,48,128]{2,1,0:T(8,128)(2,1)} %bitcast.28), channel_id=1, replica_groups=mesh['dp'=4,'space'=64] {'space'}, dimensions={0} | all-to-all | bytes 1572864 | tf_op jit(solution)/shard_map/all_to_all | solution.py:850
  (61 shorter events, 23.0 us)
Async XLA Ops:
  6.8 26.4 %all-to-all-start = ((bf16[64,8,128]{2,1,0:T(8,128)(2,1)}), bf16[64,8,128]{2,1,0:T(8,128)(2,1)S(1)}, u32[]{:S(2)}, u32[]{:S(2)}) async-start(bf16[64,8,128]{2,1,0:T(8,128)(2,1)} %bitcast.29), calls=%async_computation | async-start | bytes 262144 | tf_op jit(solution)/shard_map/all_to_all | solution.py:850
  21.9 11.2 %copy-start.1 = (bf16[2,16,4,64,64]{4,3,2,1,0:T(8,128)(2,1)S(1)}, bf16[2,16,4,64,64]{4,3,2,1,0:T(8,128)(2,1)}, u32[]{:S(2)}) copy-start(bf16[2,16,4,64,64]{4,3,2,1,0:T(8,128)(2,1)} %refs_1_.7) | copy-start | bytes 3145732
  21.9 11.2 %copy-start.3 = (bf16[128,64]{1,0:T(8,128)(2,1)S(1)}, bf16[128,64]{1,0:T(8,128)(2,1)}, u32[]{:S(2)}) copy-start(bf16[128,64]{1,0:T(8,128)(2,1)} %constant.32.clone.refs_3_) | copy-start | bytes 49156
  22.0 11.2 %copy-start.4 = (bf16[64,128]{1,0:T(8,128)(2,1)S(1)}, bf16[64,128]{1,0:T(8,128)(2,1)}, u32[]{:S(2)}) copy-start(bf16[64,128]{1,0:T(8,128)(2,1)} %constant.31.clone.refs_2_.refs_1_) | copy-start | bytes 49156
  27.2 15.4 %copy-start.17 = (bf16[64,64]{1,0:T(8,128)(2,1)S(1)}, bf16[64,64]{1,0:T(8,128)(2,1)}, u32[]{:S(2)}) copy-start(bf16[64,64]{1,0:T(8,128)(2,1)} %param.25) | copy-start | bytes 24580
  27.2 15.5 %copy-start.18 = (f32[64]{0:T(128)S(1)}, f32[64]{0:T(128)}, u32[]{:S(2)}) copy-start(f32[64]{0:T(128)} %param.27) | copy-start | bytes 772
  36.3 17.6 %all-to-all-start.1 = ((bf16[64,8,128]{2,1,0:T(8,128)(2,1)}), bf16[64,8,128]{2,1,0:T(8,128)(2,1)S(1)}, u32[]{:S(2)}, u32[]{:S(2)}) async-start(bf16[64,8,128]{2,1,0:T(8,128)(2,1)} %bitcast.32), calls=%async_computation.1 | async-start | bytes 262144 | tf_op jit(solution)/shard_map/all_to_all | solution.py:850
  42.7 11.2 %copy-start.2 = (bf16[128,64]{1,0:T(8,128)(2,1)S(1)}, bf16[128,64]{1,0:T(8,128)(2,1)}, u32[]{:S(2)}) copy-start(bf16[128,64]{1,0:T(8,128)(2,1)} %constant.30.clone.refs_1_) | copy-start | bytes 49156
  42.7 11.2 %copy-start.5 = (bf16[64,128]{1,0:T(8,128)(2,1)S(1)}, bf16[64,128]{1,0:T(8,128)(2,1)}, u32[]{:S(2)}) copy-start(bf16[64,128]{1,0:T(8,128)(2,1)} %constant.29.clone.refs_4_) | copy-start | bytes 49156
  42.7 11.2 %copy-start.6 = (bf16[64,256]{1,0:T(8,128)(2,1)S(1)}, bf16[64,256]{1,0:T(8,128)(2,1)}, u32[]{:S(2)}) copy-start(bf16[64,256]{1,0:T(8,128)(2,1)} %constant.27.clone.refs_2_) | copy-start | bytes 98308
  46.9 21.4 %copy-start.9 = (bf16[64,64]{1,0:T(8,128)(2,1)S(1)}, bf16[64,64]{1,0:T(8,128)(2,1)}, u32[]{:S(2)}) copy-start(bf16[64,64]{1,0:T(8,128)(2,1)} %refs_0_.1) | copy-start | bytes 24580
  46.9 21.4 %copy-start.19 = (f32[64]{0:T(128)S(1)}, f32[64]{0:T(128)}, u32[]{:S(2)}) copy-start(f32[64]{0:T(128)} %param.28) | copy-start | bytes 772
  63.0 16.5 %all-to-all-start.2 = ((bf16[64,8,128]{2,1,0:T(8,128)(2,1)}), bf16[64,8,128]{2,1,0:T(8,128)(2,1)S(1)}, u32[]{:S(2)}, u32[]{:S(2)}) async-start(bf16[64,8,128]{2,1,0:T(8,128)(2,1)} %bitcast.31), calls=%async_computation.2 | async-start | bytes 262144 | tf_op jit(solution)/shard_map/all_to_all | solution.py:850
  82.6 16.6 %all-to-all-start.3 = ((bf16[64,8,128]{2,1,0:T(8,128)(2,1)}), bf16[64,8,128]{2,1,0:T(8,128)(2,1)S(1)}, u32[]{:S(2)}, u32[]{:S(2)}) async-start(bf16[64,8,128]{2,1,0:T(8,128)(2,1)} %bitcast.33), calls=%async_computation.3 | async-start | bytes 262144 | tf_op jit(solution)/shard_map/all_to_all | solution.py:850
  110.6 17.4 %all-to-all-start.4 = ((bf16[64,8,128]{2,1,0:T(8,128)(2,1)}), bf16[64,8,128]{2,1,0:T(8,128)(2,1)S(1)}, u32[]{:S(2)}, u32[]{:S(2)}) async-start(bf16[64,8,128]{2,1,0:T(8,128)(2,1)} %bitcast.34), calls=%async_computation.4 | async-start | bytes 262144 | tf_op jit(solution)/shard_map/all_to_all | solution.py:850
  116.6 11.3 %copy-start.7 = (bf16[32,256]{1,0:T(8,128)(2,1)S(1)}, bf16[32,256]{1,0:T(8,128)(2,1)}, u32[]{:S(2)}) copy-start(bf16[32,256]{1,0:T(8,128)(2,1)} %get-tuple-element.25.refs_6_.refs_5_) | copy-start | bytes 49156
  116.6 11.3 %copy-start.8 = (bf16[32,256]{1,0:T(8,128)(2,1)S(1)}, bf16[32,256]{1,0:T(8,128)(2,1)}, u32[]{:S(2)}) copy-start(bf16[32,256]{1,0:T(8,128)(2,1)} %get-tuple-element.29.refs_7_.refs_6_) | copy-start | bytes 49156
  132.1 19.5 %all-to-all-start.5 = ((bf16[64,16,128]{2,1,0:T(8,128)(2,1)}), bf16[64,16,128]{2,1,0:T(8,128)(2,1)S(1)}, u32[]{:S(2)}, u32[]{:S(2)}) async-start(bf16[64,16,128]{2,1,0:T(8,128)(2,1)} %bitcast.30), calls=%async_computation.5 | async-start | bytes 524288 | tf_op jit(solution)/shard_map/all_to_all | solution.py:850
  138.8 12.8 %collective-permute-start = (bf16[96,256]{1,0:T(8,128)(2,1)}, bf16[96,256]{1,0:T(8,128)(2,1)S(1)}, u32[]{:S(2)}, u32[]{:S(2)}) collective-permute-start(bf16[96,256]{1,0:T(8,128)(2,1)} %get-tuple-element.33.refs_0_), channel_id=1, source_target_pairs={{0,64},{64,0},{128,192},{192,128},{1,65},{65,1},{129,193},{193,129... | collective-permute-start | bytes 147464 | tf_op jit(solution)/shard_map/ppermute | solution.py:869
  142.7 9.0 %collective-permute-start.1 = (bf16[96,256]{1,0:T(8,128)(2,1)}, bf16[96,256]{1,0:T(8,128)(2,1)S(1)}, u32[]{:S(2)}, u32[]{:S(2)}) collective-permute-start(bf16[96,256]{1,0:T(8,128)(2,1)} %get-tuple-element.33.refs_0_), channel_id=1, source_target_pairs={{0,128},{64,192},{128,0},{192,64},{1,129},{65,193},{129,1},{193,65... | collective-permute-start | bytes 147464 | tf_op jit(solution)/shard_map/ppermute | solution.py:869
  143.5 8.2 %collective-permute-start.2 = (bf16[96,256]{1,0:T(8,128)(2,1)}, bf16[96,256]{1,0:T(8,128)(2,1)S(1)}, u32[]{:S(2)}, u32[]{:S(2)}) collective-permute-start(bf16[96,256]{1,0:T(8,128)(2,1)} %get-tuple-element.33.refs_0_), channel_id=1, source_target_pairs={{0,192},{64,128},{128,64},{192,0},{1,193},{65,129},{129,65},{193,1... | collective-permute-start | bytes 147464 | tf_op jit(solution)/shard_map/ppermute | solution.py:869
  205.3 8.2 %collective-permute-start.3 = (bf16[112,256]{1,0:T(8,128)(2,1)}, bf16[112,256]{1,0:T(8,128)(2,1)S(1)}, u32[]{:S(2)}, u32[]{:S(2)}) collective-permute-start(bf16[112,256]{1,0:T(8,128)(2,1)} %shard_map.257.refs_4_), channel_id=1, source_target_pairs={{0,64},{64,0},{128,192},{192,128},{1,65},{65,1},{129,193},{193,129... | collective-permute-start | bytes 172040 | tf_op jit(solution)/shard_map/ppermute | solution.py:869
  208.6 5.0 %collective-permute-start.4 = (bf16[112,256]{1,0:T(8,128)(2,1)}, bf16[112,256]{1,0:T(8,128)(2,1)S(1)}, u32[]{:S(2)}, u32[]{:S(2)}) collective-permute-start(bf16[112,256]{1,0:T(8,128)(2,1)} %shard_map.257.refs_4_), channel_id=1, source_target_pairs={{0,128},{64,192},{128,0},{192,64},{1,129},{65,193},{129,1},{193,65... | collective-permute-start | bytes 172040 | tf_op jit(solution)/shard_map/ppermute | solution.py:869
  210.1 4.1 %collective-permute-start.5 = (bf16[112,256]{1,0:T(8,128)(2,1)}, bf16[112,256]{1,0:T(8,128)(2,1)S(1)}, u32[]{:S(2)}, u32[]{:S(2)}) collective-permute-start(bf16[112,256]{1,0:T(8,128)(2,1)} %shard_map.257.refs_4_), channel_id=1, source_target_pairs={{0,192},{64,128},{128,64},{192,0},{1,193},{65,129},{129,65},{193,1... | collective-permute-start | bytes 172040 | tf_op jit(solution)/shard_map/ppermute | solution.py:869
  (8 other events, 44.0 us)

commit v7 on v6

--- a/solution.py
+++ b/solution.py
@@ -133,7 +133,7 @@
 
 
 def call(
-    kernel, outs, scratch, flops, moved, *operands, big=(), kinds=(), plain=(), token=None
+    kernel, outs, scratch, flops, moved, *operands, big=(), kinds=(), plain=(), token=None, reach=False
 ):
     cut = ROWS // GROUPS
     extra = [] if token is None else list(token) if isinstance(token, list) else [token]
@@ -157,7 +157,7 @@
         for count in counts:
             parts.append(refs[at : at + count])
             at += count
-        small, big_far, _, outs_far, kinds_far, plains, own, outs_near, big_near, kinds_near, sems = parts
+        small, big_far, tokens, outs_far, kinds_far, plains, own, outs_near, big_near, kinds_near, sems = parts
         in_sem, out_sem, end_sem = sems
 
         def group_of(far, close, sem, index, group, out):
@@ -194,7 +194,7 @@
 
             return lax.fori_loop(0, GROUPS, each, carry)
 
-        kernel(small, big_near, outs_near, kinds_near, plains, own, loop)
+        kernel(small + tokens if reach else small, big_near, outs_near, kinds_near, plains, own, loop)
         last = [
             pltpu.make_async_copy(close, far, end_sem.at[index])
             for index, (close, far) in enumerate(zip(outs_near, outs_far))
@@ -408,9 +408,11 @@
 
 
 def unmix_kernel(small, _, outs, __, ___, scratch, loop):
-    got_ref, weight_ref, forward_ref, inverse_ref, term_ref, one_ref, two_ref = small
+    got_ref, weight_ref, forward_ref, inverse_ref, one_ref, two_ref, term_far = small
     out_ref, spec_ref = outs
-    wide, sent = scratch
+    wide, sent, term_ref, term_sem = scratch
+    fetch = pltpu.make_async_copy(term_far, term_ref, term_sem.at[0])
+    fetch.start()
     wide[...] = got_ref[...].astype(F32)
     forward = forward_ref[...]
     inverse = inverse_ref[...]
@@ -419,11 +421,6 @@
     spec_ref[0:32, :] = one_ref[...]
     spec_ref[32:64, :] = two_ref[...]
     sent[...] = jnp.zeros_like(sent)
-    terms = high_low(term_ref[...])
-    sent[pl.ds(8, 64, stride=16), :] = terms[:CHANNELS]
-    sent[pl.ds(9, 64, stride=16), :] = jnp.broadcast_to(
-        terms[CHANNELS : CHANNELS + 1], (CHANNELS, LANES)
-    )
     for p in range(4):
         spec = own_spectrum(wide, forward, p).astype(BF16)
         spec_ref[64:96, p * CHANNELS : (p + 1) * CHANNELS] = spec
@@ -437,6 +434,12 @@
             total = total + jnp.where(row == 2 * pair + half, piece, 0.0)
         mixed = (total + turned(total))[:, :CHANNELS].astype(BF16).astype(F32)
         send_field(mixed, inverse, p, sent, 16)
+    fetch.wait()
+    terms = high_low(term_ref[...])
+    sent[pl.ds(8, 64, stride=16), :] = terms[:CHANNELS]
+    sent[pl.ds(9, 64, stride=16), :] = jnp.broadcast_to(
+        terms[CHANNELS : CHANNELS + 1], (CHANNELS, LANES)
+    )
     out_ref[...] = sent[...].astype(BF16)
 
 
@@ -751,9 +754,8 @@
         axis=0,
     )
     for d in range(64):
-        sent[d * 48 + 8 : (d + 1) * 48, :] = terms
-    for d in range(64):
-        out[d * 48 : (d + 1) * 48, :] = sent[d * 48 : (d + 1) * 48, :].astype(BF16)
+        block = jnp.concatenate([sent[d * 48 : d * 48 + 8, :], terms], axis=0)
+        out[d * 48 : (d + 1) * 48, :] = block.astype(BF16)
 
 
 def planes(kernel, kinds, *operands, big, token):
@@ -924,16 +926,22 @@
     chunk, early = call(
         unmix_kernel,
         [((1024, LANES), BF16), ((96, 4 * CHANNELS), BF16)],
-        [WIDE, pltpu.VMEM((1024, LANES), F32)],
+        [
+            WIDE,
+            pltpu.VMEM((1024, LANES), F32),
+            pltpu.VMEM((CHANNELS + 16, CHANNELS), F32),
+            pltpu.SemaphoreType.DMA((1,)),
+        ],
         200_000_000,
         3 << 20,
         got,
         spectral_two,
         first_adj,
         first_back,
-        term_two,
         spec_one,
         spec_two,
+        token=term_two,
+        reach=True,
     )
     got = exchange(chunk)
     early = samples(early)

time: 218 us -> 218 us (level)
  no operation moved by 1% of the time
where the time goes in v7:
time: 218 us; the launch traced here: 217 us
  Pallas kernels  92.4 us (42%)
  starting transfers between devices  55.3 us (25%)
  blocking collectives  34.8 us (16%)
  waiting for transfers between devices  32.2 us (15%)
    pallas_call x11, Pallas kernels, call(): pl.pallas_call(whole_kernel, out_shape=shapes + list(plain), in_specs=[VM...  69.5 us
    all_to_all x6, starting transfers between devices, exchange(): lax.all_to_all(chunk, 'space', split_axis=0, concat_axis=0, tiled=True)  44.7 us
    all_to_all x1, blocking collectives, exchange(): lax.all_to_all(chunk, 'space', split_axis=0, concat_axis=0, tiled=True)  34.8 us
    all_to_all x6, waiting for transfers between devices, exchange(): lax.all_to_all(chunk, 'space', split_axis=0, concat_axis=0, tiled=True)  31.5 us
    ppermute x6, starting transfers between devices, samples(): lax.ppermute(spectrum, 'dp', [(i, i ^ k) for i in range(size)])  10.6 us
    pallas_call x2, Pallas kernels, relay(): pl.pallas_call(relay_kernel, out_shape=pltpu.HBM((ROWS, LANES), BF16), in...  10.3 us
    pallas_call x2, Pallas kernels, weight_call(): pl.pallas_call(kernel, out_shape=outs, in_specs=[pl.BlockSpec(memory_spac...  6.53 us
    pallas_call x1, Pallas kernels, first_partial(): pl.pallas_call(spectrum_kernel, out_shape=pltpu.HBM((512, LANES), BF16),...  6.14 us
  transfers between devices with their start and end apart: 12, of which 6 were waited for; matrix products, arithmetic and copies ran while one was open for 0% of the time, Pallas kernels for 16%

profile of v7, /device:TPU:1, one launch (start us, length us, event | category | flops | bytes accessed | tf_op | source)
XLA Modules:
  0.0 216.9 jit_solution(18074596774905066248)
XLA Ops:
  0.6 6.1 %shard_map.244._ = bf16[512,128]{1,0:T(8,128)(2,1)} custom-call(bf16[1,64,2,128,128]{4,3,2,1,0:T(8,128)(2,1)} %field.4, bf16[32,128]{1,0:T(8,128)(2,1)} %constant.25.clone.third_far.refs_3_, bf16[32,256]{1,0:T(8,128)(2,1)} %constant.24.clone.second_far), custom_call_target="tpu_custom_call" | custom-call | flops 600000000 | bytes 6291456 | tf_op jit(solution)/shard_map/pallas_call | solution.py:277
  6.8 15.1 %all-to-all-start = ((bf16[64,8,128]{2,1,0:T(8,128)(2,1)}), bf16[64,8,128]{2,1,0:T(8,128)(2,1)S(1)}, u32[]{:S(2)}, u32[]{:S(2)}) async-start(bf16[64,8,128]{2,1,0:T(8,128)(2,1)} %bitcast.29), calls=%async_computation | async-start | bytes 262144 | tf_op jit(solution)/shard_map/all_to_all | solution.py:852
  21.9 5.2 %shard_map.245.refs_4_.refs_2_.refs_7_ = bf16[16384,128]{1,0:T(8,128)(2,1)} custom-call(bf16[1,64,2,128,128]{4,3,2,1,0:T(8,128)(2,1)} %field.4, bf16[512,128]{1,0:T(8,128)(2,1)} %shard_map.244._), custom_call_target="tpu_custom_call" | custom-call | flops 600000000 | bytes 12582912 | tf_op jit(solution)/shard_map/pallas_call | solution.py:338
  27.2 6.0 %all-to-all-done = bf16[64,8,128]{2,1,0:T(8,128)(2,1)S(1)} async-done(((bf16[64,8,128]{2,1,0:T(8,128)(2,1)}), bf16[64,8,128]{2,1,0:T(8,128)(2,1)S(1)}, u32[]{:S(2)}, u32[]{:S(2)}) %all-to-all-start) | async-done | bytes 131104 | tf_op jit(solution)/shard_map/all_to_all | solution.py:852
  36.3 6.3 %all-to-all-start.1 = ((bf16[64,8,128]{2,1,0:T(8,128)(2,1)}), bf16[64,8,128]{2,1,0:T(8,128)(2,1)S(1)}, u32[]{:S(2)}, u32[]{:S(2)}) async-start(bf16[64,8,128]{2,1,0:T(8,128)(2,1)} %bitcast.32), calls=%async_computation.1 | async-start | bytes 262144 | tf_op jit(solution)/shard_map/all_to_all | solution.py:852
  42.7 4.1 %shard_map.247.refs_5_ = bf16[16384,128]{1,0:T(8,128)(2,1)} custom-call(bf16[64,64]{1,0:T(8,128)(2,1)S(1)} %bitcast.26, f32[64,128]{1,0:T(8,128)S(1)} %broadcast_in_dim.4.refs_1_, bf16[16384,128]{1,0:T(8,128)(2,1)} %shard_map.245.refs_4_.refs_2_.refs_7_, bf16[512,128]{1,0:T(8,128)(2,1)} %get-tuple-element.24.refs_3_), custom_call_target="tpu_custom_call" | custom-call | flops 500000000 | bytes 12582912 | tf_op jit(solution)/shard_map/pallas_call | solution.py:214
  46.8 7.0 %all-to-all-done.1 = bf16[64,8,128]{2,1,0:T(8,128)(2,1)S(1)} async-done(((bf16[64,8,128]{2,1,0:T(8,128)(2,1)}), bf16[64,8,128]{2,1,0:T(8,128)(2,1)S(1)}, u32[]{:S(2)}, u32[]{:S(2)}) %all-to-all-start.1) | async-done | bytes 131104 | tf_op jit(solution)/shard_map/all_to_all | solution.py:852
  53.9 9.1 %shard_map.248 = (bf16[512,128]{1,0:T(8,128)(2,1)}, bf16[16384,128]{1,0:T(8,128)(2,1)}, bf16[16384,128]{1,0:T(8,128)(2,1)}) custom-call(bf16[512,128]{1,0:T(8,128)(2,1)S(1)} %bitcast.23, bf16[128,64]{1,0:T(8,128)(2,1)S(1)} %copy-done.2, bf16[64,256]{1,0:T(8,128)(2,1)S(1)} %copy-done.6, bf16[32,128]{1,0:T(8,128)(2,1)S(1)} %copy-done.12, ...), custom_call_target="tpu_custom_call" | custom-call | flops 1000000000 | bytes 20971520 | tf_op jit(solution)/shard_map/pallas_call | solution.py:214
  63.0 5.2 %all-to-all-start.2 = ((bf16[64,8,128]{2,1,0:T(8,128)(2,1)}), bf16[64,8,128]{2,1,0:T(8,128)(2,1)S(1)}, u32[]{:S(2)}, u32[]{:S(2)}) async-start(bf16[64,8,128]{2,1,0:T(8,128)(2,1)} %bitcast.31), calls=%async_computation.2 | async-start | bytes 262144 | tf_op jit(solution)/shard_map/all_to_all | solution.py:852
  68.3 4.2 %shard_map.249.refs_4_.refs_5_ = bf16[16384,128]{1,0:T(8,128)(2,1)} custom-call(bf16[64,64]{1,0:T(8,128)(2,1)S(1)} %bitcast.27, f32[64,128]{1,0:T(8,128)S(1)} %broadcast_in_dim.5.refs_1_, bf16[16384,128]{1,0:T(8,128)(2,1)} %get-tuple-element.27.refs_2_.refs_1_, bf16[512,128]{1,0:T(8,128)(2,1)} %get-tuple-element.26.refs_3_), custom_call_target="tpu_custom_call" | custom-call | flops 500000000 | bytes 12582912 | tf_op jit(solution)/shard_map/pallas_call | solution.py:214
  72.5 7.0 %all-to-all-done.2 = bf16[64,8,128]{2,1,0:T(8,128)(2,1)S(1)} async-done(((bf16[64,8,128]{2,1,0:T(8,128)(2,1)}), bf16[64,8,128]{2,1,0:T(8,128)(2,1)S(1)}, u32[]{:S(2)}, u32[]{:S(2)}) %all-to-all-start.2) | async-done | bytes 131104 | tf_op jit(solution)/shard_map/all_to_all | solution.py:852
  82.6 5.4 %all-to-all-start.3 = ((bf16[64,8,128]{2,1,0:T(8,128)(2,1)}), bf16[64,8,128]{2,1,0:T(8,128)(2,1)S(1)}, u32[]{:S(2)}, u32[]{:S(2)}) async-start(bf16[64,8,128]{2,1,0:T(8,128)(2,1)} %bitcast.33), calls=%async_computation.3 | async-start | bytes 262144 | tf_op jit(solution)/shard_map/all_to_all | solution.py:852
  88.0 5.1 %shard_map.251.refs_6_ = bf16[16384,128]{1,0:T(8,128)(2,1)} custom-call(bf16[1,64,2,128,128]{4,3,2,1,0:T(8,128)(2,1)} %field.5, bf16[512,128]{1,0:T(8,128)(2,1)} %get-tuple-element.28._), custom_call_target="tpu_custom_call" | custom-call | flops 600000000 | bytes 12582912 | tf_op jit(solution)/shard_map/pallas_call | solution.py:338
  93.1 6.0 %all-to-all-done.3 = bf16[64,8,128]{2,1,0:T(8,128)(2,1)S(1)} async-done(((bf16[64,8,128]{2,1,0:T(8,128)(2,1)}), bf16[64,8,128]{2,1,0:T(8,128)(2,1)S(1)}, u32[]{:S(2)}, u32[]{:S(2)}) %all-to-all-start.3) | async-done | bytes 131104 | tf_op jit(solution)/shard_map/all_to_all | solution.py:852
  99.2 11.3 %shard_map.252 = (bf16[512,128]{1,0:T(8,128)(2,1)}, bf16[16384,128]{1,0:T(8,128)(2,1)}) custom-call(bf16[512,128]{1,0:T(8,128)(2,1)S(1)} %bitcast.21, bf16[128,64]{1,0:T(8,128)(2,1)S(1)} %copy-done.2, bf16[64,256]{1,0:T(8,128)(2,1)S(1)} %copy-done.6, bf16[32,128]{1,0:T(8,128)(2,1)S(1)} %copy-done.11, bf16[64,128]{1,0:T(8,128)(2,1)S(1)} %copy-done.5, ...), custom_call_target="tpu_custom_call" | custom-call | flops 1000000000 | bytes 20971520 | tf_op jit(solution)/shard_map/pallas_call | solution.py:214
  110.5 6.0 %all-to-all-start.4 = ((bf16[64,8,128]{2,1,0:T(8,128)(2,1)}), bf16[64,8,128]{2,1,0:T(8,128)(2,1)S(1)}, u32[]{:S(2)}, u32[]{:S(2)}) async-start(bf16[64,8,128]{2,1,0:T(8,128)(2,1)} %bitcast.34), calls=%async_computation.4 | async-start | bytes 262144 | tf_op jit(solution)/shard_map/all_to_all | solution.py:852
  116.5 5.8 %shard_map.253 = (f32[80,64]{1,0:T(8,128)}, bf16[16384,128]{1,0:T(8,128)(2,1)}) custom-call(bf16[64,64]{1,0:T(8,128)(2,1)S(1)} %copy-done.9, bf16[16384,128]{1,0:T(8,128)(2,1)} %get-tuple-element.27.refs_2_.refs_1_, bf16[16384,128]{1,0:T(8,128)(2,1)} %get-tuple-element.31.refs_2_), custom_call_target="tpu_custom_call" | custom-call | flops 1000000000 | bytes 12582912 | tf_op jit(solution)/shard_map/pallas_call | solution.py:214
  122.3 5.5 %all-to-all-done.4 = bf16[64,8,128]{2,1,0:T(8,128)(2,1)S(1)} async-done(((bf16[64,8,128]{2,1,0:T(8,128)(2,1)}), bf16[64,8,128]{2,1,0:T(8,128)(2,1)S(1)}, u32[]{:S(2)}, u32[]{:S(2)}) %all-to-all-start.4) | async-done | bytes 131104 | tf_op jit(solution)/shard_map/all_to_all | solution.py:852
  127.8 3.5 %shard_map.254 = (bf16[1024,128]{1,0:T(8,128)(2,1)}, bf16[96,256]{1,0:T(8,128)(2,1)}) custom-call(bf16[512,128]{1,0:T(8,128)(2,1)S(1)} %bitcast.22, bf16[2,16,4,64,64]{4,3,2,1,0:T(8,128)(2,1)S(1)} %copy-done, bf16[64,128]{1,0:T(8,128)(2,1)S(1)} %copy-done.4, bf16[128,64]{1,0:T(8,128)(2,1)S(1)} %copy-done.3, bf16[32,256]{1,0:T(8,128)(2,1)S(1)} %copy-done.7, ...), custom_call_target="tpu_custom_call" | custom-call | flops 200000000 | bytes 3145728 | tf_op jit(solution)/shard_map/pallas_call | solution.py:214
  131.4 6.7 %all-to-all-start.5 = ((bf16[64,16,128]{2,1,0:T(8,128)(2,1)}), bf16[64,16,128]{2,1,0:T(8,128)(2,1)S(1)}, u32[]{:S(2)}, u32[]{:S(2)}) async-start(bf16[64,16,128]{2,1,0:T(8,128)(2,1)} %bitcast.30), calls=%async_computation.5 | async-start | bytes 524288 | tf_op jit(solution)/shard_map/all_to_all | solution.py:852
  138.1 3.9 %collective-permute-start = (bf16[96,256]{1,0:T(8,128)(2,1)}, bf16[96,256]{1,0:T(8,128)(2,1)S(1)}, u32[]{:S(2)}, u32[]{:S(2)}) collective-permute-start(bf16[96,256]{1,0:T(8,128)(2,1)} %get-tuple-element.33.refs_0_), channel_id=1, source_target_pairs={{0,64},{64,0},{128,192},{192,128},{1,65},{65,1},{129,193},{193,129... | collective-permute-start | bytes 147464 | tf_op jit(solution)/shard_map/ppermute | solution.py:871
  143.7 7.2 %shard_map.255.refs_6_ = bf16[16384,128]{1,0:T(8,128)(2,1)} custom-call(bf16[16384,128]{1,0:T(8,128)(2,1)} %get-tuple-element.36.refs_0_, bf16[1024,128]{1,0:T(8,128)(2,1)} %get-tuple-element.34.refs_1_), custom_call_target="tpu_custom_call" | custom-call | flops 500000000 | bytes 12582912 | tf_op jit(solution)/shard_map/pallas_call | solution.py:214
  151.6 17.1 %shard_map.256 = bf16[3072,128]{1,0:T(8,128)(2,1)} custom-call(bf16[1024,128]{1,0:T(8,128)(2,1)S(1)} %bitcast.20, bf16[128,64]{1,0:T(8,128)(2,1)S(1)} %copy-done.2, bf16[64,256]{1,0:T(8,128)(2,1)S(1)} %copy-done.10, bf16[32,128]{1,0:T(8,128)(2,1)S(1)} %copy-done.11, bf16[64,128]{1,0:T(8,128)(2,1)S(1)} %copy-done.5, ...), custom_call_target="tpu_custom_call" | custom-call | flops 1500000000 | bytes 20971520 | tf_op jit(solution)/shard_map/pallas_call | solution.py:214
  168.7 34.8 %all_to_all.77 = bf16[64,48,128]{2,1,0:T(8,128)(2,1)S(1)} all-to-all(bf16[64,48,128]{2,1,0:T(8,128)(2,1)} %bitcast.28), channel_id=1, replica_groups=mesh['dp'=4,'space'=64] {'space'}, dimensions={0} | all-to-all | bytes 1572864 | tf_op jit(solution)/shard_map/all_to_all | solution.py:852
  (59 shorter events, 22.2 us)
Async XLA Ops:
  6.8 26.4 %all-to-all-start = ((bf16[64,8,128]{2,1,0:T(8,128)(2,1)}), bf16[64,8,128]{2,1,0:T(8,128)(2,1)S(1)}, u32[]{:S(2)}, u32[]{:S(2)}) async-start(bf16[64,8,128]{2,1,0:T(8,128)(2,1)} %bitcast.29), calls=%async_computation | async-start | bytes 262144 | tf_op jit(solution)/shard_map/all_to_all | solution.py:852
  21.9 11.2 %copy-start.1 = (bf16[2,16,4,64,64]{4,3,2,1,0:T(8,128)(2,1)S(1)}, bf16[2,16,4,64,64]{4,3,2,1,0:T(8,128)(2,1)}, u32[]{:S(2)}) copy-start(bf16[2,16,4,64,64]{4,3,2,1,0:T(8,128)(2,1)} %refs_1_.7) | copy-start | bytes 3145732
  21.9 11.2 %copy-start.3 = (bf16[128,64]{1,0:T(8,128)(2,1)S(1)}, bf16[128,64]{1,0:T(8,128)(2,1)}, u32[]{:S(2)}) copy-start(bf16[128,64]{1,0:T(8,128)(2,1)} %constant.32.clone.refs_3_) | copy-start | bytes 49156
  21.9 11.2 %copy-start.4 = (bf16[64,128]{1,0:T(8,128)(2,1)S(1)}, bf16[64,128]{1,0:T(8,128)(2,1)}, u32[]{:S(2)}) copy-start(bf16[64,128]{1,0:T(8,128)(2,1)} %constant.31.clone.refs_2_.refs_1_) | copy-start | bytes 49156
  27.2 15.4 %copy-start.16 = (bf16[64,64]{1,0:T(8,128)(2,1)S(1)}, bf16[64,64]{1,0:T(8,128)(2,1)}, u32[]{:S(2)}) copy-start(bf16[64,64]{1,0:T(8,128)(2,1)} %param.25) | copy-start | bytes 24580
  27.2 15.5 %copy-start.17 = (f32[64]{0:T(128)S(1)}, f32[64]{0:T(128)}, u32[]{:S(2)}) copy-start(f32[64]{0:T(128)} %param.27) | copy-start | bytes 772
  36.3 17.6 %all-to-all-start.1 = ((bf16[64,8,128]{2,1,0:T(8,128)(2,1)}), bf16[64,8,128]{2,1,0:T(8,128)(2,1)S(1)}, u32[]{:S(2)}, u32[]{:S(2)}) async-start(bf16[64,8,128]{2,1,0:T(8,128)(2,1)} %bitcast.32), calls=%async_computation.1 | async-start | bytes 262144 | tf_op jit(solution)/shard_map/all_to_all | solution.py:852
  42.7 11.2 %copy-start.2 = (bf16[128,64]{1,0:T(8,128)(2,1)S(1)}, bf16[128,64]{1,0:T(8,128)(2,1)}, u32[]{:S(2)}) copy-start(bf16[128,64]{1,0:T(8,128)(2,1)} %constant.30.clone.refs_1_) | copy-start | bytes 49156
  42.7 11.2 %copy-start.5 = (bf16[64,128]{1,0:T(8,128)(2,1)S(1)}, bf16[64,128]{1,0:T(8,128)(2,1)}, u32[]{:S(2)}) copy-start(bf16[64,128]{1,0:T(8,128)(2,1)} %constant.29.clone.refs_4_) | copy-start | bytes 49156
  42.7 11.2 %copy-start.6 = (bf16[64,256]{1,0:T(8,128)(2,1)S(1)}, bf16[64,256]{1,0:T(8,128)(2,1)}, u32[]{:S(2)}) copy-start(bf16[64,256]{1,0:T(8,128)(2,1)} %constant.27.clone.refs_2_) | copy-start | bytes 98308
  46.8 21.3 %copy-start.9 = (bf16[64,64]{1,0:T(8,128)(2,1)S(1)}, bf16[64,64]{1,0:T(8,128)(2,1)}, u32[]{:S(2)}) copy-start(bf16[64,64]{1,0:T(8,128)(2,1)} %refs_0_.1) | copy-start | bytes 24580
  46.8 21.4 %copy-start.18 = (f32[64]{0:T(128)S(1)}, f32[64]{0:T(128)}, u32[]{:S(2)}) copy-start(f32[64]{0:T(128)} %param.28) | copy-start | bytes 772
  63.0 16.5 %all-to-all-start.2 = ((bf16[64,8,128]{2,1,0:T(8,128)(2,1)}), bf16[64,8,128]{2,1,0:T(8,128)(2,1)S(1)}, u32[]{:S(2)}, u32[]{:S(2)}) async-start(bf16[64,8,128]{2,1,0:T(8,128)(2,1)} %bitcast.31), calls=%async_computation.2 | async-start | bytes 262144 | tf_op jit(solution)/shard_map/all_to_all | solution.py:852
  82.6 16.6 %all-to-all-start.3 = ((bf16[64,8,128]{2,1,0:T(8,128)(2,1)}), bf16[64,8,128]{2,1,0:T(8,128)(2,1)S(1)}, u32[]{:S(2)}, u32[]{:S(2)}) async-start(bf16[64,8,128]{2,1,0:T(8,128)(2,1)} %bitcast.33), calls=%async_computation.3 | async-start | bytes 262144 | tf_op jit(solution)/shard_map/all_to_all | solution.py:852
  110.5 17.3 %all-to-all-start.4 = ((bf16[64,8,128]{2,1,0:T(8,128)(2,1)}), bf16[64,8,128]{2,1,0:T(8,128)(2,1)S(1)}, u32[]{:S(2)}, u32[]{:S(2)}) async-start(bf16[64,8,128]{2,1,0:T(8,128)(2,1)} %bitcast.34), calls=%async_computation.4 | async-start | bytes 262144 | tf_op jit(solution)/shard_map/all_to_all | solution.py:852
  116.5 11.3 %copy-start.7 = (bf16[32,256]{1,0:T(8,128)(2,1)S(1)}, bf16[32,256]{1,0:T(8,128)(2,1)}, u32[]{:S(2)}) copy-start(bf16[32,256]{1,0:T(8,128)(2,1)} %get-tuple-element.25.refs_6_.refs_4_) | copy-start | bytes 49156
  116.5 11.3 %copy-start.8 = (bf16[32,256]{1,0:T(8,128)(2,1)S(1)}, bf16[32,256]{1,0:T(8,128)(2,1)}, u32[]{:S(2)}) copy-start(bf16[32,256]{1,0:T(8,128)(2,1)} %get-tuple-element.29.refs_7_.refs_5_) | copy-start | bytes 49156
  131.4 19.6 %all-to-all-start.5 = ((bf16[64,16,128]{2,1,0:T(8,128)(2,1)}), bf16[64,16,128]{2,1,0:T(8,128)(2,1)S(1)}, u32[]{:S(2)}, u32[]{:S(2)}) async-start(bf16[64,16,128]{2,1,0:T(8,128)(2,1)} %bitcast.30), calls=%async_computation.5 | async-start | bytes 524288 | tf_op jit(solution)/shard_map/all_to_all | solution.py:852
  138.1 12.8 %collective-permute-start = (bf16[96,256]{1,0:T(8,128)(2,1)}, bf16[96,256]{1,0:T(8,128)(2,1)S(1)}, u32[]{:S(2)}, u32[]{:S(2)}) collective-permute-start(bf16[96,256]{1,0:T(8,128)(2,1)} %get-tuple-element.33.refs_0_), channel_id=1, source_target_pairs={{0,64},{64,0},{128,192},{192,128},{1,65},{65,1},{129,193},{193,129... | collective-permute-start | bytes 147464 | tf_op jit(solution)/shard_map/ppermute | solution.py:871
  141.9 9.0 %collective-permute-start.1 = (bf16[96,256]{1,0:T(8,128)(2,1)}, bf16[96,256]{1,0:T(8,128)(2,1)S(1)}, u32[]{:S(2)}, u32[]{:S(2)}) collective-permute-start(bf16[96,256]{1,0:T(8,128)(2,1)} %get-tuple-element.33.refs_0_), channel_id=1, source_target_pairs={{0,128},{64,192},{128,0},{192,64},{1,129},{65,193},{129,1},{193,65... | collective-permute-start | bytes 147464 | tf_op jit(solution)/shard_map/ppermute | solution.py:871
  142.7 8.2 %collective-permute-start.2 = (bf16[96,256]{1,0:T(8,128)(2,1)}, bf16[96,256]{1,0:T(8,128)(2,1)S(1)}, u32[]{:S(2)}, u32[]{:S(2)}) collective-permute-start(bf16[96,256]{1,0:T(8,128)(2,1)} %get-tuple-element.33.refs_0_), channel_id=1, source_target_pairs={{0,192},{64,128},{128,64},{192,0},{1,193},{65,129},{129,65},{193,1... | collective-permute-start | bytes 147464 | tf_op jit(solution)/shard_map/ppermute | solution.py:871
  204.6 8.2 %collective-permute-start.3 = (bf16[112,256]{1,0:T(8,128)(2,1)}, bf16[112,256]{1,0:T(8,128)(2,1)S(1)}, u32[]{:S(2)}, u32[]{:S(2)}) collective-permute-start(bf16[112,256]{1,0:T(8,128)(2,1)} %shard_map.257.refs_4_), channel_id=1, source_target_pairs={{0,64},{64,0},{128,192},{192,128},{1,65},{65,1},{129,193},{193,129... | collective-permute-start | bytes 172040 | tf_op jit(solution)/shard_map/ppermute | solution.py:871
  207.9 5.0 %collective-permute-start.4 = (bf16[112,256]{1,0:T(8,128)(2,1)}, bf16[112,256]{1,0:T(8,128)(2,1)S(1)}, u32[]{:S(2)}, u32[]{:S(2)}) collective-permute-start(bf16[112,256]{1,0:T(8,128)(2,1)} %shard_map.257.refs_4_), channel_id=1, source_target_pairs={{0,128},{64,192},{128,0},{192,64},{1,129},{65,193},{129,1},{193,65... | collective-permute-start | bytes 172040 | tf_op jit(solution)/shard_map/ppermute | solution.py:871
  209.3 4.1 %collective-permute-start.5 = (bf16[112,256]{1,0:T(8,128)(2,1)}, bf16[112,256]{1,0:T(8,128)(2,1)S(1)}, u32[]{:S(2)}, u32[]{:S(2)}) collective-permute-start(bf16[112,256]{1,0:T(8,128)(2,1)} %shard_map.257.refs_4_), channel_id=1, source_target_pairs={{0,192},{64,128},{128,64},{192,0},{1,193},{65,129},{129,65},{193,1... | collective-permute-start | bytes 172040 | tf_op jit(solution)/shard_map/ppermute | solution.py:871
  (7 other events, 43.2 us)
